TPU v7x, 512 devices: a whole 4x4x16 slice. The times are simulated.
512 devices in a mesh: dp: 32 (over z_hi, y, core), tensor: 16 (over z_lo, x).
Axes of the slice: x: 4, y: 4, z: 16 (z_hi: 4, z_lo: 4; z = z_hi * 4 + z_lo), core: 2. Of those that a mesh axis runs over, the one named last changes fastest.
Arguments:
- hidden_in: bfloat16 [24576, 4096], P('dp', 'tensor'), may hold values from -40 to 40
- live_rows: int32 [32], replicated, may hold values from 1 to 768, 8192 in all
- sample_tokens: int32 [4], replicated, may hold values from 1 to 4096, 8192 in all
- w_up: bfloat16 [4096, 12288], P('dp', 'tensor'), may hold values from -3 to 3
- w_down: bfloat16 [12288, 4096], P('tensor', 'dp'), may hold values from -0.109375 to 0.109375
- modulation: float32 [3, 4, 4096], P(None, None, 'tensor'), may hold values from -3 to 3
- out_grad: bfloat16 [8192, 4096], P('dp', 'tensor'), may hold values from -6 to 6
Outputs:
- block_out: bfloat16 [8192, 4096], P('dp', 'tensor')
- input_grad: bfloat16 [24576, 4096], P('dp', 'tensor')
- mod_grad: float32 [3, 4, 4096], P(None, None, 'tensor')
Inputs may be any that keep to these rules, and one draw needn't show every extreme that they name: `live_rows`: the entries sum to 8192. `sample_tokens`: the entries sum to 8192.
All inputs are finite; a program needn't handle non-finite values.
Results may differ from a plain program's by a relative error of at most 0.023.
Values may be sent and summed in bfloat16 or wider, within the bound.
No kernel may reach another device: no remote copies, remote signals or barrier semaphores. Data moves between devices by JAX's collectives and lax.ppermute only.
A program may use at most 64 MiB of HBM per device.

v0:
```python
import jax
import jax.numpy as jnp
from jax import lax
from jax.sharding import PartitionSpec as P

GELU_K = 0.7978845608028654
GELU_C = 0.044715
EPS = 1e-06


def gelu_value(pre):
    inner = GELU_K * (pre + GELU_C * pre * pre * pre)
    return 0.5 * pre * (1.0 + jnp.tanh(inner))


def gelu_slope(pre):
    inner = GELU_K * (pre + GELU_C * pre * pre * pre)
    tangent = jnp.tanh(inner)
    return 0.5 * (1.0 + tangent) + 0.5 * pre * (1.0 - tangent * tangent) * GELU_K * (
        1.0 + 3.0 * GELU_C * pre * pre
    )


def contract_last(left, right):
    return lax.dot_general(
        left, right, (((1,), (1,)), ((), ())), preferred_element_type=jnp.float32
    )


def sample_totals(member, values):
    return lax.dot_general(
        member, values, (((0,), (0,)), ((), ())), precision=lax.Precision.HIGHEST
    )


def body(hidden_in, live_rows, sample_tokens, w_up, w_down, modulation, out_grad):
    groups = lax.axis_size("dp")
    position = lax.axis_index("dp")
    slots_in = hidden_in.shape[0]
    per_pair = slots_in // groups
    balanced = out_grad.shape[0]
    width_local = hidden_in.shape[1]
    tensor_count = lax.axis_size("tensor")
    model_width = width_local * tensor_count
    row_ends = jnp.cumsum(live_rows)
    row_starts = row_ends - live_rows
    device_ids = jnp.arange(groups, dtype=jnp.int32)
    own_start = jnp.sum(jnp.where(device_ids == position, row_starts, 0))
    own_live = jnp.sum(jnp.where(device_ids == position, live_rows, 0))
    slot_ids = jnp.arange(per_pair, dtype=jnp.int32)[None, :]
    first_row = jnp.mod(device_ids[:, None] - own_start, groups)
    local_rows = first_row + groups * slot_ids
    picked = jnp.take(hidden_in, jnp.minimum(local_rows, slots_in - 1).reshape(-1), axis=0)
    outgoing = jnp.where((local_rows < own_live).reshape(-1, 1), picked, jnp.zeros_like(picked))
    outgoing = outgoing.reshape(groups, per_pair, width_local)
    incoming = lax.all_to_all(outgoing, "dp", split_axis=0, concat_axis=0, tiled=True)
    global_rows = position + groups * jnp.arange(balanced, dtype=jnp.int32)
    owner_table = (row_ends[None, :] <= global_rows[:, None]).astype(jnp.int32)
    owners = jnp.sum(owner_table, axis=1)
    owner_start = jnp.sum(
        jnp.where(owners[:, None] == device_ids[None, :], row_starts[None, :], 0), axis=1
    )
    owner_slot = (global_rows - owner_start) // groups
    rows_bal = jnp.take(
        incoming.reshape(groups * per_pair, width_local), owners * per_pair + owner_slot, axis=0
    )
    sample_ends = jnp.cumsum(sample_tokens)
    sample_starts = sample_ends - sample_tokens
    member = (
        (global_rows[:, None] >= sample_starts[None, :])
        & (global_rows[:, None] < sample_ends[None, :])
    ).astype(jnp.float32)
    shift_rows = jnp.dot(member, modulation[0], precision=lax.Precision.HIGHEST)
    scale_rows = jnp.dot(member, modulation[1], precision=lax.Precision.HIGHEST)
    gate_rows = jnp.dot(member, modulation[2], precision=lax.Precision.HIGHEST)
    rows_f = rows_bal.astype(jnp.float32)
    average = lax.psum(jnp.sum(rows_f, axis=1), "tensor") / model_width
    centred = rows_f - average[:, None]
    spread = lax.psum(jnp.sum(centred * centred, axis=1), "tensor") / model_width
    inv_scale = lax.rsqrt(spread + EPS)[:, None]
    normed = centred * inv_scale
    modulated = (normed * (1.0 + scale_rows) + shift_rows).astype(jnp.bfloat16)
    up_whole = lax.all_gather(w_up, "dp", axis=0, tiled=True)
    down_whole = lax.all_gather(w_down, "dp", axis=1, tiled=True)
    pre = jnp.dot(
        lax.all_gather(modulated, "tensor", axis=1, tiled=True),
        up_whole,
        preferred_element_type=jnp.float32,
    )
    hidden = gelu_value(pre).astype(jnp.bfloat16)
    partial_out = jnp.dot(hidden, down_whole, preferred_element_type=jnp.float32)
    branch = lax.psum_scatter(
        partial_out.astype(jnp.bfloat16), "tensor", scatter_dimension=1, tiled=True
    ).astype(jnp.float32)
    block_out = (rows_f + gate_rows * branch).astype(jnp.bfloat16)
    grad_f = out_grad.astype(jnp.float32)
    scaled_grad = (gate_rows * grad_f).astype(jnp.bfloat16)
    hidden_grad = contract_last(
        lax.all_gather(scaled_grad, "tensor", axis=1, tiled=True), down_whole
    )
    pre_grad = (hidden_grad * gelu_slope(pre)).astype(jnp.bfloat16)
    partial_in = contract_last(pre_grad, up_whole)
    mod_in_grad = lax.psum_scatter(
        partial_in.astype(jnp.bfloat16), "tensor", scatter_dimension=1, tiled=True
    ).astype(jnp.float32)
    normed_grad = mod_in_grad * (1.0 + scale_rows)
    first_sum, second_sum = lax.psum(
        (jnp.sum(normed_grad, axis=1), jnp.sum(normed_grad * normed, axis=1)), "tensor"
    )
    first_mean = (first_sum / model_width)[:, None]
    second_mean = (second_sum / model_width)[:, None]
    row_grad = (grad_f + inv_scale * (normed_grad - first_mean - normed * second_mean)).astype(
        jnp.bfloat16
    )
    local_mod = jnp.stack(
        [
            sample_totals(member, mod_in_grad),
            sample_totals(member, mod_in_grad * normed),
            sample_totals(member, grad_f * branch),
        ]
    )
    mod_grad = lax.psum(local_mod, "dp")
    source_first = jnp.mod(position - row_starts[:, None], groups)
    source_rows = source_first + groups * slot_ids
    back_valid = source_rows < live_rows[:, None]
    back_index = (row_starts[:, None] + source_rows - position) // groups
    taken = jnp.take(row_grad, jnp.clip(back_index, 0, balanced - 1).reshape(-1), axis=0)
    returning = jnp.where(back_valid.reshape(-1, 1), taken, jnp.zeros_like(taken)).reshape(
        groups, per_pair, width_local
    )
    arrived = lax.all_to_all(returning, "dp", split_axis=0, concat_axis=0, tiled=True)
    own_rows = jnp.arange(slots_in, dtype=jnp.int32)
    target_of = jnp.mod(own_start + own_rows, groups)
    target_slot = own_rows // groups
    gathered_back = jnp.take(
        arrived.reshape(groups * per_pair, width_local), target_of * per_pair + target_slot, axis=0
    )
    input_grad = jnp.where(
        (own_rows < own_live)[:, None], gathered_back, jnp.zeros_like(gathered_back)
    )
    return (block_out, input_grad, mod_grad)


def solution(mesh):
    return jax.shard_map(
        body,
        mesh=mesh,
        in_specs=(
            P("dp", "tensor"),
            P(),
            P(),
            P("dp", "tensor"),
            P("tensor", "dp"),
            P(None, None, "tensor"),
            P("dp", "tensor"),
        ),
        out_specs=(P("dp", "tensor"), P("dp", "tensor"), P(None, None, "tensor")),
        check_vma=False,
    )
```

profile of v0, /device:TPU:2, one launch (start us, length us, event | category | flops | bytes accessed | tf_op | source)
XLA Modules:
  0.0 972.7 jit_solution(12522392451060567400)
XLA Ops:
  7.2 0.8 copy.14
  8.0 0.1 reduce
  8.2 1.3 and_select_fusion.2
  9.5 0.7 fusion.53
  10.2 0.7 and_select_fusion.3
  11.1 1.4 add_compare_fusion
  12.5 0.1 lt.107
  12.6 2.7 gather_fusion.2
  15.3 1.0 select_select_fusion.1
  16.3 18.1 %all-to-all-start = ((bf16[32,24,256]{2,1,0:T(8,128)(2,1)}), bf16[32,24,256]{2,1,0:T(8,128)(2,1)S(1)}, u32[]{:S(2)}, u32[]{:S(2)}) async-start(bf16[32,24,256]{2,1,0:T(8,128)(2,1)} %bitcast.1), calls=%async_computation | async-start | bytes 786432 | tf_op jit(solution)/shard_map/all_to_all | solution.py:56
  34.4 0.8 reduce-window.17
  35.3 0.1 convert_reduce_fusion.1
  35.5 0.7 bitcast_subtract_fusion
  36.2 1.0 convolution_add_fusion.1
  37.2 21.0 %all-to-all-done = bf16[32,24,256]{2,1,0:T(8,128)(2,1)S(1)} async-done(((bf16[32,24,256]{2,1,0:T(8,128)(2,1)}), bf16[32,24,256]{2,1,0:T(8,128)(2,1)S(1)}, u32[]{:S(2)}, u32[]{:S(2)}) %all-to-all-start) | async-done | bytes 393248 | tf_op jit(solution)/shard_map/all_to_all | solution.py:56
  58.2 1.2 gather_fusion
  59.4 0.2 convert_reduce_fusion
  59.6 40.7 %psum.35 = f32[256]{0:T(256)S(1)} all-reduce(f32[256]{0:T(256)S(1)} %convert_reduce_fusion), channel_id=1, replica_groups=mesh['dp'=32,'tensor'=16] {'tensor'}, use_global_device_ids=true, to_apply=%region_7.9 | all-reduce | flops 256 | bytes 2048 | tf_op jit(solution)/shard_map/psum | solution.py:77
  100.3 0.2 fusion.25
  100.5 42.9 %psum.36 = f32[256]{0:T(256)S(1)} all-reduce(f32[256]{0:T(256)S(1)} %fusion.25), channel_id=1, replica_groups=mesh['dp'=32,'tensor'=16] {'tensor'}, use_global_device_ids=true, to_apply=%region_9.11 | all-reduce | flops 256 | bytes 2048 | tf_op jit(solution)/shard_map/psum | solution.py:79
  143.4 1.0 fusion.1
  144.5 0.7 all-gather.7.cloned.1.call-update
  145.2 0.7 all-gather.9.cloned.1.call-update
  145.9 66.7 %all-gather.5.cloned.1.call-done = bf16[256,4096]{1,0:T(8,128)(2,1)} async-done(((bf16[256,256]{1,0:T(8,128)(2,1)}), bf16[256,4096]{1,0:T(8,128)(2,1)}) %all-gather.5.cloned.1.call-update) | async-done | bytes 2097168 | tf_op jit(solution)/shard_map/all_gather | solution.py:86
  212.7 118.5 %all-gather.7.cloned.1.call-done = bf16[4096,768]{1,0:T(8,128)(2,1)} async-done(((bf16[128,768]{1,0:T(8,128)(2,1)}), bf16[4096,768]{1,0:T(8,128)(2,1)}) %all-gather.7.cloned.1.call-update) | async-done | bytes 6291472 | tf_op jit(solution)/shard_map/all_gather | solution.py:83
  331.2 5.2 fusion.66
  336.4 116.6 %all-gather.9.cloned.1.call-done = bf16[768,4096]{1,0:T(8,128)(2,1)} async-done(((bf16[768,128]{1,0:T(8,128)(2,1)}), bf16[768,4096]{1,0:T(8,128)(2,1)}) %all-gather.9.cloned.1.call-update) | async-done | bytes 6291472 | tf_op jit(solution)/shard_map/all_gather | solution.py:84
  453.0 6.1 convolution_convert_fusion.1
  459.2 82.2 %reduce-scatter.3.cloned.1.call-done = bf16[256,256]{1,0:T(8,128)(2,1)} async-done(((bf16[256,4096]{1,0:T(8,128)(2,1)}), bf16[256,256]{1,0:T(8,128)(2,1)}) %reduce-scatter.3.cloned.1.call-update) | async-done | bytes 131088 | tf_op jit(solution)/shard_map/reduce_scatter | solution.py:92
  541.3 1.9 fusion.27
  543.3 79.9 %all-gather.11.cloned.1.call-done = bf16[256,4096]{1,0:T(8,128)(2,1)} async-done(((bf16[256,256]{1,0:T(8,128)(2,1)}), bf16[256,4096]{1,0:T(8,128)(2,1)}) %all-gather.11.cloned.1.call-update) | async-done | bytes 2097168 | tf_op jit(solution)/shard_map/all_gather | solution.py:99
  623.2 11.3 %convolution_convert_fusion = bf16[256,4096]{1,0:T(8,128)(2,1)} fusion(bf16[4096,768]{1,0:T(8,128)(2,1)} %all-gather.7.cloned.1.call-done, bf16[256,4096]{1,0:T(8,128)(2,1)} %all-gather.11.cloned.1.call-done, bf16[768,4096]{1,0:T(8,128)(2,1)} %all-gather.9.cloned.1.call-done, f32[256,768]{1,0:T(8,128)S(1)} %fusion.66), kind=kOutput, calls=%fused_computation.4 | convolution fusion | flops 3226009600 | bytes 17563648 | tf_op jit(solution)/shard_map/dot_general | solution.py:25
  634.7 88.6 %reduce-scatter.5.cloned.1.call-done = bf16[256,256]{1,0:T(8,128)(2,1)} async-done(((bf16[256,4096]{1,0:T(8,128)(2,1)}), bf16[256,256]{1,0:T(8,128)(2,1)}) %reduce-scatter.5.cloned.1.call-update) | async-done | bytes 131088 | tf_op jit(solution)/shard_map/reduce_scatter | solution.py:103
  723.3 1.2 fusion.31
  724.6 42.7 %all-reduce = (f32[256]{0:T(256)S(1)}, f32[256]{0:T(256)S(1)}) all-reduce(f32[256]{0:T(256)S(1)} %get-tuple-element.5, f32[256]{0:T(256)S(1)} %get-tuple-element.4), channel_id=1, replica_groups=mesh['dp'=32,'tensor'=16] {'tensor'}, use_global_device_ids=true, to_apply=%region_15.17 | all-reduce | flops 512 | bytes 4096 | tf_op jit(solution)/shard_map/psum | solution.py:107
  767.3 1.1 fusion.28
  768.5 2.7 gather_fusion.1
  771.1 1.0 select_select_fusion.2
  772.1 12.4 %all-to-all-start.1 = ((bf16[32,24,256]{2,1,0:T(8,128)(2,1)}), bf16[32,24,256]{2,1,0:T(8,128)(2,1)S(1)}, u32[]{:S(2)}, u32[]{:S(2)}) async-start(bf16[32,24,256]{2,1,0:T(8,128)(2,1)} %select_select_fusion.2), calls=%async_computation.3 | async-start | bytes 786432 | tf_op jit(solution)/shard_map/all_to_all | solution.py:131
  784.6 0.7 compare_and_fusion.2
  785.3 0.7 iota_compare_fusion.1
  785.9 0.7 compare_select_fusion.2
  786.6 0.3 convolution_bitcast_fusion
  787.0 0.3 convolution_bitcast_fusion.2
  787.2 0.4 convolution_bitcast_fusion.1
  787.7 174.5 %psum.39 = f32[3,4,256]{2,1,0:T(4,128)} all-reduce(f32[3,4,256]{2,1,0:T(4,128)S(1)} %pad_maximum_fusion), channel_id=1, replica_groups=mesh['dp'=32,'tensor'=16] {'dp'}, use_global_device_ids=true, to_apply=%region_16.18 | all-reduce | flops 3072 | bytes 24576 | tf_op jit(solution)/shard_map/psum | solution.py:122
  962.2 2.6 gather_fusion.3
  964.9 1.0 select_select_fusion
  (42 shorter events, 0.9 us)
Async XLA Ops:
  7.2 5.4 copy-start
  7.2 136.2 %copy-start.3 = (f32[3,4,256]{2,1,0:T(4,128)S(1)}, f32[3,4,256]{2,1,0:T(4,128)}, u32[]{:S(2)}) copy-start(f32[3,4,256]{2,1,0:T(4,128)} %param.14) | copy-start | bytes 36868
  16.3 42.0 %all-to-all-start = ((bf16[32,24,256]{2,1,0:T(8,128)(2,1)}), bf16[32,24,256]{2,1,0:T(8,128)(2,1)S(1)}, u32[]{:S(2)}, u32[]{:S(2)}) async-start(bf16[32,24,256]{2,1,0:T(8,128)(2,1)} %bitcast.1), calls=%async_computation | async-start | bytes 786432 | tf_op jit(solution)/shard_map/all_to_all | solution.py:56
  34.4 178.3 %all-gather.5.cloned.1.call-start = ((), (), s32[]{:S(2)}) async-start(), calls=%async_computation.4 | async-start | bytes 2228224 | tf_op jit(solution)/shard_map/all_gather | solution.py:86
  144.4 186.8 %all-gather.7.cloned.1.call-start = ((), (), s32[]{:S(2)}) async-start(), calls=%async_computation.5 | async-start | bytes 6488064 | tf_op jit(solution)/shard_map/all_gather | solution.py:83
  145.2 307.9 %all-gather.9.cloned.1.call-start = ((), (), s32[]{:S(2)}) async-start(), calls=%async_computation.6 | async-start | bytes 6488064 | tf_op jit(solution)/shard_map/all_gather | solution.py:84
  145.9 395.4 %reduce-scatter.3.cloned.1.call-start = ((), (), s32[]{:S(2)}) async-start(), calls=%async_computation.7 | async-start | bytes 2228224 | tf_op jit(solution)/shard_map/reduce_scatter | solution.py:92
  336.4 204.9 %copy-start.2 = (bf16[256,256]{1,0:T(8,128)(2,1)S(1)}, bf16[256,256]{1,0:T(8,128)(2,1)}, u32[]{:S(2)}) copy-start(bf16[256,256]{1,0:T(8,128)(2,1)} %param.15) | copy-start | bytes 393220
  459.1 164.1 %all-gather.11.cloned.1.call-start = ((), (), s32[]{:S(2)}) async-start(), calls=%async_computation.8 | async-start | bytes 2228224 | tf_op jit(solution)/shard_map/all_gather | solution.py:99
  543.3 180.1 %reduce-scatter.5.cloned.1.call-start = ((), (), s32[]{:S(2)}) async-start(), calls=%async_computation.9 | async-start | bytes 2228224 | tf_op jit(solution)/shard_map/reduce_scatter | solution.py:103
  634.5 152.1 %copy-start.4 = (bf16[256,256]{1,0:T(8,128)(2,1)S(1)}, bf16[256,256]{1,0:T(8,128)(2,1)}, u32[]{:S(2)}) copy-start(bf16[256,256]{1,0:T(8,128)(2,1)} %reduce-scatter.3.cloned.1.call-done) | copy-start | bytes 393220
  723.3 63.6 %copy-start.1 = (bf16[256,256]{1,0:T(8,128)(2,1)S(1)}, bf16[256,256]{1,0:T(8,128)(2,1)}, u32[]{:S(2)}) copy-start(bf16[256,256]{1,0:T(8,128)(2,1)} %reduce-scatter.5.cloned.1.call-done) | copy-start | bytes 393220
  772.1 190.1 %all-to-all-start.1 = ((bf16[32,24,256]{2,1,0:T(8,128)(2,1)}), bf16[32,24,256]{2,1,0:T(8,128)(2,1)S(1)}, u32[]{:S(2)}, u32[]{:S(2)}) async-start(bf16[32,24,256]{2,1,0:T(8,128)(2,1)} %select_select_fusion.2), calls=%async_computation.3 | async-start | bytes 786432 | tf_op jit(solution)/shard_map/all_to_all | solution.py:131
Sparse Core Ops, SparseCore 0:
  144.5 68.0 all-gather.4
  215.8 115.3 all-gather.6
  334.3 118.6 all-gather.8
  459.2 82.0 reduce-scatter.2
  543.7 79.4 all-gather.10
  634.7 88.6 reduce-scatter.4
where the time goes:
time: 973 us
  waiting for transfers between devices  575 us (59%)
  blocking collectives  301 us (31%)
  starting transfers between devices  30.8 us (3%)
  matrix products  27.5 us (3%)
  between operations  14.3 us (1%)
  other arithmetic  14.1 us (1%)
  local copies, waits for them, and re-layouts  10.2 us (1%)
    psum x1, blocking collectives, body(): mod_grad = lax.psum(local_mod, 'dp')  175 us
    all_gather x1, waiting for transfers between devices, body(): up_whole = lax.all_gather(w_up, 'dp', axis=0, tiled=True)  119 us
    all_gather x1, waiting for transfers between devices, body(): down_whole = lax.all_gather(w_down, 'dp', axis=1, tiled=True)  117 us
    reduce_scatter x1, waiting for transfers between devices, body(): lax.psum_scatter(partial_in.astype(jnp.bfloat16), 'tensor', scatter_dimen...  88.6 us
    reduce_scatter x1, waiting for transfers between devices, body(): lax.psum_scatter(partial_out.astype(jnp.bfloat16), 'tensor', scatter_dime...  82.2 us
    all_gather x1, waiting for transfers between devices, body(): lax.all_gather(scaled_grad, 'tensor', axis=1, tiled=True)  79.9 us
    all_gather x1, waiting for transfers between devices, body(): lax.all_gather(modulated, 'tensor', axis=1, tiled=True)  66.7 us
    psum x1, blocking collectives, body(): lax.psum(jnp.sum(centred * centred, axis=1), 'tensor') / model_width  42.9 us
  transfers between devices with their start and end apart: 8, of which 7 were waited for; matrix products, arithmetic and copies ran while one was open for 1% of the time, Pallas kernels for 0%

commit v1 on v0

v1 whole, which is shorter than its diff:
```python
import jax
import jax.numpy as jnp
from jax import lax
from jax.experimental import pallas as pl
from jax.experimental.pallas import tpu as pltpu
from jax.sharding import Mesh, PartitionSpec as P

GELU_K = 0.7978845608028654
GELU_C = 0.044715
EPS = 1e-06
AXES = ("zh", "y", "c", "zl", "x")
SIZES = (4, 4, 2, 4, 4)
DP = ("zh", "y", "c")
TP = ("zl", "x")
SAMPLES = 4
VMEM = 48 * 1024 * 1024


def gelu_value(pre):
    inner = GELU_K * (pre + GELU_C * pre * pre * pre)
    return 0.5 * pre * (1.0 + jnp.tanh(inner))


def gelu_slope(pre):
    inner = GELU_K * (pre + GELU_C * pre * pre * pre)
    tangent = jnp.tanh(inner)
    return 0.5 * (1.0 + tangent) + 0.5 * pre * (1.0 - tangent * tangent) * GELU_K * (
        1.0 + 3.0 * GELU_C * pre * pre
    )


def contract_last(left, right):
    return lax.dot_general(
        left, right, (((1,), (1,)), ((), ())), preferred_element_type=jnp.float32
    )


def sample_totals(member, values):
    return lax.dot_general(
        member, values, (((0,), (0,)), ((), ())), precision=lax.Precision.HIGHEST
    )


def shifted(value, axis, step):
    size = lax.axis_size(axis)
    return lax.ppermute(value, axis, [(i, (i + step) % size) for i in range(size)])


def crossed(value, axis, mask):
    size = lax.axis_size(axis)
    return lax.ppermute(value, axis, [(i, i ^ mask) for i in range(size)])


def ring_pieces(value, axis):
    half = value.shape[0] // 2
    before = shifted(value, axis, 1)
    after = shifted(value, axis, -1)
    far = jnp.concatenate(
        [shifted(before[:half], axis, 1), shifted(after[half:], axis, -1)], axis=0
    )
    return value, before, far, after


def spread(value, axis):
    copies = jnp.broadcast_to(value[None], (lax.axis_size(axis),) + value.shape)
    return lax.all_to_all(copies, axis, split_axis=0, concat_axis=0, tiled=True)


def summed(value, axis):
    if lax.axis_size(axis) == 2:
        return value + crossed(value, axis, 1)
    return (value + crossed(value, axis, 1)) + (crossed(value, axis, 2) + crossed(value, axis, 3))


def gathered_weight(part):
    over_zh = jnp.stack(ring_pieces(part, "zh"))
    own = ring_pieces(over_zh, "y")
    other = tuple(shifted(piece, "c", 1) for piece in own)
    return own + other


def sample_mix(member, table):
    out = jnp.broadcast_to(table[SAMPLES - 1 : SAMPLES], (member.shape[0], table.shape[1]))
    for q in range(SAMPLES - 1):
        out = jnp.where(member[:, q : q + 1] > 0.5, table[q : q + 1], out)
    return out


def prepare_kernel(place, rows, grad, modulation, member, mod_out, grad_out, average, inv_scale):
    y, zh, c = place[0], place[1], place[2]
    live = member[...]
    count = rows.shape[0]
    width = rows.shape[3]
    half = width // 2
    features = count * count * width

    total = jnp.zeros(rows.shape[2:], jnp.float32)
    for i in range(count):
        for j in range(count):
            total = total + rows[i, j].astype(jnp.float32)
    mean = jnp.sum(total, axis=1, keepdims=True) / features
    total = jnp.zeros(rows.shape[2:], jnp.float32)
    for i in range(count):
        for j in range(count):
            centred = rows[i, j].astype(jnp.float32) - mean
            total = total + centred * centred
    inv = lax.rsqrt(jnp.sum(total, axis=1, keepdims=True) / features + EPS)
    average[...] = mean
    inv_scale[...] = inv

    def step(index, carry):
        dy, dz = index // count, index % count
        xi = lax.rem(y - dy + count, count)
        zi = lax.rem(zh - dz + count, count)
        table = modulation[zi * count + xi]
        shift, scale, gate = table[0:4], table[4:8], table[8:12]
        normed = (rows[xi, zi].astype(jnp.float32) - mean) * inv
        value = (normed * (1.0 + sample_mix(live, scale)) + sample_mix(live, shift)).astype(
            jnp.bfloat16
        )
        gated = (sample_mix(live, gate) * grad[xi, zi].astype(jnp.float32)).astype(jnp.bfloat16)
        first = pl.ds(pl.multiple_of(c * half, half), half)
        second = pl.ds(pl.multiple_of((1 - c) * half, half), half)
        mod_out[dy, dz, :, first] = value[:, :half]
        mod_out[dy, dz, :, second] = value[:, half:]
        grad_out[dy, dz, :, first] = gated[:, :half]
        grad_out[dy, dz, :, second] = gated[:, half:]
        return carry

    lax.fori_loop(0, count * count, step, 0)


def product_in(blocks, pieces, total):
    count = blocks.shape[0]
    total[...] = jnp.zeros_like(total)
    for dy in range(count):
        own, other = pieces[dy], pieces[count + dy]

        def step(dz, carry, dy=dy, own=own, other=other):
            weight = jnp.concatenate([own[dz], other[dz]], axis=0)
            total[...] += jnp.dot(blocks[dy, dz], weight, preferred_element_type=jnp.float32)
            return carry

        lax.fori_loop(0, count, step, 0)


def product_out(place, hidden, pieces, out):
    y, zh, c = place[0], place[1], place[2]
    count = out.shape[0]
    half = out.shape[3] // 2
    first = pl.ds(pl.multiple_of(c * half, half), half)
    second = pl.ds(pl.multiple_of((1 - c) * half, half), half)
    for dy in range(count):
        own, other = pieces[dy], pieces[count + dy]

        def step(dz, carry, dy=dy, own=own, other=other):
            weight = jnp.concatenate([own[dz], other[dz]], axis=0)
            value = contract_last(hidden[...], weight).astype(jnp.bfloat16)
            xi = lax.rem(y - dy + count, count)
            zi = lax.rem(zh - dz + count, count)
            out[xi, zi, :, first] = value[:, :half]
            out[xi, zi, :, second] = value[:, half:]
            return carry

        lax.fori_loop(0, count, step, 0)


def forward_kernel(place, blocks, *refs):
    up, down = refs[:8], refs[8:16]
    pre, out, hidden = refs[16:]
    product_in(blocks, up, pre)
    hidden[...] = gelu_value(pre[...]).astype(jnp.bfloat16)
    product_out(place, hidden, down, out)


def backward_kernel(place, blocks, pre, *refs):
    up, down = refs[:8], refs[8:16]
    out, total, pre_grad = refs[16:]
    product_in(blocks, down, total)
    pre_grad[...] = (total[...] * gelu_slope(pre[...])).astype(jnp.bfloat16)
    product_out(place, pre_grad, up, out)


SMEM_SPEC = pl.BlockSpec(memory_space=pltpu.SMEM)
VMEM_SPEC = pl.BlockSpec(memory_space=pltpu.VMEM)


def call(kernel, outs, scratch, flops, moved, *args):
    return pl.pallas_call(
        kernel,
        out_shape=outs,
        in_specs=[SMEM_SPEC] + [VMEM_SPEC] * (len(args) - 1),
        out_specs=jax.tree.map(lambda _: VMEM_SPEC, outs),
        scratch_shapes=scratch,
        compiler_params=pltpu.CompilerParams(vmem_limit_bytes=VMEM),
        cost_estimate=pl.CostEstimate(flops=flops, bytes_accessed=moved, transcendentals=0),
    )(*args)


def scattered_sum(blocks):
    from_x = lax.all_to_all(blocks, "x", split_axis=0, concat_axis=0, tiled=True)
    over_x = jnp.sum(from_x.astype(jnp.float32), axis=0).astype(jnp.bfloat16)
    from_zl = lax.all_to_all(over_x, "zl", split_axis=0, concat_axis=0, tiled=True)
    return jnp.sum(from_zl.astype(jnp.float32), axis=0)


def body(hidden_in, live_rows, sample_tokens, w_up, w_down, modulation, out_grad):
    groups = lax.axis_size(DP)
    position = lax.axis_index(DP)
    slots_in = hidden_in.shape[0]
    per_pair = slots_in // groups
    balanced = out_grad.shape[0]
    width_local = hidden_in.shape[1]
    tensor_count = lax.axis_size(TP)
    model_width = width_local * tensor_count
    hid = w_up.shape[1]
    f32, bf16 = jnp.float32, jnp.bfloat16
    shape = jax.ShapeDtypeStruct

    up = gathered_weight(w_up)
    down = gathered_weight(w_down.T)

    row_ends = jnp.cumsum(live_rows)
    row_starts = row_ends - live_rows
    device_ids = jnp.arange(groups, dtype=jnp.int32)
    own_start = jnp.sum(jnp.where(device_ids == position, row_starts, 0))
    own_live = jnp.sum(jnp.where(device_ids == position, live_rows, 0))
    slot_ids = jnp.arange(per_pair, dtype=jnp.int32)[None, :]
    first_row = jnp.mod(device_ids[:, None] - own_start, groups)
    local_rows = first_row + groups * slot_ids
    picked = jnp.take(hidden_in, jnp.minimum(local_rows, slots_in - 1).reshape(-1), axis=0)
    outgoing = jnp.where((local_rows < own_live).reshape(-1, 1), picked, jnp.zeros_like(picked))
    outgoing = outgoing.reshape(groups, per_pair, width_local)
    incoming = lax.all_to_all(outgoing, DP, split_axis=0, concat_axis=0, tiled=True)
    global_rows = position + groups * jnp.arange(balanced, dtype=jnp.int32)
    owner_table = (row_ends[None, :] <= global_rows[:, None]).astype(jnp.int32)
    owners = jnp.sum(owner_table, axis=1)
    owner_start = jnp.sum(
        jnp.where(owners[:, None] == device_ids[None, :], row_starts[None, :], 0), axis=1
    )
    owner_slot = (global_rows - owner_start) // groups
    rows_bal = jnp.take(
        incoming.reshape(groups * per_pair, width_local), owners * per_pair + owner_slot, axis=0
    )
    sample_ends = jnp.cumsum(sample_tokens)
    sample_starts = sample_ends - sample_tokens
    member = (
        (global_rows[:, None] >= sample_starts[None, :])
        & (global_rows[:, None] < sample_ends[None, :])
    ).astype(f32)

    rows_all = spread(spread(rows_bal, "zl"), "x")
    grad_all = spread(spread(out_grad, "zl"), "x")
    modulation_all = lax.all_gather(modulation.reshape(-1, width_local), TP, axis=0)

    place = jnp.stack([lax.axis_index("y"), lax.axis_index("zh"), lax.axis_index("c")]).astype(
        jnp.int32
    )
    block_shape = shape(rows_all.shape, bf16)
    column = shape((balanced, 1), f32)
    modulated, scaled_grad, average, inv_scale = call(
        prepare_kernel,
        (block_shape, block_shape, column, column),
        [],
        40 * balanced * model_width,
        8 * balanced * model_width,
        place, rows_all, grad_all, modulation_all, member,
    )
    product = 4 * balanced * model_width * hid
    moved = 4 * model_width * hid
    pre, partial_out = call(
        forward_kernel,
        (shape((balanced, hid), f32), block_shape),
        [pltpu.VMEM((balanced, hid), bf16)],
        product, moved,
        place, modulated, *up, *down,
    )
    (partial_in,) = call(
        backward_kernel,
        (block_shape,),
        [pltpu.VMEM((balanced, hid), f32), pltpu.VMEM((balanced, hid), bf16)],
        product, moved,
        place, scaled_grad, pre, *up, *down,
    )
    branch = scattered_sum(partial_out)
    mod_in_grad = scattered_sum(partial_in)

    shift_scale_gate = [
        jnp.dot(member, modulation[i], precision=lax.Precision.HIGHEST) for i in (1, 2)
    ]
    scale_rows, gate_rows = shift_scale_gate
    rows_f = rows_bal.astype(f32)
    normed = (rows_f - average) * inv_scale
    block_out = (rows_f + gate_rows * branch).astype(bf16)
    grad_f = out_grad.astype(f32)
    normed_grad = mod_in_grad * (1.0 + scale_rows)
    sums = jnp.stack([jnp.sum(normed_grad, axis=1), jnp.sum(normed_grad * normed, axis=1)])
    means = jnp.sum(spread(sums, TP), axis=0) / model_width
    row_grad = (
        grad_f + inv_scale * (normed_grad - means[0][:, None] - normed * means[1][:, None])
    ).astype(bf16)
    local_mod = jnp.stack(
        [
            sample_totals(member, mod_in_grad),
            sample_totals(member, mod_in_grad * normed),
            sample_totals(member, grad_f * branch),
        ]
    )
    mod_grad = summed(summed(summed(local_mod, "c"), "y"), "zh")

    source_first = jnp.mod(position - row_starts[:, None], groups)
    source_rows = source_first + groups * slot_ids
    back_valid = source_rows < live_rows[:, None]
    back_index = (row_starts[:, None] + source_rows - position) // groups
    taken = jnp.take(row_grad, jnp.clip(back_index, 0, balanced - 1).reshape(-1), axis=0)
    returning = jnp.where(back_valid.reshape(-1, 1), taken, jnp.zeros_like(taken)).reshape(
        groups, per_pair, width_local
    )
    arrived = lax.all_to_all(returning, DP, split_axis=0, concat_axis=0, tiled=True)
    own_rows = jnp.arange(slots_in, dtype=jnp.int32)
    target_of = jnp.mod(own_start + own_rows, groups)
    target_slot = own_rows // groups
    gathered_back = jnp.take(
        arrived.reshape(groups * per_pair, width_local), target_of * per_pair + target_slot, axis=0
    )
    input_grad = jnp.where(
        (own_rows < own_live)[:, None], gathered_back, jnp.zeros_like(gathered_back)
    )
    return (block_out, input_grad, mod_grad)


def solution(mesh):
    cut = Mesh(mesh.devices.reshape(SIZES), AXES)
    return jax.shard_map(
        body,
        mesh=cut,
        in_specs=(
            P(DP, TP),
            P(),
            P(),
            P(DP, TP),
            P(TP, DP),
            P(None, None, TP),
            P(DP, TP),
        ),
        out_specs=(P(DP, TP), P(DP, TP), P(None, None, TP)),
        check_vma=False,
    )
```

time: 973 us -> 482 us (0.50)
  waiting for transfers between devices: 575 us -> 124 us
  blocking collectives: 301 us -> 109 us
  starting transfers between devices: 30.8 us -> 153 us
  Pallas kernels: 0 us -> 38.4 us
  matrix products: 27.5 us -> 2.45 us
  local copies, waits for them, and re-layouts: 10.2 us -> 31.5 us
  between operations: 14.3 us -> 1.63 us
    all_gather x4 -> x0, waiting for transfers between devices: 382 us -> none  [the longest x1 119 us: body(): up_whole = lax.all_gather(w_up, 'dp', axis=0, tiled=True)]
    psum x4 -> x0, blocking collectives: 301 us -> none  [the longest x1 175 us: body(): mod_grad = lax.psum(local_mod, 'dp')]
    reduce_scatter x2 -> x0, waiting for transfers between devices: 171 us -> none  [the longest x1 88.6 us: body(): lax.psum_scatter(partial_in.astype(jnp.bfloat16), 'tensor', scatter_dimen...]
    ppermute x0 -> x31, starting transfers between devices: none -> 108 us  [the longest x24 78.7 us: shifted(): lax.ppermute(value, axis, [(i, (i + step) % size) for i in range(size)])]
    all_to_all x0 -> x2, blocking collectives: none -> 68.7 us  [the longest x1 41.7 us: body(): lax.all_to_all(outgoing, DP, split_axis=0, concat_axis=0, tiled=True)]
    all_to_all x2 -> x9, waiting for transfers between devices: 21 us -> 79.2 us  [the longest x5 42.1 us: spread(): return lax.all_to_all(copies, axis, split_axis=0, concat_axis=0, tiled=True)]
    ppermute x0 -> x31, waiting for transfers between devices: none -> 45.2 us  [the longest x24 34.7 us: shifted(): lax.ppermute(value, axis, [(i, (i + step) % size) for i in range(size)])]
    all_gather x0 -> x1, blocking collectives: none -> 40.7 us  [body(): lax.all_gather(modulation.reshape(-1, width_local), TP, axis=0)]
  transfers between devices with their start and end apart: 8 -> 40, of which waited for: 7 -> 15; matrix products, arithmetic and copies ran while one was open for 1% -> 5% of each run, Pallas kernels for 0% -> 2%
where the time goes in v1:
time: 482 us; the launch traced here: 480 us
  starting transfers between devices  153 us (32%)
  waiting for transfers between devices  124 us (26%)
  blocking collectives  109 us (23%)
  Pallas kernels  38.4 us (8%)
  local copies, waits for them, and re-layouts  31.5 us (7%)
  other arithmetic  19.5 us (4%)
    ppermute x24, starting transfers between devices, shifted(): lax.ppermute(value, axis, [(i, (i + step) % size) for i in range(size)])  78.7 us
    all_to_all x5, waiting for transfers between devices, spread(): return lax.all_to_all(copies, axis, split_axis=0, concat_axis=0, tiled=True)  42.1 us
    all_to_all x1, blocking collectives, body(): lax.all_to_all(outgoing, DP, split_axis=0, concat_axis=0, tiled=True)  41.7 us
    all_gather x1, blocking collectives, body(): lax.all_gather(modulation.reshape(-1, width_local), TP, axis=0)  40.7 us
    pallas_call x3, Pallas kernels, call(): pl.pallas_call(kernel, out_shape=outs, in_specs=[SMEM_SPEC] + [VMEM_SPEC]...  38.4 us
    ppermute x24, waiting for transfers between devices, shifted(): lax.ppermute(value, axis, [(i, (i + step) % size) for i in range(size)])  34.7 us
    ppermute x7, starting transfers between devices, crossed(): return lax.ppermute(value, axis, [(i, i ^ mask) for i in range(size)])  29.6 us
    all_to_all x1, blocking collectives, scattered_sum(): lax.all_to_all(blocks, 'x', split_axis=0, concat_axis=0, tiled=True)  27 us
  transfers between devices with their start and end apart: 40, of which 15 were waited for; matrix products, arithmetic and copies ran while one was open for 5% of the time, Pallas kernels for 2%

profile of v1, /device:TPU:2, one launch (start us, length us, event | category | flops | bytes accessed | tf_op | source)
XLA Modules:
  0.0 480.0 jit_solution(5437901318986079460)
XLA Ops:
  7.3 2.6 gather_fusion.2
  10.2 41.7 %all_to_all.55 = bf16[32,24,256]{2,1,0:T(8,128)(2,1)S(1)} all-to-all(bf16[32,24,256]{2,1,0:T(8,128)(2,1)S(1)} %bitcast.47), channel_id=1, replica_groups=mesh['zh'=4,'y'=4,'c'=2,'zl'=4,'x'=4] {'zh','y','c'}, dimensions={0} | all-to-all | bytes 786432 | tf_op jit(solution)/shard_map/all_to_all | solution.py:234
  52.8 6.8 %all-to-all-start.3 = ((bf16[4,256,256]{2,1,0:T(8,128)(2,1)}), bf16[4,256,256]{2,1,0:T(8,128)(2,1)S(1)}, u32[]{:S(2)}, u32[]{:S(2)}) async-start(bf16[4,256,256]{2,1,0:T(8,128)(2,1)} %broadcast_in_dim.117), calls=%async_computation.3 | async-start | bytes 1048576 | tf_op jit(solution)/shard_map/all_to_all | solution.py:66
  61.2 13.9 %all-to-all-done.3 = bf16[4,256,256]{2,1,0:T(8,128)(2,1)S(1)} async-done(((bf16[4,256,256]{2,1,0:T(8,128)(2,1)}), bf16[4,256,256]{2,1,0:T(8,128)(2,1)S(1)}, u32[]{:S(2)}, u32[]{:S(2)}) %all-to-all-start.3) | async-done | bytes 524320 | tf_op jit(solution)/shard_map/all_to_all | solution.py:66
  75.9 3.5 all-to-all-start.1
  79.5 4.3 collective-permute-start.12
  83.8 5.5 %collective-permute-start.14 = (bf16[128,768]{1,0:T(8,128)(2,1)S(1)}, bf16[128,768]{1,0:T(8,128)(2,1)S(1)}, u32[]{:S(2)}, u32[]{:S(2)}) collective-permute-start(bf16[128,768]{1,0:T(8,128)(2,1)S(1)} %bitcast.50), channel_id=1, source_target_pairs={{0,384},{128,0},{256,128},{384,256},{1,385},{129,1},{257,129},{385... | collective-permute-start | bytes 589832 | tf_op jit(solution)/shard_map/ppermute | solution.py:46
  89.3 4.3 collective-permute-start
  93.6 5.5 %collective-permute-start.2 = (bf16[128,768]{1,0:T(8,128)(2,1)S(1)}, bf16[128,768]{1,0:T(8,128)(2,1)S(1)}, u32[]{:S(2)}, u32[]{:S(2)}) collective-permute-start(bf16[128,768]{1,0:T(8,128)(2,1)S(1)} %copy-done.21), channel_id=1, source_target_pairs={{0,384},{128,0},{256,128},{384,256},{1,385},{129,1},{257,129},{385... | collective-permute-start | bytes 589832 | tf_op jit(solution)/shard_map/ppermute | solution.py:46
  99.1 21.4 %all-to-all-done.1 = bf16[4,256,256]{2,1,0:T(8,128)(2,1)S(1)} async-done(((bf16[4,256,256]{2,1,0:T(8,128)(2,1)}), bf16[4,256,256]{2,1,0:T(8,128)(2,1)S(1)}, u32[]{:S(2)}, u32[]{:S(2)}) %all-to-all-start.1) | async-done | bytes 524320 | tf_op jit(solution)/shard_map/all_to_all | solution.py:66
  122.1 4.9 %all-to-all-start.4 = ((bf16[4,4,256,256]{3,2,1,0:T(8,128)(2,1)}), bf16[4,4,256,256]{3,2,1,0:T(8,128)(2,1)}, u32[]{:S(2)}, u32[]{:S(2)}) async-start(bf16[4,4,256,256]{3,2,1,0:T(8,128)(2,1)} %broadcast_in_dim.118), calls=%async_computation.4 | async-start | bytes 4194304 | tf_op jit(solution)/shard_map/all_to_all | solution.py:66
  127.0 3.9 collective-permute-start.13
  131.0 5.8 %collective-permute-start.15 = (bf16[64,768]{1,0:T(8,128)(2,1)S(1)}, bf16[64,768]{1,0:T(8,128)(2,1)S(1)}, u32[]{:S(2)}, u32[]{:S(2)}) collective-permute-start(bf16[64,768]{1,0:T(8,128)(2,1)S(1)} %slice.61), channel_id=1, source_target_pairs={{0,384},{128,0},{256,128},{384,256},{1,385},{129,1},{257,129},{385... | collective-permute-start | bytes 294920 | tf_op jit(solution)/shard_map/ppermute | solution.py:46
  136.8 3.9 collective-permute-start.1
  140.8 5.8 %collective-permute-start.3 = (bf16[64,768]{1,0:T(8,128)(2,1)S(1)}, bf16[64,768]{1,0:T(8,128)(2,1)S(1)}, u32[]{:S(2)}, u32[]{:S(2)}) collective-permute-start(bf16[64,768]{1,0:T(8,128)(2,1)S(1)} %slice.57), channel_id=1, source_target_pairs={{0,384},{128,0},{256,128},{384,256},{1,385},{129,1},{257,129},{385... | collective-permute-start | bytes 294920 | tf_op jit(solution)/shard_map/ppermute | solution.py:46
  147.7 3.1 collective-permute-start.16
  150.8 3.1 collective-permute-done.3
  154.0 3.2 collective-permute-start.4
  157.1 3.9 collective-permute-start.18
  163.0 8.6 %collective-permute-done.16.refs_9_ = bf16[4,128,768]{2,1,0:T(8,128)(2,1)} collective-permute-done((bf16[4,128,768]{2,1,0:T(8,128)(2,1)}, bf16[4,128,768]{2,1,0:T(8,128)(2,1)}, u32[]{:S(2)}, u32[]{:S(2)}) %collective-permute-start.16) | collective-permute-done | bytes 786464 | tf_op jit(solution)/shard_map/ppermute | solution.py:46
  175.2 13.1 %collective-permute-done.4.refs_1_ = bf16[4,128,768]{2,1,0:T(8,128)(2,1)S(1)} collective-permute-done((bf16[4,128,768]{2,1,0:T(8,128)(2,1)S(1)}, bf16[4,128,768]{2,1,0:T(8,128)(2,1)S(1)}, u32[]{:S(2)}, u32[]{:S(2)}) %collective-permute-start.4) | collective-permute-done | bytes 786464 | tf_op jit(solution)/shard_map/ppermute | solution.py:46
  193.6 4.8 all-to-all-start.2
  204.8 5.1 %collective-permute-start.19 = (bf16[2,128,768]{2,1,0:T(8,128)(2,1)S(1)}, bf16[2,128,768]{2,1,0:T(8,128)(2,1)S(1)}, u32[]{:S(2)}, u32[]{:S(2)}) collective-permute-start(bf16[2,128,768]{2,1,0:T(8,128)(2,1)S(1)} %slice.63), channel_id=1, source_target_pairs={{0,96},{32,0},{64,32},{96,64},{1,97},{33,1},{65,33},{97,65},{2,98}... | collective-permute-start | bytes 1179656 | tf_op jit(solution)/shard_map/ppermute | solution.py:46
  214.7 4.6 collective-permute-done.19
  222.0 5.3 %collective-permute-done.7 = bf16[2,128,768]{2,1,0:T(8,128)(2,1)S(1)} collective-permute-done((bf16[2,128,768]{2,1,0:T(8,128)(2,1)S(1)}, bf16[2,128,768]{2,1,0:T(8,128)(2,1)S(1)}, u32[]{:S(2)}, u32[]{:S(2)}) %collective-permute-start.7) | collective-permute-done | bytes 393248 | tf_op jit(solution)/shard_map/ppermute | solution.py:46
  239.4 40.7 %all_gather.3.modulation = f32[16,12,256]{2,1,0:T(8,128)} all-gather(f32[1,12,256]{2,1,0:T(8,128)S(1)} %all_gather_reshape.3), channel_id=1, replica_groups=mesh['zh'=4,'y'=4,'c'=2,'zl'=4,'x'=4] {'zl','x'}, dimensions={0}, use_global_device_ids=true | all-gather | bytes 208896 | tf_op jit(solution)/shard_map/all_gather | solution.py:254
  284.1 8.0 %shard_map.94 = (bf16[4,4,256,256]{3,2,1,0:T(8,128)(2,1)S(1)}, bf16[4,4,256,256]{3,2,1,0:T(8,128)(2,1)S(1)}, f32[256,1]{1,0:T(8,128)S(1)}, f32[256,1]{1,0:T(8,128)S(1)}) custom-call(s32[3]{0:T(128)S(1)} %pad_add_fusion.place, bf16[4,4,256,256]{3,2,1,0:T(8,128)(2,1)} %all-to-all-done.2.rows, bf16[4,4,256,256]{3,2,1,0:T(8,128)(2,1)} %all-to-all-done.4.grad, ...), custom_call_target="tpu_custom_call" | custom-call | flops 41943040 | bytes 8388608 | tf_op jit(solution)/shard_map/pallas_call | solution.py:189
  296.2 15.0 %shard_map.95 = (f32[256,768]{1,0:T(8,128)S(1)}, bf16[4,4,256,256]{3,2,1,0:T(8,128)(2,1)}) custom-call(s32[3]{0:T(128)S(1)} %pad_add_fusion.place, bf16[4,4,256,256]{3,2,1,0:T(8,128)(2,1)} %copy-done.4, bf16[4,128,768]{2,1,0:T(8,128)(2,1)S(1)} %pad_maximum_fusion.refs_0_, bf16[4,128,768]{2,1,0:T(8,128)(2,1)S(1)} %collective-permute-done.4.refs_1_, ...), custom_call_target="tpu_custom_call" | custom-call | flops 3221225472 | bytes 12582912 | tf_op jit(solution)/shard_map/pallas_call | solution.py:189
  311.2 15.3 %shard_map.96 = bf16[4,4,256,256]{3,2,1,0:T(8,128)(2,1)} custom-call(s32[3]{0:T(128)S(1)} %pad_add_fusion.place, bf16[4,4,256,256]{3,2,1,0:T(8,128)(2,1)} %copy-done.3, f32[256,768]{1,0:T(8,128)S(1)} %get-tuple-element.14.pre, bf16[4,128,768]{2,1,0:T(8,128)(2,1)S(1)} %pad_maximum_fusion.refs_0_, bf16[4,128,768]{2,1,0:T(8,128)(2,1)S(1)} %collective-permute-done.4.refs_1_, ...), custom_call_target="tpu_custom_call" | custom-call | flops 3221225472 | bytes 12582912 | tf_op jit(solution)/shard_map/pallas_call | solution.py:189
  326.5 27.0 %all_to_all.56 = bf16[4,4,256,256]{3,2,1,0:T(8,128)(2,1)} all-to-all(bf16[4,4,256,256]{3,2,1,0:T(8,128)(2,1)} %shard_map.96), channel_id=1, replica_groups=mesh['zh'=4,'y'=4,'c'=2,'zl'=4,'x'=4] {'x'}, dimensions={0} | all-to-all | bytes 4194304 | tf_op jit(solution)/shard_map/all_to_all | solution.py:201
  353.5 5.0 %all-to-all-start.5 = ((bf16[4,4,256,256]{3,2,1,0:T(8,128)(2,1)}), bf16[4,4,256,256]{3,2,1,0:T(8,128)(2,1)S(1)}, u32[]{:S(2)}, u32[]{:S(2)}) async-start(bf16[4,4,256,256]{3,2,1,0:T(8,128)(2,1)} %get-tuple-element.11), calls=%async_computation.5 | async-start | bytes 4194304 | tf_op jit(solution)/shard_map/all_to_all | solution.py:201
  358.5 2.8 reduce_sum.114
  361.3 14.7 %all-to-all-done.5 = bf16[4,4,256,256]{3,2,1,0:T(8,128)(2,1)S(1)} async-done(((bf16[4,4,256,256]{3,2,1,0:T(8,128)(2,1)}), bf16[4,4,256,256]{3,2,1,0:T(8,128)(2,1)S(1)}, u32[]{:S(2)}, u32[]{:S(2)}) %all-to-all-start.5) | async-done | bytes 2097184 | tf_op jit(solution)/shard_map/all_to_all | solution.py:201
  376.1 3.5 all-to-all-start.8
  380.9 13.2 %all-to-all-done.8 = bf16[4,256,256]{2,1,0:T(8,128)(2,1)S(1)} async-done(((bf16[4,256,256]{2,1,0:T(8,128)(2,1)}), bf16[4,256,256]{2,1,0:T(8,128)(2,1)S(1)}, u32[]{:S(2)}, u32[]{:S(2)}) %all-to-all-start.8) | async-done | bytes 524320 | tf_op jit(solution)/shard_map/all_to_all | solution.py:203
  394.1 3.5 all-to-all-start.6
  399.0 9.1 %all-to-all-done.6 = bf16[4,256,256]{2,1,0:T(8,128)(2,1)S(1)} async-done(((bf16[4,256,256]{2,1,0:T(8,128)(2,1)}), bf16[4,256,256]{2,1,0:T(8,128)(2,1)S(1)}, u32[]{:S(2)}, u32[]{:S(2)}) %all-to-all-start.6) | async-done | bytes 524320 | tf_op jit(solution)/shard_map/all_to_all | solution.py:203
  408.8 4.8 %all-to-all-start.9 = ((f32[16,2,256]{2,1,0:T(2,128)}), f32[16,2,256]{2,1,0:T(2,128)S(1)}, u32[]{:S(2)}, u32[]{:S(2)}) async-start(f32[16,2,256]{2,1,0:T(2,128)} %broadcast_in_dim.122), calls=%async_computation.9 | async-start | bytes 65536 | tf_op jit(solution)/shard_map/all_to_all | solution.py:66
  413.7 6.7 %all-to-all-done.9 = f32[16,2,256]{2,1,0:T(2,128)S(1)} async-done(((f32[16,2,256]{2,1,0:T(2,128)}), f32[16,2,256]{2,1,0:T(2,128)S(1)}, u32[]{:S(2)}, u32[]{:S(2)}) %all-to-all-start.9) | async-done | bytes 32800 | tf_op jit(solution)/shard_map/all_to_all | solution.py:66
  420.8 2.7 gather_fusion.1
  424.5 7.7 %all-to-all-start.10 = ((bf16[32,24,256]{2,1,0:T(8,128)(2,1)}), bf16[32,24,256]{2,1,0:T(8,128)(2,1)S(1)}, u32[]{:S(2)}, u32[]{:S(2)}) async-start(bf16[32,24,256]{2,1,0:T(8,128)(2,1)} %select_select_fusion.2), calls=%async_computation.10 | async-start | bytes 786432 | tf_op jit(solution)/shard_map/all_to_all | solution.py:319
  436.3 3.7 collective-permute-start.25
  440.0 4.6 collective-permute-start.26
  448.1 3.3 collective-permute-done.27
  451.4 7.3 %collective-permute-start.28 = (f32[3,4,256]{2,1,0:T(4,128)S(1)}, f32[3,4,256]{2,1,0:T(4,128)S(1)}, u32[]{:S(2)}, u32[]{:S(2)}) collective-permute-start(f32[3,4,256]{2,1,0:T(4,128)S(1)} %add_add_fusion.2), channel_id=1, source_target_pairs={{0,128},{128,0},{256,384},{384,256},{1,129},{129,1},{257,385},{385... | collective-permute-start | bytes 36872 | tf_op jit(solution)/shard_map/ppermute | solution.py:51
  458.7 7.5 %collective-permute-start.29 = (f32[3,4,256]{2,1,0:T(4,128)S(1)}, f32[3,4,256]{2,1,0:T(4,128)S(1)}, u32[]{:S(2)}, u32[]{:S(2)}) collective-permute-start(f32[3,4,256]{2,1,0:T(4,128)S(1)} %add_add_fusion.2), channel_id=1, source_target_pairs={{0,256},{128,384},{256,0},{384,128},{1,257},{129,385},{257,1},{385... | collective-permute-start | bytes 36872 | tf_op jit(solution)/shard_map/ppermute | solution.py:51
  469.4 3.6 collective-permute-done.29
  476.3 2.6 gather_fusion.3
  (185 shorter events, 77.3 us)
Async XLA Ops:
  7.3 44.7 %copy-start.17 = (bf16[256,256]{1,0:T(8,128)(2,1)S(1)}, bf16[256,256]{1,0:T(8,128)(2,1)}, u32[]{:S(2)}) copy-start(bf16[256,256]{1,0:T(8,128)(2,1)} %param.15) | copy-start | bytes 393220
  52.8 36.5 %copy-start.21 = (bf16[128,768]{1,0:T(8,128)(2,1)S(1)}, bf16[128,768]{1,0:T(8,128)(2,1)}, u32[]{:S(2)}) copy-start(bf16[128,768]{1,0:T(8,128)(2,1)} %param.12) | copy-start | bytes 589828
  52.8 22.2 %all-to-all-start.3 = ((bf16[4,256,256]{2,1,0:T(8,128)(2,1)}), bf16[4,256,256]{2,1,0:T(8,128)(2,1)S(1)}, u32[]{:S(2)}, u32[]{:S(2)}) async-start(bf16[4,256,256]{2,1,0:T(8,128)(2,1)} %broadcast_in_dim.117), calls=%async_computation.3 | async-start | bytes 1048576 | tf_op jit(solution)/shard_map/all_to_all | solution.py:66
  61.2 60.9 %copy-start.12 = (bf16[256,256]{1,0:T(8,128)(2,1)}, bf16[256,256]{1,0:T(8,128)(2,1)S(1)}, u32[]{:S(2)}) copy-start(bf16[256,256]{1,0:T(8,128)(2,1)S(1)} %broadcast_select_fusion) | copy-start | bytes 393220
  75.9 44.6 %all-to-all-start.1 = ((bf16[4,256,256]{2,1,0:T(8,128)(2,1)}), bf16[4,256,256]{2,1,0:T(8,128)(2,1)S(1)}, u32[]{:S(2)}, u32[]{:S(2)}) async-start(bf16[4,256,256]{2,1,0:T(8,128)(2,1)} %broadcast_in_dim.115), calls=%async_computation.1 | async-start | bytes 1048576 | tf_op jit(solution)/shard_map/all_to_all | solution.py:66
  79.5 47.5 %collective-permute-start.12 = (bf16[128,768]{1,0:T(8,128)(2,1)S(1)}, bf16[128,768]{1,0:T(8,128)(2,1)S(1)}, u32[]{:S(2)}, u32[]{:S(2)}) collective-permute-start(bf16[128,768]{1,0:T(8,128)(2,1)S(1)} %bitcast.49), channel_id=1, source_target_pairs={{0,128},{128,256},{256,384},{384,0},{1,129},{129,257},{257,385},{3... | collective-permute-start | bytes 589832 | tf_op jit(solution)/shard_map/ppermute | solution.py:46
  83.8 47.1 %collective-permute-start.14 = (bf16[128,768]{1,0:T(8,128)(2,1)S(1)}, bf16[128,768]{1,0:T(8,128)(2,1)S(1)}, u32[]{:S(2)}, u32[]{:S(2)}) collective-permute-start(bf16[128,768]{1,0:T(8,128)(2,1)S(1)} %bitcast.50), channel_id=1, source_target_pairs={{0,384},{128,0},{256,128},{384,256},{1,385},{129,1},{257,129},{385... | collective-permute-start | bytes 589832 | tf_op jit(solution)/shard_map/ppermute | solution.py:46
  89.3 47.5 %collective-permute-start = (bf16[128,768]{1,0:T(8,128)(2,1)S(1)}, bf16[128,768]{1,0:T(8,128)(2,1)S(1)}, u32[]{:S(2)}, u32[]{:S(2)}) collective-permute-start(bf16[128,768]{1,0:T(8,128)(2,1)S(1)} %copy-done.21), channel_id=1, source_target_pairs={{0,128},{128,256},{256,384},{384,0},{1,129},{129,257},{257,385},{3... | collective-permute-start | bytes 589832 | tf_op jit(solution)/shard_map/ppermute | solution.py:46
  93.6 47.2 %collective-permute-start.2 = (bf16[128,768]{1,0:T(8,128)(2,1)S(1)}, bf16[128,768]{1,0:T(8,128)(2,1)S(1)}, u32[]{:S(2)}, u32[]{:S(2)}) collective-permute-start(bf16[128,768]{1,0:T(8,128)(2,1)S(1)} %copy-done.21), channel_id=1, source_target_pairs={{0,384},{128,0},{256,128},{384,256},{1,385},{129,1},{257,129},{385... | collective-permute-start | bytes 589832 | tf_op jit(solution)/shard_map/ppermute | solution.py:46
  122.1 68.9 %all-to-all-start.4 = ((bf16[4,4,256,256]{3,2,1,0:T(8,128)(2,1)}), bf16[4,4,256,256]{3,2,1,0:T(8,128)(2,1)}, u32[]{:S(2)}, u32[]{:S(2)}) async-start(bf16[4,4,256,256]{3,2,1,0:T(8,128)(2,1)} %broadcast_in_dim.118), calls=%async_computation.4 | async-start | bytes 4194304 | tf_op jit(solution)/shard_map/all_to_all | solution.py:66
  127.0 19.6 %collective-permute-start.13 = (bf16[64,768]{1,0:T(8,128)(2,1)S(1)}, bf16[64,768]{1,0:T(8,128)(2,1)S(1)}, u32[]{:S(2)}, u32[]{:S(2)}) collective-permute-start(bf16[64,768]{1,0:T(8,128)(2,1)S(1)} %slice.60), channel_id=1, source_target_pairs={{0,128},{128,256},{256,384},{384,0},{1,129},{129,257},{257,385},{3... | collective-permute-start | bytes 294920 | tf_op jit(solution)/shard_map/ppermute | solution.py:46
  131.0 15.7 %collective-permute-start.15 = (bf16[64,768]{1,0:T(8,128)(2,1)S(1)}, bf16[64,768]{1,0:T(8,128)(2,1)S(1)}, u32[]{:S(2)}, u32[]{:S(2)}) collective-permute-start(bf16[64,768]{1,0:T(8,128)(2,1)S(1)} %slice.61), channel_id=1, source_target_pairs={{0,384},{128,0},{256,128},{384,256},{1,385},{129,1},{257,129},{385... | collective-permute-start | bytes 294920 | tf_op jit(solution)/shard_map/ppermute | solution.py:46
  136.8 13.9 %collective-permute-start.1 = (bf16[64,768]{1,0:T(8,128)(2,1)S(1)}, bf16[64,768]{1,0:T(8,128)(2,1)S(1)}, u32[]{:S(2)}, u32[]{:S(2)}) collective-permute-start(bf16[64,768]{1,0:T(8,128)(2,1)S(1)} %slice.56), channel_id=1, source_target_pairs={{0,128},{128,256},{256,384},{384,0},{1,129},{129,257},{257,385},{3... | collective-permute-start | bytes 294920 | tf_op jit(solution)/shard_map/ppermute | solution.py:46
  140.8 13.0 %collective-permute-start.3 = (bf16[64,768]{1,0:T(8,128)(2,1)S(1)}, bf16[64,768]{1,0:T(8,128)(2,1)S(1)}, u32[]{:S(2)}, u32[]{:S(2)}) collective-permute-start(bf16[64,768]{1,0:T(8,128)(2,1)S(1)} %slice.57), channel_id=1, source_target_pairs={{0,384},{128,0},{256,128},{384,256},{1,385},{129,1},{257,129},{385... | collective-permute-start | bytes 294920 | tf_op jit(solution)/shard_map/ppermute | solution.py:46
  147.7 23.9 %collective-permute-start.16 = (bf16[4,128,768]{2,1,0:T(8,128)(2,1)}, bf16[4,128,768]{2,1,0:T(8,128)(2,1)}, u32[]{:S(2)}, u32[]{:S(2)}) collective-permute-start(bf16[4,128,768]{2,1,0:T(8,128)(2,1)} %pad_maximum_fusion.1.refs_8_), channel_id=1, source_target_pairs={{0,32},{32,64},{64,96},{96,0},{1,33},{33,65},{65,97},{97,1},{2,34}... | collective-permute-start | bytes 2359304 | tf_op jit(solution)/shard_map/ppermute | solution.py:46
  154.0 34.3 %collective-permute-start.4 = (bf16[4,128,768]{2,1,0:T(8,128)(2,1)S(1)}, bf16[4,128,768]{2,1,0:T(8,128)(2,1)S(1)}, u32[]{:S(2)}, u32[]{:S(2)}) collective-permute-start(bf16[4,128,768]{2,1,0:T(8,128)(2,1)S(1)} %pad_maximum_fusion.refs_0_), channel_id=1, source_target_pairs={{0,32},{32,64},{64,96},{96,0},{1,33},{33,65},{65,97},{97,1},{2,34}... | collective-permute-start | bytes 2359304 | tf_op jit(solution)/shard_map/ppermute | solution.py:46
  157.1 43.2 %collective-permute-start.18 = (bf16[4,128,768]{2,1,0:T(8,128)(2,1)}, bf16[4,128,768]{2,1,0:T(8,128)(2,1)S(1)}, u32[]{:S(2)}, u32[]{:S(2)}) collective-permute-start(bf16[4,128,768]{2,1,0:T(8,128)(2,1)} %pad_maximum_fusion.1.refs_8_), channel_id=1, source_target_pairs={{0,96},{32,0},{64,32},{96,64},{1,97},{33,1},{65,33},{97,65},{2,98}... | collective-permute-start | bytes 2359304 | tf_op jit(solution)/shard_map/ppermute | solution.py:46
  161.0 41.8 %collective-permute-start.6 = (bf16[4,128,768]{2,1,0:T(8,128)(2,1)S(1)}, bf16[4,128,768]{2,1,0:T(8,128)(2,1)S(1)}, u32[]{:S(2)}, u32[]{:S(2)}) collective-permute-start(bf16[4,128,768]{2,1,0:T(8,128)(2,1)S(1)} %pad_maximum_fusion.refs_0_), channel_id=1, source_target_pairs={{0,96},{32,0},{64,32},{96,64},{1,97},{33,1},{65,33},{97,65},{2,98}... | collective-permute-start | bytes 2359304 | tf_op jit(solution)/shard_map/ppermute | solution.py:46
  173.3 31.5 %collective-permute-start.17 = (bf16[2,128,768]{2,1,0:T(8,128)(2,1)}, bf16[2,128,768]{2,1,0:T(8,128)(2,1)}, u32[]{:S(2)}, u32[]{:S(2)}) collective-permute-start(bf16[2,128,768]{2,1,0:T(8,128)(2,1)} %slice.62), channel_id=1, source_target_pairs={{0,32},{32,64},{64,96},{96,0},{1,33},{33,65},{65,97},{97,1},{2,34}... | collective-permute-start | bytes 1179656 | tf_op jit(solution)/shard_map/ppermute | solution.py:46
  189.1 20.9 %collective-permute-start.5 = (bf16[2,128,768]{2,1,0:T(8,128)(2,1)}, bf16[2,128,768]{2,1,0:T(8,128)(2,1)}, u32[]{:S(2)}, u32[]{:S(2)}) collective-permute-start(bf16[2,128,768]{2,1,0:T(8,128)(2,1)} %slice.58), channel_id=1, source_target_pairs={{0,32},{32,64},{64,96},{96,0},{1,33},{33,65},{65,97},{97,1},{2,34}... | collective-permute-start | bytes 1179656 | tf_op jit(solution)/shard_map/ppermute | solution.py:46
  193.6 88.6 %all-to-all-start.2 = ((bf16[4,4,256,256]{3,2,1,0:T(8,128)(2,1)}), bf16[4,4,256,256]{3,2,1,0:T(8,128)(2,1)}, u32[]{:S(2)}, u32[]{:S(2)}) async-start(bf16[4,4,256,256]{3,2,1,0:T(8,128)(2,1)} %broadcast_in_dim.116), calls=%async_computation.2 | async-start | bytes 4194304 | tf_op jit(solution)/shard_map/all_to_all | solution.py:66
  198.4 30.9 %collective-permute-start.20 = (bf16[4,128,768]{2,1,0:T(8,128)(2,1)}, bf16[4,128,768]{2,1,0:T(8,128)(2,1)S(1)}, u32[]{:S(2)}, u32[]{:S(2)}) collective-permute-start(bf16[4,128,768]{2,1,0:T(8,128)(2,1)} %pad_maximum_fusion.1.refs_8_), channel_id=1, source_target_pairs={{0,16},{16,0},{1,17},{17,1},{2,18},{18,2},{3,19},{19,3},{4,20},{20... | collective-permute-start | bytes 2359304 | tf_op jit(solution)/shard_map/ppermute | solution.py:46
  200.4 31.4 %collective-permute-start.8 = (bf16[4,128,768]{2,1,0:T(8,128)(2,1)S(1)}, bf16[4,128,768]{2,1,0:T(8,128)(2,1)S(1)}, u32[]{:S(2)}, u32[]{:S(2)}) collective-permute-start(bf16[4,128,768]{2,1,0:T(8,128)(2,1)S(1)} %pad_maximum_fusion.refs_0_), channel_id=1, source_target_pairs={{0,16},{16,0},{1,17},{17,1},{2,18},{18,2},{3,19},{19,3},{4,20},{20... | collective-permute-start | bytes 2359304 | tf_op jit(solution)/shard_map/ppermute | solution.py:46
  202.8 31.8 %collective-permute-start.21 = (bf16[4,128,768]{2,1,0:T(8,128)(2,1)}, bf16[4,128,768]{2,1,0:T(8,128)(2,1)S(1)}, u32[]{:S(2)}, u32[]{:S(2)}) collective-permute-start(bf16[4,128,768]{2,1,0:T(8,128)(2,1)} %collective-permute-done.16.refs_9_), channel_id=1, source_target_pairs={{0,16},{16,0},{1,17},{17,1},{2,18},{18,2},{3,19},{19,3},{4,20},{20... | collective-permute-start | bytes 2359304 | tf_op jit(solution)/shard_map/ppermute | solution.py:46
  204.8 33.1 %copy-start.32 = (s32[4]{0:T(128)S(1)}, s32[4]{0:T(128)}, u32[]{:S(2)}) copy-start(s32[4]{0:T(128)} %param.11) | copy-start | bytes 52
  204.8 14.5 %collective-permute-start.19 = (bf16[2,128,768]{2,1,0:T(8,128)(2,1)S(1)}, bf16[2,128,768]{2,1,0:T(8,128)(2,1)S(1)}, u32[]{:S(2)}, u32[]{:S(2)}) collective-permute-start(bf16[2,128,768]{2,1,0:T(8,128)(2,1)S(1)} %slice.63), channel_id=1, source_target_pairs={{0,96},{32,0},{64,32},{96,64},{1,97},{33,1},{65,33},{97,65},{2,98}... | collective-permute-start | bytes 1179656 | tf_op jit(solution)/shard_map/ppermute | solution.py:46
  210.0 17.4 %collective-permute-start.7 = (bf16[2,128,768]{2,1,0:T(8,128)(2,1)S(1)}, bf16[2,128,768]{2,1,0:T(8,128)(2,1)S(1)}, u32[]{:S(2)}, u32[]{:S(2)}) collective-permute-start(bf16[2,128,768]{2,1,0:T(8,128)(2,1)S(1)} %slice.59), channel_id=1, source_target_pairs={{0,96},{32,0},{64,32},{96,64},{1,97},{33,1},{65,33},{97,65},{2,98}... | collective-permute-start | bytes 1179656 | tf_op jit(solution)/shard_map/ppermute | solution.py:46
  219.3 76.8 %collective-permute-start.23 = (bf16[4,128,768]{2,1,0:T(8,128)(2,1)}, bf16[4,128,768]{2,1,0:T(8,128)(2,1)}, u32[]{:S(2)}, u32[]{:S(2)}) collective-permute-start(bf16[4,128,768]{2,1,0:T(8,128)(2,1)} %copy-done.11), channel_id=1, source_target_pairs={{0,16},{16,0},{1,17},{17,1},{2,18},{18,2},{3,19},{19,3},{4,20},{20... | collective-permute-start | bytes 2359304 | tf_op jit(solution)/shard_map/ppermute | solution.py:46
  227.4 68.8 %collective-permute-start.11 = (bf16[4,128,768]{2,1,0:T(8,128)(2,1)S(1)}, bf16[4,128,768]{2,1,0:T(8,128)(2,1)}, u32[]{:S(2)}, u32[]{:S(2)}) collective-permute-start(bf16[4,128,768]{2,1,0:T(8,128)(2,1)S(1)} %collective-permute-done.6.refs_3_), channel_id=1, source_target_pairs={{0,16},{16,0},{1,17},{17,1},{2,18},{18,2},{3,19},{19,3},{4,20},{20... | collective-permute-start | bytes 2359304 | tf_op jit(solution)/shard_map/ppermute | solution.py:46
  229.3 66.8 %collective-permute-start.9 = (bf16[4,128,768]{2,1,0:T(8,128)(2,1)S(1)}, bf16[4,128,768]{2,1,0:T(8,128)(2,1)}, u32[]{:S(2)}, u32[]{:S(2)}) collective-permute-start(bf16[4,128,768]{2,1,0:T(8,128)(2,1)S(1)} %collective-permute-done.4.refs_1_), channel_id=1, source_target_pairs={{0,16},{16,0},{1,17},{17,1},{2,18},{18,2},{3,19},{19,3},{4,20},{20... | collective-permute-start | bytes 2359304 | tf_op jit(solution)/shard_map/ppermute | solution.py:46
  232.6 63.5 %collective-permute-start.22 = (bf16[4,128,768]{2,1,0:T(8,128)(2,1)}, bf16[4,128,768]{2,1,0:T(8,128)(2,1)}, u32[]{:S(2)}, u32[]{:S(2)}) collective-permute-start(bf16[4,128,768]{2,1,0:T(8,128)(2,1)} %constant_dynamic-update-slice_fusion.2.refs_10_), channel_id=1, source_target_pairs={{0,16},{16,0},{1,17},{17,1},{2,18},{18,2},{3,19},{19,3},{4,20},{20... | collective-permute-start | bytes 2359304 | tf_op jit(solution)/shard_map/ppermute | solution.py:46
  235.5 60.7 %collective-permute-start.10 = (bf16[4,128,768]{2,1,0:T(8,128)(2,1)S(1)}, bf16[4,128,768]{2,1,0:T(8,128)(2,1)}, u32[]{:S(2)}, u32[]{:S(2)}) collective-permute-start(bf16[4,128,768]{2,1,0:T(8,128)(2,1)S(1)} %constant_dynamic-update-slice_fusion.refs_2_), channel_id=1, source_target_pairs={{0,16},{16,0},{1,17},{17,1},{2,18},{18,2},{3,19},{19,3},{4,20},{20... | collective-permute-start | bytes 2359304 | tf_op jit(solution)/shard_map/ppermute | solution.py:46
  353.5 22.6 %all-to-all-start.5 = ((bf16[4,4,256,256]{3,2,1,0:T(8,128)(2,1)}), bf16[4,4,256,256]{3,2,1,0:T(8,128)(2,1)S(1)}, u32[]{:S(2)}, u32[]{:S(2)}) async-start(bf16[4,4,256,256]{3,2,1,0:T(8,128)(2,1)} %get-tuple-element.11), calls=%async_computation.5 | async-start | bytes 4194304 | tf_op jit(solution)/shard_map/all_to_all | solution.py:201
  376.1 18.0 %all-to-all-start.8 = ((bf16[4,256,256]{2,1,0:T(8,128)(2,1)}), bf16[4,256,256]{2,1,0:T(8,128)(2,1)S(1)}, u32[]{:S(2)}, u32[]{:S(2)}) async-start(bf16[4,256,256]{2,1,0:T(8,128)(2,1)} %reduce_sum.114), calls=%async_computation.8 | async-start | bytes 1048576 | tf_op jit(solution)/shard_map/all_to_all | solution.py:203
  380.9 39.6 %copy-start.18 = (bf16[256,256]{1,0:T(8,128)(2,1)S(1)}, bf16[256,256]{1,0:T(8,128)(2,1)}, u32[]{:S(2)}) copy-start(bf16[256,256]{1,0:T(8,128)(2,1)} %param.15) | copy-start | bytes 393220
  380.9 39.6 %copy-start.20 = (bf16[256,256]{1,0:T(8,128)(2,1)S(1)}, bf16[256,256]{1,0:T(8,128)(2,1)}, u32[]{:S(2)}) copy-start(bf16[256,256]{1,0:T(8,128)(2,1)} %copy-done.19) | copy-start | bytes 393220
  380.9 39.6 %copy-start.31 = (pred[256]{0:T(512)(128)(4,1)S(1)}, pred[256]{0:T(512)(128)(4,1)}, u32[]{:S(2)}) copy-start(pred[256]{0:T(512)(128)(4,1)} %copy-done.30) | copy-start | bytes 772
  380.9 39.9 %copy-start.29 = (s32[1024]{0:T(1024)S(1)}, s32[1024]{0:T(1024)}, u32[]{:S(2)}) copy-start(s32[1024]{0:T(1024)} %get-tuple-element.29) | copy-start | bytes 12292
  394.1 14.1 %all-to-all-start.6 = ((bf16[4,256,256]{2,1,0:T(8,128)(2,1)}), bf16[4,256,256]{2,1,0:T(8,128)(2,1)S(1)}, u32[]{:S(2)}, u32[]{:S(2)}) async-start(bf16[4,256,256]{2,1,0:T(8,128)(2,1)} %reduce_sum.112), calls=%async_computation.6 | async-start | bytes 1048576 | tf_op jit(solution)/shard_map/all_to_all | solution.py:203
  408.8 11.6 %all-to-all-start.9 = ((f32[16,2,256]{2,1,0:T(2,128)}), f32[16,2,256]{2,1,0:T(2,128)S(1)}, u32[]{:S(2)}, u32[]{:S(2)}) async-start(f32[16,2,256]{2,1,0:T(2,128)} %broadcast_in_dim.122), calls=%async_computation.9 | async-start | bytes 65536 | tf_op jit(solution)/shard_map/all_to_all | solution.py:66
  424.5 51.8 %all-to-all-start.10 = ((bf16[32,24,256]{2,1,0:T(8,128)(2,1)}), bf16[32,24,256]{2,1,0:T(8,128)(2,1)S(1)}, u32[]{:S(2)}, u32[]{:S(2)}) async-start(bf16[32,24,256]{2,1,0:T(8,128)(2,1)} %select_select_fusion.2), calls=%async_computation.10 | async-start | bytes 786432 | tf_op jit(solution)/shard_map/all_to_all | solution.py:319
  433.3 3.1 collective-permute-start.24
  436.3 11.7 %collective-permute-start.25 = (f32[3,4,256]{2,1,0:T(4,128)S(1)}, f32[3,4,256]{2,1,0:T(4,128)S(1)}, u32[]{:S(2)}, u32[]{:S(2)}) collective-permute-start(f32[3,4,256]{2,1,0:T(4,128)S(1)} %fusion.36), channel_id=1, source_target_pairs={{0,32},{32,0},{64,96},{96,64},{1,33},{33,1},{65,97},{97,65},{2,34}... | collective-permute-start | bytes 36872 | tf_op jit(solution)/shard_map/ppermute | solution.py:51
  440.0 8.0 %collective-permute-start.26 = (f32[3,4,256]{2,1,0:T(4,128)S(1)}, f32[3,4,256]{2,1,0:T(4,128)S(1)}, u32[]{:S(2)}, u32[]{:S(2)}) collective-permute-start(f32[3,4,256]{2,1,0:T(4,128)S(1)} %fusion.36), channel_id=1, source_target_pairs={{0,64},{32,96},{64,0},{96,32},{1,65},{33,97},{65,1},{97,33},{2,66}... | collective-permute-start | bytes 36872 | tf_op jit(solution)/shard_map/ppermute | solution.py:51
  444.6 6.8 %collective-permute-start.27 = (f32[3,4,256]{2,1,0:T(4,128)S(1)}, f32[3,4,256]{2,1,0:T(4,128)S(1)}, u32[]{:S(2)}, u32[]{:S(2)}) collective-permute-start(f32[3,4,256]{2,1,0:T(4,128)S(1)} %fusion.36), channel_id=1, source_target_pairs={{0,96},{32,64},{64,32},{96,0},{1,97},{33,65},{65,33},{97,1},{2,98}... | collective-permute-start | bytes 36872 | tf_op jit(solution)/shard_map/ppermute | solution.py:51
  451.4 18.0 %collective-permute-start.28 = (f32[3,4,256]{2,1,0:T(4,128)S(1)}, f32[3,4,256]{2,1,0:T(4,128)S(1)}, u32[]{:S(2)}, u32[]{:S(2)}) collective-permute-start(f32[3,4,256]{2,1,0:T(4,128)S(1)} %add_add_fusion.2), channel_id=1, source_target_pairs={{0,128},{128,0},{256,384},{384,256},{1,129},{129,1},{257,385},{385... | collective-permute-start | bytes 36872 | tf_op jit(solution)/shard_map/ppermute | solution.py:51
  458.7 14.3 %collective-permute-start.29 = (f32[3,4,256]{2,1,0:T(4,128)S(1)}, f32[3,4,256]{2,1,0:T(4,128)S(1)}, u32[]{:S(2)}, u32[]{:S(2)}) collective-permute-start(f32[3,4,256]{2,1,0:T(4,128)S(1)} %add_add_fusion.2), channel_id=1, source_target_pairs={{0,256},{128,384},{256,0},{384,128},{1,257},{129,385},{257,1},{385... | collective-permute-start | bytes 36872 | tf_op jit(solution)/shard_map/ppermute | solution.py:51
  466.2 9.5 %collective-permute-start.30 = (f32[3,4,256]{2,1,0:T(4,128)S(1)}, f32[3,4,256]{2,1,0:T(4,128)S(1)}, u32[]{:S(2)}, u32[]{:S(2)}) collective-permute-start(f32[3,4,256]{2,1,0:T(4,128)S(1)} %add_add_fusion.2), channel_id=1, source_target_pairs={{0,384},{128,256},{256,128},{384,0},{1,385},{129,257},{257,129},{3... | collective-permute-start | bytes 36872 | tf_op jit(solution)/shard_map/ppermute | solution.py:51
  (25 other events, 237.7 us)

commit v2 on v1

v2 whole, which is shorter than its diff:
```python
import functools

import jax
import jax.numpy as jnp
from jax import lax
from jax.experimental import pallas as pl
from jax.experimental.pallas import tpu as pltpu
from jax.sharding import Mesh, PartitionSpec as P

GELU_K = 0.7978845608028654
GELU_C = 0.044715
EPS = 1e-06
AXES = ("zh", "y", "c", "zl", "x")
SIZES = (4, 4, 2, 4, 4)
DP = ("zh", "y", "c")
TP = ("zl", "x")
SAMPLES = 4
VMEM = 48 * 1024 * 1024
US = 10**9


def gelu_value(pre):
    inner = GELU_K * (pre + GELU_C * pre * pre * pre)
    return 0.5 * pre * (1.0 + jnp.tanh(inner))


def gelu_slope(pre):
    inner = GELU_K * (pre + GELU_C * pre * pre * pre)
    tangent = jnp.tanh(inner)
    return 0.5 * (1.0 + tangent) + 0.5 * pre * (1.0 - tangent * tangent) * GELU_K * (
        1.0 + 3.0 * GELU_C * pre * pre
    )


def shifted(value, axis, step):
    size = lax.axis_size(axis)
    return lax.ppermute(value, axis, [(i, (i + step) % size) for i in range(size)])


def crossed(value, axis, mask):
    size = lax.axis_size(axis)
    return lax.ppermute(value, axis, [(i, i ^ mask) for i in range(size)])


def direct_pieces(value, axis):
    return jnp.stack([value] + [shifted(value, axis, k) for k in (1, 2, 3)])


def spread(value, axis):
    copies = jnp.broadcast_to(value[None], (lax.axis_size(axis),) + value.shape)
    return lax.all_to_all(copies, axis, split_axis=0, concat_axis=0, tiled=True)


def summed(value, axis):
    mask = 1
    while mask < lax.axis_size(axis):
        value = value + crossed(value, axis, mask)
        mask *= 2
    return value


def three_terms(value):
    terms = []
    for _ in range(3):
        term = lax.reduce_precision(value, 8, 7)
        terms.append(term.astype(jnp.bfloat16))
        value = value - term
    return terms


def sample_mix(member, table):
    out = jnp.broadcast_to(table[SAMPLES - 1 : SAMPLES], (member.shape[0], table.shape[1]))
    for q in range(SAMPLES - 1):
        out = jnp.where(member[:, q : q + 1] > 0.5, table[q : q + 1], out)
    return out


def halves(c, half):
    first = pl.ds(pl.multiple_of(c * half, half), half)
    second = pl.ds(pl.multiple_of((1 - c) * half, half), half)
    return first, second


def zh_of(zh, n, count):
    step = jnp.where(n == 1, count - 1, jnp.where(n == 2, 1, jnp.where(n == 3, 2, 0)))
    return lax.rem(zh + step, count)


def weight_of(first, first_other, last, last_other, n, which):
    own, other = (first, first_other) if n < 3 else (last, last_other)
    return jnp.concatenate([own[0, n % 3, which], other[0, n % 3, which]], axis=0)


def gate_kernel(place, gathered, member, grad_out, table_out):
    y, zh, c = place[0], place[1], place[2]
    live = member[...]
    count = grad_out.shape[0]
    rows = grad_out.shape[2]
    half = grad_out.shape[3] // 2

    def step(index, carry):
        dy, n = index // count, index % count
        xi = lax.rem(y - dy + count, count)
        zi = zh_of(zh, n, count)
        block = zi * count + xi
        terms = gathered[block, rows : rows + 48].astype(jnp.float32)
        table = (terms[0:16] + terms[16:32]) + terms[32:48]
        table_out[block] = table
        grad = gathered[block, 0:rows].astype(jnp.float32)
        gated = (sample_mix(live, table[8:12]) * grad).astype(jnp.bfloat16)
        first, second = halves(c, half)
        grad_out[dy, n, :, first] = gated[:, :half]
        grad_out[dy, n, :, second] = gated[:, half:]
        return carry

    lax.fori_loop(0, count * count, step, 0)


def rows_kernel(place, rows, table_in, member, mod_out, average, inv_scale):
    y, zh, c = place[0], place[1], place[2]
    live = member[...]
    count = rows.shape[0]
    balanced = rows.shape[2]
    width = rows.shape[3]
    half = width // 2
    features = count * count * width

    total = jnp.zeros(rows.shape[2:], jnp.float32)
    for i in range(count):
        for j in range(count):
            total = total + rows[i, j].astype(jnp.float32)
    mean = jnp.sum(total, axis=1, keepdims=True) / features
    total = jnp.zeros(rows.shape[2:], jnp.float32)
    for i in range(count):
        for j in range(count):
            centred = rows[i, j].astype(jnp.float32) - mean
            total = total + centred * centred
    inv = lax.rsqrt(jnp.sum(total, axis=1, keepdims=True) / features + EPS)
    average[...] = mean
    inv_scale[...] = inv

    def step(index, carry):
        dy, n = index // count, index % count
        xi = lax.rem(y - dy + count, count)
        zi = zh_of(zh, n, count)
        table = table_in[zi * count + xi]
        shift, scale = table[0:4], 1.0 + table[4:8]
        normed = (rows[xi, zi].astype(jnp.float32) - mean) * inv
        value = (normed * sample_mix(live, scale) + sample_mix(live, shift)).astype(jnp.bfloat16)
        scale_hi = scale.astype(jnp.bfloat16).astype(jnp.float32)
        shift_hi = shift.astype(jnp.bfloat16).astype(jnp.float32)
        extra = jnp.concatenate(
            [scale_hi, scale - scale_hi, shift_hi, shift - shift_hi], axis=0
        ).astype(jnp.bfloat16)
        first, second = halves(c, half)
        mod_out[dy, n, 0:balanced, first] = value[:, :half]
        mod_out[dy, n, 0:balanced, second] = value[:, half:]
        mod_out[dy, n, balanced : balanced + 16, first] = extra[:, :half]
        mod_out[dy, n, balanced : balanced + 16, second] = extra[:, half:]
        return carry

    lax.fori_loop(0, count * count, step, 0)


def hidden_kernel(
    modulated, scaled, member, first, first_other, last, last_other,
    hidden_out, pre_grad_out, sums_out, pre_total, grad_total,
):
    live = member[...]
    rows = scaled.shape[2]
    step = pl.program_id(0)

    @pl.when(step == 0)
    def _():
        pre_total[...] = jnp.zeros_like(pre_total)
        grad_total[...] = jnp.zeros_like(grad_total)

    for n in range(scaled.shape[1]):
        up = weight_of(first, first_other, last, last_other, n, 0)
        pre_total[...] += jnp.dot(modulated[0, n], up, preferred_element_type=jnp.float32)
        down = weight_of(first, first_other, last, last_other, n, 1)
        grad_total[...] += jnp.dot(scaled[0, n], down, preferred_element_type=jnp.float32)

    @pl.when(step == pl.num_programs(0) - 1)
    def _():
        pre = pre_total[0:rows]
        extra = pre_total[rows : rows + 16]
        hidden_out[...] = gelu_value(pre).astype(jnp.bfloat16).T
        pre_grad = (grad_total[...] * gelu_slope(pre)).astype(jnp.bfloat16)
        pre_grad_out[...] = pre_grad.T
        pre_grad = pre_grad.astype(jnp.float32)
        scale_part = sample_mix(live, extra[0:4] + extra[4:8])
        shift_part = sample_mix(live, extra[8:12] + extra[12:16])
        first = jnp.sum(pre_grad * scale_part, axis=1, keepdims=True)
        second = jnp.sum(pre_grad * (pre - shift_part), axis=1, keepdims=True)
        lane = lax.broadcasted_iota(jnp.int32, (rows, 128), 1)
        both = jnp.where(lane == 0, first, jnp.where(lane == 1, second, 0.0))
        sums = both.T[0:8]
        high = sums.astype(jnp.bfloat16).astype(jnp.float32)
        sums_out[...] = jnp.concatenate([high, sums - high], axis=0).astype(jnp.bfloat16)


def outward_kernel(place, hidden, first, first_other, last, last_other, *refs):
    out = refs[-1]
    zh, c = place[1], place[2]
    count = out.shape[1]
    rows = out.shape[3]
    half = rows // 2
    low, high = halves(c, half)
    for n in range(count):
        weight = weight_of(first, first_other, last, last_other, n, 0)
        value = jnp.dot(weight, hidden[...], preferred_element_type=jnp.float32).astype(
            jnp.bfloat16
        )
        zi = zh_of(zh, n, count)
        out[0, zi, low, :] = value[:half]
        out[0, zi, high, :] = value[half:]
        if len(refs) == 2:
            out[0, zi, rows : rows + 16, :] = refs[0][...]


def joined_sums(terms):
    total = terms[0:8] + terms[8:16]
    high = total.astype(jnp.bfloat16).astype(jnp.float32)
    return jnp.concatenate([high, total - high], axis=0)


def fold_kernel(place, blocks, *refs):
    zl = place[3]
    count, places, height, width = blocks.shape
    out = refs[0] if height > width else refs[2]

    def step(m, carry):
        total = blocks[0, m].astype(jnp.float32)
        for k in range(1, count):
            total = total + blocks[k, m].astype(jnp.float32)
        to = lax.rem(m - zl + places, places)
        out[to, 0:width] = total[0:width].astype(jnp.bfloat16)
        if height > width:
            out[to, width:height] = joined_sums(total[width:height]).astype(jnp.bfloat16)
        else:
            grad, member, _, totals = refs
            part = image_sums(member[...], grad[m].astype(jnp.float32) * total.T)
            totals[to] = jnp.concatenate(part, axis=0)
        return carry

    lax.fori_loop(0, places, step, 0)


def picked(index, values):
    lanes = lax.broadcasted_iota(jnp.int32, (index.shape[0], values.shape[0]), 1)
    chosen = jnp.where(lanes == index, 1.0, 0.0).astype(jnp.bfloat16)
    return jnp.dot(chosen, values, preferred_element_type=jnp.float32).astype(jnp.bfloat16)


def image_sums(live, values):
    return [
        jnp.sum(jnp.where(live[:, q : q + 1] > 0.5, values, 0.0), axis=0, keepdims=True)
        for q in range(SAMPLES)
    ]


def finish_in_kernel(
    features, piece0, piece1, piece2, piece3,
    rows, grad, average, inv_scale, member, table, index, back, totals,
):
    live = member[...]
    balanced = rows.shape[0]
    total = piece0[...].astype(jnp.float32)
    for piece in (piece1, piece2, piece3):
        total = total + piece[...].astype(jnp.float32)
    mod_in_grad = total[0:balanced].T
    sums = total[balanced : balanced + 8] + total[balanced + 8 : balanced + 16]
    means = jnp.concatenate([sums, jnp.zeros((120, balanced), jnp.float32)], axis=0).T / features
    inv = inv_scale[...]
    normed = (rows[...].astype(jnp.float32) - average[...]) * inv
    normed_grad = mod_in_grad * (1.0 + sample_mix(live, table[4:8]))
    row_grad = grad[...].astype(jnp.float32) + inv * (
        normed_grad - means[:, 0:1] - normed * means[:, 1:2]
    )
    back[...] = picked(index[...], row_grad.astype(jnp.bfloat16))
    totals[...] = jnp.concatenate(
        image_sums(live, mod_in_grad) + image_sums(live, mod_in_grad * normed), axis=0
    )


def finish_out_kernel(piece0, piece1, piece2, piece3, rows, member, table, out):
    live = member[...]
    branch = piece0[...].astype(jnp.float32)
    for piece in (piece1, piece2, piece3):
        branch = branch + piece[...].astype(jnp.float32)
    branch = branch.T
    gate = sample_mix(live, table[8:12])
    out[...] = (rows[...].astype(jnp.float32) + gate * branch).astype(jnp.bfloat16)


def pick_kernel(index, values, out):
    out[...] = picked(index[...], values[...])


SMEM_SPEC = pl.BlockSpec(memory_space=pltpu.SMEM)
VMEM_SPEC = pl.BlockSpec(memory_space=pltpu.VMEM)


def call(kernel, outs, scratch, flops, moved, *args):
    return pl.pallas_call(
        kernel,
        out_shape=outs,
        in_specs=[SMEM_SPEC if a.ndim == 1 else VMEM_SPEC for a in args],
        out_specs=jax.tree.map(lambda _: VMEM_SPEC, outs),
        scratch_shapes=scratch,
        compiler_params=pltpu.CompilerParams(vmem_limit_bytes=VMEM),
        cost_estimate=pl.CostEstimate(flops=flops, bytes_accessed=moved, transcendentals=0),
    )(*args)


def body(hidden_in, live_rows, sample_tokens, w_up, w_down, modulation, out_grad):
    groups = lax.axis_size(DP)
    position = lax.axis_index(DP)
    slots_in = hidden_in.shape[0]
    per_pair = slots_in // groups
    balanced = out_grad.shape[0]
    width_local = hidden_in.shape[1]
    tensor_count = lax.axis_size(TP)
    model_width = width_local * tensor_count
    hid = w_up.shape[1]
    f32, bf16 = jnp.float32, jnp.bfloat16
    shape = jax.ShapeDtypeStruct
    low = groups - 1
    bits = groups.bit_length() - 1

    weights = jnp.stack([w_up, w_down.T])
    before = shifted(weights, "zh", 1)
    after = shifted(weights, "zh", -1)

    table = modulation.reshape(-1, width_local)
    pad = jnp.zeros((16 - table.shape[0], width_local), f32)
    payload = jnp.concatenate([out_grad] + three_terms(jnp.concatenate([table, pad])), axis=0)

    row_ends = jnp.cumsum(live_rows)
    row_starts = row_ends - live_rows
    device_ids = jnp.arange(groups, dtype=jnp.int32)
    own_start = jnp.sum(jnp.where(device_ids < position, live_rows, 0))
    own_live = jnp.sum(jnp.where(device_ids == position, live_rows, 0))
    slot_ids = jnp.arange(per_pair, dtype=jnp.int32)[None, :]
    local_rows = ((device_ids[:, None] - own_start) & low) + groups * slot_ids
    outgoing = hidden_in[local_rows.reshape(-1)].reshape(groups, per_pair, width_local)
    gathered = lax.all_gather(payload, TP, axis=0)
    far = jnp.concatenate([shifted(before[:1], "zh", 1), shifted(after[1:], "zh", -1)], axis=0)
    first = direct_pieces(jnp.stack([weights, before, after]), "y")
    incoming = lax.all_to_all(outgoing, DP, split_axis=0, concat_axis=0, tiled=True)
    global_rows = position + groups * jnp.arange(balanced, dtype=jnp.int32)
    before_row = row_ends[None, :] <= global_rows[:, None]
    owners = jnp.sum(before_row.astype(jnp.int32), axis=1)
    owner_start = jnp.sum(jnp.where(before_row, live_rows[None, :], 0), axis=1)
    owner_slot = (global_rows - owner_start) >> bits
    incoming, far, first = lax.optimization_barrier((incoming, far, first))
    rows_bal = incoming.reshape(groups * per_pair, width_local)[owners * per_pair + owner_slot]
    sample_ends = jnp.cumsum(sample_tokens)
    sample_starts = sample_ends - sample_tokens
    member = (
        (global_rows[:, None] >= sample_starts[None, :])
        & (global_rows[:, None] < sample_ends[None, :])
    ).astype(f32)

    rows_zl = spread(rows_bal, "zl")
    rows_zl, gathered = lax.optimization_barrier((rows_zl, gathered))
    last = direct_pieces(far[None], "y")
    first_other = shifted(first, "c", 1)
    rows_all = spread(rows_zl, "x")

    by_place = gathered.reshape(4, 4, -1, width_local)
    grad_zl = lax.dynamic_index_in_dim(by_place, lax.axis_index("x"), 1, keepdims=False)[:, :balanced]
    place = jnp.stack([lax.axis_index(a) for a in ("y", "zh", "c", "zl")]).astype(jnp.int32)
    block_shape = shape((4, 4, balanced, width_local), bf16)
    column = shape((balanced, 1), f32)
    scaled_grad, table_all = call(
        gate_kernel,
        (block_shape, shape((tensor_count, 16, width_local), f32)),
        [],
        4 * US,
        0,
        place, gathered, member,
    )
    rows_all, first_other, last, scaled_grad = lax.optimization_barrier(
        (rows_all, first_other, last, scaled_grad)
    )
    last_other = shifted(last, "c", 1)
    weight_parts = (first, first_other, last, last_other)
    modulated, average, inv_scale = call(
        rows_kernel,
        (shape((4, 4, balanced + 16, width_local), bf16), column, column),
        [],
        6 * US,
        0,
        place, rows_all, table_all, member,
    )
    unit_rows = shape((hid, balanced), bf16)
    whole = lambda *dims: pl.BlockSpec(dims, lambda *_: (0,) * len(dims))
    by_dy = lambda *dims: pl.BlockSpec((1,) + dims, lambda dy, *_: (dy,) + (0,) * len(dims))
    params = pltpu.CompilerParams(vmem_limit_bytes=VMEM)
    planes = weights.shape[1:]
    hidden, pre_grad, sums = pl.pallas_call(
        hidden_kernel,
        grid=(4,),
        out_shape=(unit_rows, unit_rows, shape((16, balanced), bf16)),
        in_specs=[
            by_dy(4, balanced + 16, width_local),
            by_dy(4, balanced, width_local),
            whole(balanced, SAMPLES),
            by_dy(3, 2, *planes), by_dy(3, 2, *planes),
            by_dy(1, 2, *planes), by_dy(1, 2, *planes),
        ],
        out_specs=(whole(hid, balanced), whole(hid, balanced), whole(16, balanced)),
        scratch_shapes=[
            pltpu.VMEM((balanced + 16, hid), f32), pltpu.VMEM((balanced, hid), f32)
        ],
        compiler_params=params,
        cost_estimate=pl.CostEstimate(flops=8 * US, bytes_accessed=0, transcendentals=0),
    )(modulated, scaled_grad, member, *weight_parts)

    def outward(which, units, *extra):
        pick = lambda n: pl.BlockSpec(
            (1, n, 1) + planes, lambda dy, _: (dy, 0, which, 0, 0)
        )
        height = width_local + sum(e.shape[0] for e in extra)
        return pl.pallas_call(
            outward_kernel,
            grid_spec=pltpu.PrefetchScalarGridSpec(
                num_scalar_prefetch=1,
                grid=(4,),
                in_specs=[whole(hid, balanced), pick(3), pick(3), pick(1), pick(1)]
                + [whole(*e.shape) for e in extra],
                out_specs=pl.BlockSpec(
                    (1, 4, height, balanced),
                    lambda dy, at: (lax.rem(at[0] - dy + 4, 4), 0, 0, 0),
                ),
            ),
            out_shape=shape((4, 4, height, balanced), bf16),
            compiler_params=params,
            cost_estimate=pl.CostEstimate(flops=5 * US, bytes_accessed=0, transcendentals=0),
        )(place, units, *weight_parts, *extra)

    partial_in = outward(0, pre_grad, sums)
    partial_out = outward(1, hidden)

    from_x = lax.all_to_all(partial_in, "x", split_axis=0, concat_axis=0, tiled=True)
    from_x, partial_out = lax.optimization_barrier((from_x, partial_out))
    out_x = lax.all_to_all(partial_out, "x", split_axis=0, concat_axis=0, tiled=True)
    (in_x,) = call(fold_kernel, (shape(partial_in.shape[1:], bf16),), [], 2 * US, 0, place, from_x)
    in_zl = [in_x[0]] + [shifted(in_x[k], "zl", k) for k in (1, 2, 3)]
    out_x, in_zl = lax.optimization_barrier((out_x, in_zl))
    out_x, totals_zl = call(
        fold_kernel,
        (shape(partial_out.shape[1:], bf16), shape((4, SAMPLES, width_local), f32)),
        [], 3 * US, 0,
        place, out_x, grad_zl, member,
    )
    totals_out = totals_zl[0]
    for k in (1, 2, 3):
        totals_out = totals_out + shifted(totals_zl[k], "zl", k)

    source_rows = ((position - row_starts[:, None]) & low) + groups * slot_ids
    back_index = jnp.where(
        source_rows < live_rows[:, None],
        (row_starts[:, None] + source_rows - position) >> bits,
        -1,
    ).reshape(-1, 1)
    returning, totals_in = call(
        functools.partial(finish_in_kernel, model_width),
        (shape((slots_in, width_local), bf16), shape((2 * SAMPLES, width_local), f32)),
        [], 4 * US, 0,
        *in_zl, rows_bal, out_grad, average, inv_scale, member, table, back_index,
    )
    returning = returning.reshape(groups, per_pair, width_local)
    arrived = lax.all_to_all(returning, DP, split_axis=0, concat_axis=0, tiled=True)

    mod_grad = summed(jnp.concatenate([totals_in, totals_out], axis=0), "c")
    mod_grad, out_x = lax.optimization_barrier((mod_grad, out_x))
    mod_grad = summed(summed(mod_grad, "y"), "zh").reshape(modulation.shape)
    out_zl = [out_x[0]] + [shifted(out_x[k], "zl", k) for k in (1, 2, 3)]
    (block_out,) = call(
        finish_out_kernel, (shape((balanced, width_local), bf16),), [], 2 * US, 0,
        *out_zl, rows_bal, member, table,
    )

    own_rows = jnp.arange(slots_in, dtype=jnp.int32)
    target = ((own_start + own_rows) & low) * per_pair + (own_rows >> bits)
    target = jnp.where(own_rows < own_live, target, -1).reshape(-1, 1)
    (input_grad,) = call(
        pick_kernel, (shape((slots_in, width_local), bf16),), [], 2 * US, 0,
        target, arrived.reshape(slots_in, width_local),
    )
    return (block_out, input_grad, mod_grad)


def solution(mesh):
    cut = Mesh(mesh.devices.reshape(SIZES), AXES)
    return jax.shard_map(
        body,
        mesh=cut,
        in_specs=(
            P(DP, TP),
            P(),
            P(),
            P(DP, TP),
            P(TP, DP),
            P(None, None, TP),
            P(DP, TP),
        ),
        out_specs=(P(DP, TP), P(DP, TP), P(None, None, TP)),
        check_vma=False,
    )
```

time: 482 us -> 372 us (0.77)
  the two profiles are of different devices: /device:TPU:2 before, /device:TPU:40 now
where the time goes in v2:
time: 372 us; the launch traced here: 370 us
  starting transfers between devices  140 us (38%)
  waiting for transfers between devices  132 us (35%)
  Pallas kernels  35 us (9%)
  local copies, waits for them, and re-layouts  18.3 us (5%)
  blocking collectives  16.4 us (4%)
  between operations  14.8 us (4%)
  other arithmetic  12.9 us (3%)
    ppermute x21, waiting for transfers between devices, shifted(): lax.ppermute(value, axis, [(i, (i + step) % size) for i in range(size)])  89.8 us
    ppermute x21, starting transfers between devices, shifted(): lax.ppermute(value, axis, [(i, (i + step) % size) for i in range(size)])  80.4 us
    ppermute x5, starting transfers between devices, crossed(): return lax.ppermute(value, axis, [(i, i ^ mask) for i in range(size)])  23.8 us
    all_to_all x1, waiting for transfers between devices, body(): lax.all_to_all(partial_in, 'x', split_axis=0, concat_axis=0, tiled=True)  19.3 us
    all_to_all x1, blocking collectives, spread(): return lax.all_to_all(copies, axis, split_axis=0, concat_axis=0, tiled=True)  16.4 us
    pallas_call x7, Pallas kernels, call(): pl.pallas_call(kernel, out_shape=outs, in_specs=[SMEM_SPEC if a.ndim == 1...  16.2 us
    all_to_all x1, starting transfers between devices, body(): lax.all_to_all(outgoing, DP, split_axis=0, concat_axis=0, tiled=True)  14.9 us
    ppermute x5, waiting for transfers between devices, crossed(): return lax.ppermute(value, axis, [(i, i ^ mask) for i in range(size)])  14.7 us
  transfers between devices with their start and end apart: 32, of which 15 were waited for; matrix products, arithmetic and copies ran while one was open for 5% of the time, Pallas kernels for 5%

profile of v2, /device:TPU:40, one launch (start us, length us, event | category | flops | bytes accessed | tf_op | source)
XLA Modules:
  0.0 370.4 jit_solution(6401072231814335169)
XLA Ops:
  9.4 11.8 %collective-permute-start.2 = (bf16[2,128,768]{2,1,0:T(8,128)(2,1)S(1)}, bf16[2,128,768]{2,1,0:T(8,128)(2,1)S(1)}, u32[]{:S(2)}, u32[]{:S(2)}) collective-permute-start(bf16[2,128,768]{2,1,0:T(8,128)(2,1)S(1)} %get-tuple-element.80), channel_id=1, source_target_pairs={{0,384},{128,0},{256,128},{384,256},{1,385},{129,1},{257,129},{385... | collective-permute-start | bytes 1179656 | tf_op jit(solution)/shard_map/ppermute | solution.py:37
  21.2 1.9 collective-permute-start
  25.7 31.3 %collective-permute-done.2 = bf16[2,128,768]{2,1,0:T(8,128)(2,1)S(1)} collective-permute-done((bf16[2,128,768]{2,1,0:T(8,128)(2,1)S(1)}, bf16[2,128,768]{2,1,0:T(8,128)(2,1)S(1)}, u32[]{:S(2)}, u32[]{:S(2)}) %collective-permute-start.2) | collective-permute-done | bytes 393248 | tf_op jit(solution)/shard_map/ppermute | solution.py:37
  58.2 4.4 %collective-permute-start.5 = (bf16[3,2,128,768]{3,2,1,0:T(8,128)(2,1)}, bf16[3,2,128,768]{3,2,1,0:T(8,128)(2,1)}, u32[]{:S(2)}, u32[]{:S(2)}) collective-permute-start(bf16[3,2,128,768]{3,2,1,0:T(8,128)(2,1)} %get-tuple-element.70), channel_id=1, source_target_pairs={{0,64},{32,96},{64,0},{96,32},{1,65},{33,97},{65,1},{97,33},{2,66}... | collective-permute-start | bytes 3538952 | tf_op jit(solution)/shard_map/ppermute | solution.py:37
  62.6 1.9 collective-permute-start.4
  64.5 3.9 %collective-permute-start.6 = (bf16[3,2,128,768]{3,2,1,0:T(8,128)(2,1)}, bf16[3,2,128,768]{3,2,1,0:T(8,128)(2,1)}, u32[]{:S(2)}, u32[]{:S(2)}) collective-permute-start(bf16[3,2,128,768]{3,2,1,0:T(8,128)(2,1)} %get-tuple-element.70), channel_id=1, source_target_pairs={{0,96},{32,0},{64,32},{96,64},{1,97},{33,1},{65,33},{97,65},{2,98}... | collective-permute-start | bytes 3538952 | tf_op jit(solution)/shard_map/ppermute | solution.py:37
  68.5 3.3 gather_fusion
  71.8 14.9 %all-to-all-start = ((bf16[32,24,256]{2,1,0:T(8,128)(2,1)}), bf16[32,24,256]{2,1,0:T(8,128)(2,1)S(1)}, u32[]{:S(2)}, u32[]{:S(2)}) async-start(bf16[32,24,256]{2,1,0:T(8,128)(2,1)} %bitcast.4), calls=%async_computation | async-start | bytes 786432 | tf_op jit(solution)/shard_map/all_to_all | solution.py:351
  86.7 7.3 %collective-permute-start.3 = (bf16[1,128,768]{2,1,0:T(8,128)(2,1)S(1)}, bf16[1,128,768]{2,1,0:T(8,128)(2,1)S(1)}, u32[]{:S(2)}, u32[]{:S(2)}) collective-permute-start(bf16[1,128,768]{2,1,0:T(8,128)(2,1)S(1)} %slice.65), channel_id=1, source_target_pairs={{0,384},{128,0},{256,128},{384,256},{1,385},{129,1},{257,129},{385... | collective-permute-start | bytes 589832 | tf_op jit(solution)/shard_map/ppermute | solution.py:37
  94.0 2.4 collective-permute-start.1
  96.5 38.1 %collective-permute-done.3 = bf16[1,128,768]{2,1,0:T(8,128)(2,1)S(1)} collective-permute-done((bf16[1,128,768]{2,1,0:T(8,128)(2,1)S(1)}, bf16[1,128,768]{2,1,0:T(8,128)(2,1)S(1)}, u32[]{:S(2)}, u32[]{:S(2)}) %collective-permute-start.3) | collective-permute-done | bytes 196640 | tf_op jit(solution)/shard_map/ppermute | solution.py:37
  134.6 3.9 %pad_maximum_fusion.first = bf16[4,3,2,128,768]{4,3,2,1,0:T(8,128)(2,1)} fusion(bf16[1,3,2,128,768]{4,3,2,1,0:T(8,128)(2,1)} %bitcast.14, bf16[1,3,2,128,768]{4,3,2,1,0:T(8,128)(2,1)} %bitcast.13, bf16[1,3,2,128,768]{4,3,2,1,0:T(8,128)(2,1)} %bitcast.12, bf16[1,3,2,128,768]{4,3,2,1,0:T(8,128)(2,1)S(1)} %get-tuple-element.69), kind=kLoop, calls=%fused_computation.2 | loop fusion | flops 7077888 | bytes 9437184 | tf_op jit(solution)/shard_map/stack | solution.py:46
  141.7 16.4 %all_to_all.30 = bf16[4,256,256]{2,1,0:T(8,128)(2,1)S(1)} all-to-all(bf16[4,256,256]{2,1,0:T(8,128)(2,1)S(1)} %broadcast_in_dim.30), channel_id=1, replica_groups=mesh['zh'=4,'y'=4,'c'=2,'zl'=4,'x'=4] {'zl'}, dimensions={0} | all-to-all | bytes 1048576 | tf_op jit(solution)/shard_map/all_to_all | solution.py:51
  159.7 3.7 %all-to-all-start.2 = ((bf16[4,4,256,256]{3,2,1,0:T(8,128)(2,1)}), bf16[4,4,256,256]{3,2,1,0:T(8,128)(2,1)S(1)}, u32[]{:S(2)}, u32[]{:S(2)}) async-start(bf16[4,4,256,256]{3,2,1,0:T(8,128)(2,1)} %broadcast_in_dim.31), calls=%async_computation.2 | async-start | bytes 4194304 | tf_op jit(solution)/shard_map/all_to_all | solution.py:51
  163.6 2.4 collective-permute-start.10
  166.1 4.5 %collective-permute-start.9 = (bf16[1,2,128,768]{3,2,1,0:T(8,128)(2,1)S(1)}, bf16[1,2,128,768]{3,2,1,0:T(8,128)(2,1)}, u32[]{:S(2)}, u32[]{:S(2)}) collective-permute-start(bf16[1,2,128,768]{3,2,1,0:T(8,128)(2,1)S(1)} %bitcast.72), channel_id=1, source_target_pairs={{0,64},{32,96},{64,0},{96,32},{1,65},{33,97},{65,1},{97,33},{2,66}... | collective-permute-start | bytes 1179656 | tf_op jit(solution)/shard_map/ppermute | solution.py:37
  170.6 3.5 collective-permute-start.8
  174.2 2.3 collective-permute-done.10
  176.6 8.6 %collective-permute-done.9 = bf16[1,2,128,768]{3,2,1,0:T(8,128)(2,1)} collective-permute-done((bf16[1,2,128,768]{3,2,1,0:T(8,128)(2,1)S(1)}, bf16[1,2,128,768]{3,2,1,0:T(8,128)(2,1)}, u32[]{:S(2)}, u32[]{:S(2)}) %collective-permute-start.9) | collective-permute-done | bytes 393248 | tf_op jit(solution)/shard_map/ppermute | solution.py:37
  185.2 2.7 collective-permute-done.8
  187.9 2.8 pad_maximum_fusion.1.last
  190.6 3.6 shard_map.94
  197.5 5.0 %shard_map.95 = (bf16[4,4,272,256]{3,2,1,0:T(8,128)(2,1)S(1)}, f32[256,1]{1,0:T(8,128)S(1)}, f32[256,1]{1,0:T(8,128)S(1)}) custom-call(s32[4]{0:T(128)S(1)} %pad_add_fusion.place, bf16[4,4,256,256]{3,2,1,0:T(8,128)(2,1)S(1)} %all-to-all-done.2.rows, f32[16,16,256]{2,1,0:T(8,128)S(1)} %get-tuple-element.40.table_in, f32[256,4]{1,0:T(8,128)S(1)} %and_convert_fusion.member.refs_1_), custom_call_target="tpu_custom_call" | custom-call | flops 6000000000 | tf_op jit(solution)/shard_map/pallas_call | solution.py:306
  204.6 9.0 %shard_map.96 = (bf16[768,256]{1,0:T(8,128)(2,1)S(1)}, bf16[768,256]{1,0:T(8,128)(2,1)S(1)}, bf16[16,256]{1,0:T(8,128)(2,1)S(1)}) custom-call(bf16[4,4,272,256]{3,2,1,0:T(8,128)(2,1)} %copy-done.11, bf16[4,4,256,256]{3,2,1,0:T(8,128)(2,1)S(1)} %copy-done.10, f32[256,4]{1,0:T(8,128)S(1)} %and_convert_fusion.member.refs_1_, ...), custom_call_target="tpu_custom_call" | custom-call | flops 8000000000 | tf_op jit(solution)/shard_map/pallas_call | solution.py:403
  213.6 5.0 %shard_map.97 = bf16[4,4,272,256]{3,2,1,0:T(8,128)(2,1)S(1)} custom-call(s32[4]{0:T(128)S(1)} %pad_add_fusion.place, bf16[768,256]{1,0:T(8,128)(2,1)S(1)} %get-tuple-element.45.hidden, bf16[4,3,2,128,768]{4,3,2,1,0:T(8,128)(2,1)} %pad_maximum_fusion.first, bf16[4,3,2,128,768]{4,3,2,1,0:T(8,128)(2,1)} %collective-permute-done.7.first_other, ...), custom_call_target="tpu_custom_call" | custom-call | flops 5000000000 | tf_op jit(solution)/shard_map/pallas_call | solution.py:427
  220.0 4.5 %all-to-all-start.3 = ((bf16[4,4,272,256]{3,2,1,0:T(8,128)(2,1)}), bf16[4,4,272,256]{3,2,1,0:T(8,128)(2,1)S(1)}, u32[]{:S(2)}, u32[]{:S(2)}) async-start(bf16[4,4,272,256]{3,2,1,0:T(8,128)(2,1)} %copy-done.1), calls=%async_computation.3 | async-start | bytes 4456448 | tf_op jit(solution)/shard_map/all_to_all | solution.py:447
  227.3 4.9 %shard_map.98 = bf16[4,4,256,256]{3,2,1,0:T(8,128)(2,1)S(1)} custom-call(s32[4]{0:T(128)S(1)} %pad_add_fusion.place, bf16[768,256]{1,0:T(8,128)(2,1)S(1)} %get-tuple-element.47.hidden, bf16[4,3,2,128,768]{4,3,2,1,0:T(8,128)(2,1)} %pad_maximum_fusion.first, bf16[4,3,2,128,768]{4,3,2,1,0:T(8,128)(2,1)} %collective-permute-done.7.first_other, ...), custom_call_target="tpu_custom_call" | custom-call | flops 5000000000 | tf_op jit(solution)/shard_map/pallas_call | solution.py:427
  233.5 19.3 %all-to-all-done.3.blocks = bf16[4,4,272,256]{3,2,1,0:T(8,128)(2,1)S(1)} async-done(((bf16[4,4,272,256]{3,2,1,0:T(8,128)(2,1)}), bf16[4,4,272,256]{3,2,1,0:T(8,128)(2,1)S(1)}, u32[]{:S(2)}, u32[]{:S(2)}) %all-to-all-start.3) | async-done | bytes 2228256 | tf_op jit(solution)/shard_map/all_to_all | solution.py:447
  252.8 4.5 %all-to-all-start.4 = ((bf16[4,4,256,256]{3,2,1,0:T(8,128)(2,1)}), bf16[4,4,256,256]{3,2,1,0:T(8,128)(2,1)}, u32[]{:S(2)}, u32[]{:S(2)}) async-start(bf16[4,4,256,256]{3,2,1,0:T(8,128)(2,1)} %copy-done.2), calls=%async_computation.4 | async-start | bytes 4194304 | tf_op jit(solution)/shard_map/all_to_all | solution.py:449
  258.2 4.2 %collective-permute-start.14 = (bf16[272,256]{1,0:T(8,128)(2,1)S(1)}, bf16[272,256]{1,0:T(8,128)(2,1)S(1)}, u32[]{:S(2)}, u32[]{:S(2)}) collective-permute-start(bf16[272,256]{1,0:T(8,128)(2,1)S(1)} %get-tuple-element.71), channel_id=1, source_target_pairs={{0,12},{4,0},{8,4},{12,8},{1,13},{5,1},{9,5},{13,9},{2,14},{6,2},{... | collective-permute-start | bytes 417800 | tf_op jit(solution)/shard_map/ppermute | solution.py:37
  262.4 2.0 collective-permute-start.13
  264.4 4.8 %collective-permute-start.12 = (bf16[272,256]{1,0:T(8,128)(2,1)S(1)}, bf16[272,256]{1,0:T(8,128)(2,1)S(1)}, u32[]{:S(2)}, u32[]{:S(2)}) collective-permute-start(bf16[272,256]{1,0:T(8,128)(2,1)S(1)} %get-tuple-element.73), channel_id=1, source_target_pairs={{0,4},{4,8},{8,12},{12,0},{1,5},{5,9},{9,13},{13,1},{2,6},{6,10},{... | collective-permute-start | bytes 417800 | tf_op jit(solution)/shard_map/ppermute | solution.py:37
  272.0 2.9 collective-permute-done.12.piece1
  274.9 8.7 %all-to-all-done.4.blocks = bf16[4,4,256,256]{3,2,1,0:T(8,128)(2,1)} async-done(((bf16[4,4,256,256]{3,2,1,0:T(8,128)(2,1)}), bf16[4,4,256,256]{3,2,1,0:T(8,128)(2,1)}, u32[]{:S(2)}, u32[]{:S(2)}) %all-to-all-start.4) | async-done | bytes 2097184 | tf_op jit(solution)/shard_map/all_to_all | solution.py:449
  285.1 8.7 %all-to-all-start.5 = ((bf16[32,24,256]{2,1,0:T(8,128)(2,1)}), bf16[32,24,256]{2,1,0:T(8,128)(2,1)S(1)}, u32[]{:S(2)}, u32[]{:S(2)}) async-start(bf16[32,24,256]{2,1,0:T(8,128)(2,1)} %bitcast.42), calls=%async_computation.5 | async-start | bytes 786432 | tf_op jit(solution)/shard_map/all_to_all | solution.py:476
  293.8 2.8 shard_map.101
  296.7 2.6 collective-permute-start.15
  299.3 3.4 collective-permute-start.17
  302.7 4.3 %collective-permute-start.16 = (f32[4,256]{1,0:T(4,128)S(1)}, f32[4,256]{1,0:T(4,128)S(1)}, u32[]{:S(2)}, u32[]{:S(2)}) collective-permute-start(f32[4,256]{1,0:T(4,128)S(1)} %get-tuple-element.83), channel_id=1, source_target_pairs={{0,8},{4,12},{8,0},{12,4},{1,9},{5,13},{9,1},{13,5},{2,10},{6,14},... | collective-permute-start | bytes 12296 | tf_op jit(solution)/shard_map/ppermute | solution.py:37
  314.5 3.7 %collective-permute-done.22 = f32[12,256]{1,0:T(8,128)S(1)} collective-permute-done((f32[12,256]{1,0:T(8,128)S(1)}, f32[12,256]{1,0:T(8,128)S(1)}, u32[]{:S(2)}, u32[]{:S(2)}) %collective-permute-start.22) | collective-permute-done | bytes 12320 | tf_op jit(solution)/shard_map/ppermute | solution.py:42
  318.2 3.7 %collective-permute-start.23 = (f32[12,256]{1,0:T(8,128)S(1)}, f32[12,256]{1,0:T(8,128)S(1)}, u32[]{:S(2)}, u32[]{:S(2)}) collective-permute-start(f32[12,256]{1,0:T(8,128)S(1)} %add.203), channel_id=1, source_target_pairs={{0,64},{32,96},{64,0},{96,32},{1,65},{33,97},{65,1},{97,33},{2,66}... | collective-permute-start | bytes 36872 | tf_op jit(solution)/shard_map/ppermute | solution.py:42
  322.0 3.4 collective-permute-done.23
  325.4 9.5 %collective-permute-start.24 = (f32[12,256]{1,0:T(8,128)S(1)}, f32[12,256]{1,0:T(8,128)S(1)}, u32[]{:S(2)}, u32[]{:S(2)}) collective-permute-start(f32[12,256]{1,0:T(8,128)S(1)} %add.204), channel_id=1, source_target_pairs={{0,128},{128,0},{256,384},{384,256},{1,129},{129,1},{257,385},{385... | collective-permute-start | bytes 36872 | tf_op jit(solution)/shard_map/ppermute | solution.py:42
  334.9 5.0 %collective-permute-start.21 = (bf16[256,256]{1,0:T(8,128)(2,1)S(1)}, bf16[256,256]{1,0:T(8,128)(2,1)S(1)}, u32[]{:S(2)}, u32[]{:S(2)}) collective-permute-start(bf16[256,256]{1,0:T(8,128)(2,1)S(1)} %get-tuple-element.75), channel_id=1, source_target_pairs={{0,12},{4,0},{8,4},{12,8},{1,13},{5,1},{9,5},{13,9},{2,14},{6,2},{... | collective-permute-start | bytes 393224 | tf_op jit(solution)/shard_map/ppermute | solution.py:37
  339.9 1.9 collective-permute-start.20
  341.8 4.3 %collective-permute-start.19 = (bf16[256,256]{1,0:T(8,128)(2,1)S(1)}, bf16[256,256]{1,0:T(8,128)(2,1)S(1)}, u32[]{:S(2)}, u32[]{:S(2)}) collective-permute-start(bf16[256,256]{1,0:T(8,128)(2,1)S(1)} %get-tuple-element.77), channel_id=1, source_target_pairs={{0,4},{4,8},{8,12},{12,0},{1,5},{5,9},{9,13},{13,1},{2,6},{6,10},{... | collective-permute-start | bytes 393224 | tf_op jit(solution)/shard_map/ppermute | solution.py:37
  346.1 6.7 %collective-permute-start.25 = (f32[12,256]{1,0:T(8,128)S(1)}, f32[12,256]{1,0:T(8,128)S(1)}, u32[]{:S(2)}, u32[]{:S(2)}) collective-permute-start(f32[12,256]{1,0:T(8,128)S(1)} %add.205), channel_id=1, source_target_pairs={{0,256},{128,384},{256,0},{384,128},{1,257},{129,385},{257,1},{385... | collective-permute-start | bytes 36872 | tf_op jit(solution)/shard_map/ppermute | solution.py:42
  354.2 6.4 %collective-permute-done.25 = f32[12,256]{1,0:T(8,128)S(1)} collective-permute-done((f32[12,256]{1,0:T(8,128)S(1)}, f32[12,256]{1,0:T(8,128)S(1)}, u32[]{:S(2)}, u32[]{:S(2)}) %collective-permute-start.25) | collective-permute-done | bytes 12320 | tf_op jit(solution)/shard_map/ppermute | solution.py:42
  (115 shorter events, 38.8 us)
Async XLA Ops:
  7.2 61.3 %copy-start = (bf16[768,256]{1,0:T(8,128)(2,1)S(1)}, bf16[768,256]{1,0:T(8,128)(2,1)}, u32[]{:S(2)}) copy-start(bf16[768,256]{1,0:T(8,128)(2,1)} %param.7) | copy-start | bytes 1179652
  7.2 16.0 %copy-start.16 = (f32[3,4,256]{2,1,0:T(4,128)S(1)}, f32[3,4,256]{2,1,0:T(4,128)}, u32[]{:S(2)}) copy-start(f32[3,4,256]{2,1,0:T(4,128)} %param.12) | copy-start | bytes 36868
  7.2 16.0 %copy-start.6 = (bf16[256,256]{1,0:T(8,128)(2,1)S(1)}, bf16[256,256]{1,0:T(8,128)(2,1)}, u32[]{:S(2)}) copy-start(bf16[256,256]{1,0:T(8,128)(2,1)} %grad.1) | copy-start | bytes 393220
  7.2 16.7 %copy-start.17 = (s32[32]{0:T(128)S(1)}, s32[32]{0:T(128)}, u32[]{:S(2)}) copy-start(s32[32]{0:T(128)} %param.8) | copy-start | bytes 388
  7.2 151.0 %all-gather.3.cloned.1.call-start = ((), (), s32[]{:S(2)}) async-start(), calls=%async_computation.6 | async-start | bytes 2646016 | tf_op jit(solution)/shard_map/all_gather | solution.py:348
  9.4 47.6 %collective-permute-start.2 = (bf16[2,128,768]{2,1,0:T(8,128)(2,1)S(1)}, bf16[2,128,768]{2,1,0:T(8,128)(2,1)S(1)}, u32[]{:S(2)}, u32[]{:S(2)}) collective-permute-start(bf16[2,128,768]{2,1,0:T(8,128)(2,1)S(1)} %get-tuple-element.80), channel_id=1, source_target_pairs={{0,384},{128,0},{256,128},{384,256},{1,385},{129,1},{257,129},{385... | collective-permute-start | bytes 1179656 | tf_op jit(solution)/shard_map/ppermute | solution.py:37
  21.2 35.8 %collective-permute-start = (bf16[2,128,768]{2,1,0:T(8,128)(2,1)S(1)}, bf16[2,128,768]{2,1,0:T(8,128)(2,1)S(1)}, u32[]{:S(2)}, u32[]{:S(2)}) collective-permute-start(bf16[2,128,768]{2,1,0:T(8,128)(2,1)S(1)} %get-tuple-element.80), channel_id=1, source_target_pairs={{0,128},{128,256},{256,384},{384,0},{1,129},{129,257},{257,385},{3... | collective-permute-start | bytes 1179656 | tf_op jit(solution)/shard_map/ppermute | solution.py:37
  58.2 76.4 %collective-permute-start.5 = (bf16[3,2,128,768]{3,2,1,0:T(8,128)(2,1)}, bf16[3,2,128,768]{3,2,1,0:T(8,128)(2,1)}, u32[]{:S(2)}, u32[]{:S(2)}) collective-permute-start(bf16[3,2,128,768]{3,2,1,0:T(8,128)(2,1)} %get-tuple-element.70), channel_id=1, source_target_pairs={{0,64},{32,96},{64,0},{96,32},{1,65},{33,97},{65,1},{97,33},{2,66}... | collective-permute-start | bytes 3538952 | tf_op jit(solution)/shard_map/ppermute | solution.py:37
  62.6 72.0 %collective-permute-start.4 = (bf16[3,2,128,768]{3,2,1,0:T(8,128)(2,1)}, bf16[3,2,128,768]{3,2,1,0:T(8,128)(2,1)}, u32[]{:S(2)}, u32[]{:S(2)}) collective-permute-start(bf16[3,2,128,768]{3,2,1,0:T(8,128)(2,1)} %get-tuple-element.70), channel_id=1, source_target_pairs={{0,32},{32,64},{64,96},{96,0},{1,33},{33,65},{65,97},{97,1},{2,34}... | collective-permute-start | bytes 3538952 | tf_op jit(solution)/shard_map/ppermute | solution.py:37
  64.5 70.1 %collective-permute-start.6 = (bf16[3,2,128,768]{3,2,1,0:T(8,128)(2,1)}, bf16[3,2,128,768]{3,2,1,0:T(8,128)(2,1)}, u32[]{:S(2)}, u32[]{:S(2)}) collective-permute-start(bf16[3,2,128,768]{3,2,1,0:T(8,128)(2,1)} %get-tuple-element.70), channel_id=1, source_target_pairs={{0,96},{32,0},{64,32},{96,64},{1,97},{33,1},{65,33},{97,65},{2,98}... | collective-permute-start | bytes 3538952 | tf_op jit(solution)/shard_map/ppermute | solution.py:37
  71.8 66.7 %all-to-all-start = ((bf16[32,24,256]{2,1,0:T(8,128)(2,1)}), bf16[32,24,256]{2,1,0:T(8,128)(2,1)S(1)}, u32[]{:S(2)}, u32[]{:S(2)}) async-start(bf16[32,24,256]{2,1,0:T(8,128)(2,1)} %bitcast.4), calls=%async_computation | async-start | bytes 786432 | tf_op jit(solution)/shard_map/all_to_all | solution.py:351
  86.7 47.9 %collective-permute-start.3 = (bf16[1,128,768]{2,1,0:T(8,128)(2,1)S(1)}, bf16[1,128,768]{2,1,0:T(8,128)(2,1)S(1)}, u32[]{:S(2)}, u32[]{:S(2)}) collective-permute-start(bf16[1,128,768]{2,1,0:T(8,128)(2,1)S(1)} %slice.65), channel_id=1, source_target_pairs={{0,384},{128,0},{256,128},{384,256},{1,385},{129,1},{257,129},{385... | collective-permute-start | bytes 589832 | tf_op jit(solution)/shard_map/ppermute | solution.py:37
  94.0 40.5 %collective-permute-start.1 = (bf16[1,128,768]{2,1,0:T(8,128)(2,1)S(1)}, bf16[1,128,768]{2,1,0:T(8,128)(2,1)S(1)}, u32[]{:S(2)}, u32[]{:S(2)}) collective-permute-start(bf16[1,128,768]{2,1,0:T(8,128)(2,1)S(1)} %slice.64), channel_id=1, source_target_pairs={{0,128},{128,256},{256,384},{384,0},{1,129},{129,257},{257,385},{3... | collective-permute-start | bytes 589832 | tf_op jit(solution)/shard_map/ppermute | solution.py:37
  138.5 57.1 %collective-permute-start.7 = (bf16[4,3,2,128,768]{4,3,2,1,0:T(8,128)(2,1)}, bf16[4,3,2,128,768]{4,3,2,1,0:T(8,128)(2,1)}, u32[]{:S(2)}, u32[]{:S(2)}) collective-permute-start(bf16[4,3,2,128,768]{4,3,2,1,0:T(8,128)(2,1)} %pad_maximum_fusion.first), channel_id=1, source_target_pairs={{0,16},{16,0},{1,17},{17,1},{2,18},{18,2},{3,19},{19,3},{4,20},{20... | collective-permute-start | bytes 14155784 | tf_op jit(solution)/shard_map/ppermute | solution.py:37
  159.7 3.8 %copy-start.18 = (s32[4]{0:T(128)S(1)}, s32[4]{0:T(128)}, u32[]{:S(2)}) copy-start(s32[4]{0:T(128)} %param.9) | copy-start | bytes 52
  159.7 35.9 %all-to-all-start.2 = ((bf16[4,4,256,256]{3,2,1,0:T(8,128)(2,1)}), bf16[4,4,256,256]{3,2,1,0:T(8,128)(2,1)S(1)}, u32[]{:S(2)}, u32[]{:S(2)}) async-start(bf16[4,4,256,256]{3,2,1,0:T(8,128)(2,1)} %broadcast_in_dim.31), calls=%async_computation.2 | async-start | bytes 4194304 | tf_op jit(solution)/shard_map/all_to_all | solution.py:51
  163.6 12.9 %collective-permute-start.10 = (bf16[1,2,128,768]{3,2,1,0:T(8,128)(2,1)S(1)}, bf16[1,2,128,768]{3,2,1,0:T(8,128)(2,1)}, u32[]{:S(2)}, u32[]{:S(2)}) collective-permute-start(bf16[1,2,128,768]{3,2,1,0:T(8,128)(2,1)S(1)} %bitcast.71), channel_id=1, source_target_pairs={{0,96},{32,0},{64,32},{96,64},{1,97},{33,1},{65,33},{97,65},{2,98}... | collective-permute-start | bytes 1179656 | tf_op jit(solution)/shard_map/ppermute | solution.py:37
  166.1 19.1 %collective-permute-start.9 = (bf16[1,2,128,768]{3,2,1,0:T(8,128)(2,1)S(1)}, bf16[1,2,128,768]{3,2,1,0:T(8,128)(2,1)}, u32[]{:S(2)}, u32[]{:S(2)}) collective-permute-start(bf16[1,2,128,768]{3,2,1,0:T(8,128)(2,1)S(1)} %bitcast.72), channel_id=1, source_target_pairs={{0,64},{32,96},{64,0},{96,32},{1,65},{33,97},{65,1},{97,33},{2,66}... | collective-permute-start | bytes 1179656 | tf_op jit(solution)/shard_map/ppermute | solution.py:37
  170.6 17.3 %collective-permute-start.8 = (bf16[1,2,128,768]{3,2,1,0:T(8,128)(2,1)S(1)}, bf16[1,2,128,768]{3,2,1,0:T(8,128)(2,1)}, u32[]{:S(2)}, u32[]{:S(2)}) collective-permute-start(bf16[1,2,128,768]{3,2,1,0:T(8,128)(2,1)S(1)} %bitcast.73), channel_id=1, source_target_pairs={{0,32},{32,64},{64,96},{96,0},{1,33},{33,65},{65,97},{97,1},{2,34}... | collective-permute-start | bytes 1179656 | tf_op jit(solution)/shard_map/ppermute | solution.py:37
  187.9 2.8 copy-start.5
  195.6 9.0 %collective-permute-start.11 = (bf16[4,1,2,128,768]{4,3,2,1,0:T(8,128)(2,1)}, bf16[4,1,2,128,768]{4,3,2,1,0:T(8,128)(2,1)S(1)}, u32[]{:S(2)}, u32[]{:S(2)}) collective-permute-start(bf16[4,1,2,128,768]{4,3,2,1,0:T(8,128)(2,1)} %pad_maximum_fusion.1.last), channel_id=1, source_target_pairs={{0,16},{16,0},{1,17},{17,1},{2,18},{18,2},{3,19},{19,3},{4,20},{20... | collective-permute-start | bytes 4718600 | tf_op jit(solution)/shard_map/ppermute | solution.py:37
  197.5 7.1 %copy-start.3 = (bf16[4,1,2,128,768]{4,3,2,1,0:T(8,128)(2,1)S(1)}, bf16[4,1,2,128,768]{4,3,2,1,0:T(8,128)(2,1)}, u32[]{:S(2)}) copy-start(bf16[4,1,2,128,768]{4,3,2,1,0:T(8,128)(2,1)} %pad_maximum_fusion.1.last) | copy-start | bytes 4718596
  197.5 7.1 %copy-start.10 = (bf16[4,4,256,256]{3,2,1,0:T(8,128)(2,1)S(1)}, bf16[4,4,256,256]{3,2,1,0:T(8,128)(2,1)}, u32[]{:S(2)}) copy-start(bf16[4,4,256,256]{3,2,1,0:T(8,128)(2,1)} %copy-done.9) | copy-start | bytes 6291460
  202.5 1.4 copy-start.11
  204.6 9.0 %copy-start.12 = (f32[256,1]{1,0:T(8,128)}, f32[256,1]{1,0:T(8,128)S(1)}, u32[]{:S(2)}) copy-start(f32[256,1]{1,0:T(8,128)S(1)} %get-tuple-element.54.average) | copy-start | bytes 3076
  204.6 9.0 %copy-start.7 = (bf16[4,1,2,128,768]{4,3,2,1,0:T(8,128)(2,1)}, bf16[4,1,2,128,768]{4,3,2,1,0:T(8,128)(2,1)S(1)}, u32[]{:S(2)}) copy-start(bf16[4,1,2,128,768]{4,3,2,1,0:T(8,128)(2,1)S(1)} %collective-permute-done.11.last_other) | copy-start | bytes 4718596
  218.6 1.4 copy-start.1
  220.0 32.9 %all-to-all-start.3 = ((bf16[4,4,272,256]{3,2,1,0:T(8,128)(2,1)}), bf16[4,4,272,256]{3,2,1,0:T(8,128)(2,1)S(1)}, u32[]{:S(2)}, u32[]{:S(2)}) async-start(bf16[4,4,272,256]{3,2,1,0:T(8,128)(2,1)} %copy-done.1), calls=%async_computation.3 | async-start | bytes 4456448 | tf_op jit(solution)/shard_map/all_to_all | solution.py:447
  224.4 1.4 copy-start.4
  225.8 1.4 copy-start.8
  252.8 30.7 %all-to-all-start.4 = ((bf16[4,4,256,256]{3,2,1,0:T(8,128)(2,1)}), bf16[4,4,256,256]{3,2,1,0:T(8,128)(2,1)}, u32[]{:S(2)}, u32[]{:S(2)}) async-start(bf16[4,4,256,256]{3,2,1,0:T(8,128)(2,1)} %copy-done.2), calls=%async_computation.4 | async-start | bytes 4194304 | tf_op jit(solution)/shard_map/all_to_all | solution.py:449
  258.2 25.3 %copy-start.13 = (f32[256,1]{1,0:T(8,128)S(1)}, f32[256,1]{1,0:T(8,128)}, u32[]{:S(2)}) copy-start(f32[256,1]{1,0:T(8,128)} %copy-done.12) | copy-start | bytes 3076
  258.2 25.3 %copy-start.15 = (f32[256,1]{1,0:T(8,128)S(1)}, f32[256,1]{1,0:T(8,128)}, u32[]{:S(2)}) copy-start(f32[256,1]{1,0:T(8,128)} %copy-done.14) | copy-start | bytes 3076
  258.2 12.4 %collective-permute-start.14 = (bf16[272,256]{1,0:T(8,128)(2,1)S(1)}, bf16[272,256]{1,0:T(8,128)(2,1)S(1)}, u32[]{:S(2)}, u32[]{:S(2)}) collective-permute-start(bf16[272,256]{1,0:T(8,128)(2,1)S(1)} %get-tuple-element.71), channel_id=1, source_target_pairs={{0,12},{4,0},{8,4},{12,8},{1,13},{5,1},{9,5},{13,9},{2,14},{6,2},{... | collective-permute-start | bytes 417800 | tf_op jit(solution)/shard_map/ppermute | solution.py:37
  262.4 9.6 %collective-permute-start.13 = (bf16[272,256]{1,0:T(8,128)(2,1)S(1)}, bf16[272,256]{1,0:T(8,128)(2,1)S(1)}, u32[]{:S(2)}, u32[]{:S(2)}) collective-permute-start(bf16[272,256]{1,0:T(8,128)(2,1)S(1)} %get-tuple-element.72), channel_id=1, source_target_pairs={{0,8},{4,12},{8,0},{12,4},{1,9},{5,13},{9,1},{13,5},{2,10},{6,14},... | collective-permute-start | bytes 417800 | tf_op jit(solution)/shard_map/ppermute | solution.py:37
  264.4 10.4 %collective-permute-start.12 = (bf16[272,256]{1,0:T(8,128)(2,1)S(1)}, bf16[272,256]{1,0:T(8,128)(2,1)S(1)}, u32[]{:S(2)}, u32[]{:S(2)}) collective-permute-start(bf16[272,256]{1,0:T(8,128)(2,1)S(1)} %get-tuple-element.73), channel_id=1, source_target_pairs={{0,4},{4,8},{8,12},{12,0},{1,5},{5,9},{9,13},{13,1},{2,6},{6,10},{... | collective-permute-start | bytes 417800 | tf_op jit(solution)/shard_map/ppermute | solution.py:37
  285.1 77.0 %all-to-all-start.5 = ((bf16[32,24,256]{2,1,0:T(8,128)(2,1)}), bf16[32,24,256]{2,1,0:T(8,128)(2,1)S(1)}, u32[]{:S(2)}, u32[]{:S(2)}) async-start(bf16[32,24,256]{2,1,0:T(8,128)(2,1)} %bitcast.42), calls=%async_computation.5 | async-start | bytes 786432 | tf_op jit(solution)/shard_map/all_to_all | solution.py:476
  296.7 11.5 %collective-permute-start.15 = (f32[4,256]{1,0:T(4,128)S(1)}, f32[4,256]{1,0:T(4,128)S(1)}, u32[]{:S(2)}, u32[]{:S(2)}) collective-permute-start(f32[4,256]{1,0:T(4,128)S(1)} %get-tuple-element.81), channel_id=1, source_target_pairs={{0,4},{4,8},{8,12},{12,0},{1,5},{5,9},{9,13},{13,1},{2,6},{6,10},{... | collective-permute-start | bytes 12296 | tf_op jit(solution)/shard_map/ppermute | solution.py:37
  299.3 8.9 %collective-permute-start.17 = (f32[4,256]{1,0:T(4,128)S(1)}, f32[4,256]{1,0:T(4,128)S(1)}, u32[]{:S(2)}, u32[]{:S(2)}) collective-permute-start(f32[4,256]{1,0:T(4,128)S(1)} %get-tuple-element.82), channel_id=1, source_target_pairs={{0,12},{4,0},{8,4},{12,8},{1,13},{5,1},{9,5},{13,9},{2,14},{6,2},{... | collective-permute-start | bytes 12296 | tf_op jit(solution)/shard_map/ppermute | solution.py:37
  302.7 6.8 %collective-permute-start.16 = (f32[4,256]{1,0:T(4,128)S(1)}, f32[4,256]{1,0:T(4,128)S(1)}, u32[]{:S(2)}, u32[]{:S(2)}) collective-permute-start(f32[4,256]{1,0:T(4,128)S(1)} %get-tuple-element.83), channel_id=1, source_target_pairs={{0,8},{4,12},{8,0},{12,4},{1,9},{5,13},{9,1},{13,5},{2,10},{6,14},... | collective-permute-start | bytes 12296 | tf_op jit(solution)/shard_map/ppermute | solution.py:37
  309.5 3.1 collective-permute-start.18
  312.6 5.6 %collective-permute-start.22 = (f32[12,256]{1,0:T(8,128)S(1)}, f32[12,256]{1,0:T(8,128)S(1)}, u32[]{:S(2)}, u32[]{:S(2)}) collective-permute-start(f32[12,256]{1,0:T(8,128)S(1)} %fusion.12), channel_id=1, source_target_pairs={{0,32},{32,0},{64,96},{96,64},{1,33},{33,1},{65,97},{97,65},{2,34}... | collective-permute-start | bytes 36872 | tf_op jit(solution)/shard_map/ppermute | solution.py:42
  318.2 7.1 %collective-permute-start.23 = (f32[12,256]{1,0:T(8,128)S(1)}, f32[12,256]{1,0:T(8,128)S(1)}, u32[]{:S(2)}, u32[]{:S(2)}) collective-permute-start(f32[12,256]{1,0:T(8,128)S(1)} %add.203), channel_id=1, source_target_pairs={{0,64},{32,96},{64,0},{96,32},{1,65},{33,97},{65,1},{97,33},{2,66}... | collective-permute-start | bytes 36872 | tf_op jit(solution)/shard_map/ppermute | solution.py:42
  325.4 20.8 %collective-permute-start.24 = (f32[12,256]{1,0:T(8,128)S(1)}, f32[12,256]{1,0:T(8,128)S(1)}, u32[]{:S(2)}, u32[]{:S(2)}) collective-permute-start(f32[12,256]{1,0:T(8,128)S(1)} %add.204), channel_id=1, source_target_pairs={{0,128},{128,0},{256,384},{384,256},{1,129},{129,1},{257,385},{385... | collective-permute-start | bytes 36872 | tf_op jit(solution)/shard_map/ppermute | solution.py:42
  334.9 26.3 %collective-permute-start.21 = (bf16[256,256]{1,0:T(8,128)(2,1)S(1)}, bf16[256,256]{1,0:T(8,128)(2,1)S(1)}, u32[]{:S(2)}, u32[]{:S(2)}) collective-permute-start(bf16[256,256]{1,0:T(8,128)(2,1)S(1)} %get-tuple-element.75), channel_id=1, source_target_pairs={{0,12},{4,0},{8,4},{12,8},{1,13},{5,1},{9,5},{13,9},{2,14},{6,2},{... | collective-permute-start | bytes 393224 | tf_op jit(solution)/shard_map/ppermute | solution.py:37
  339.9 21.4 %collective-permute-start.20 = (bf16[256,256]{1,0:T(8,128)(2,1)S(1)}, bf16[256,256]{1,0:T(8,128)(2,1)S(1)}, u32[]{:S(2)}, u32[]{:S(2)}) collective-permute-start(bf16[256,256]{1,0:T(8,128)(2,1)S(1)} %get-tuple-element.76), channel_id=1, source_target_pairs={{0,8},{4,12},{8,0},{12,4},{1,9},{5,13},{9,1},{13,5},{2,10},{6,14},... | collective-permute-start | bytes 393224 | tf_op jit(solution)/shard_map/ppermute | solution.py:37
  341.8 19.4 %collective-permute-start.19 = (bf16[256,256]{1,0:T(8,128)(2,1)S(1)}, bf16[256,256]{1,0:T(8,128)(2,1)S(1)}, u32[]{:S(2)}, u32[]{:S(2)}) collective-permute-start(bf16[256,256]{1,0:T(8,128)(2,1)S(1)} %get-tuple-element.77), channel_id=1, source_target_pairs={{0,4},{4,8},{8,12},{12,0},{1,5},{5,9},{9,13},{13,1},{2,6},{6,10},{... | collective-permute-start | bytes 393224 | tf_op jit(solution)/shard_map/ppermute | solution.py:37
  346.1 14.5 %collective-permute-start.25 = (f32[12,256]{1,0:T(8,128)S(1)}, f32[12,256]{1,0:T(8,128)S(1)}, u32[]{:S(2)}, u32[]{:S(2)}) collective-permute-start(f32[12,256]{1,0:T(8,128)S(1)} %add.205), channel_id=1, source_target_pairs={{0,256},{128,384},{256,0},{384,128},{1,257},{129,385},{257,1},{385... | collective-permute-start | bytes 36872 | tf_op jit(solution)/shard_map/ppermute | solution.py:42
  (3 other events, 3.3 us)
Sparse Core Ops, SparseCore 0:
  24.0 114.3 all-gather.2

commit v3 on v2

--- a/solution.py
+++ b/solution.py
@@ -86,9 +86,11 @@
     return lax.rem(zh + step, count)
 
 
-def weight_of(first, first_other, last, last_other, n, which):
-    own, other = (first, first_other) if n < 3 else (last, last_other)
-    return jnp.concatenate([own[0, n % 3, which], other[0, n % 3, which]], axis=0)
+def weight_of(parts, n, which):
+    group, place = ((0, 0), (1, 0), (1, 1), (2, 0))[n]
+    return jnp.concatenate(
+        [parts[group][0, place, which], parts[3 + group][0, place, which]], axis=0
+    )
 
 
 def gate_kernel(place, gathered, member, grad_out, table_out):
@@ -163,9 +165,10 @@
 
 
 def hidden_kernel(
-    modulated, scaled, member, first, first_other, last, last_other,
+    modulated, scaled, member, part0, part1, part2, part3, part4, part5,
     hidden_out, pre_grad_out, sums_out, pre_total, grad_total,
 ):
+    parts = (part0, part1, part2, part3, part4, part5)
     live = member[...]
     rows = scaled.shape[2]
     step = pl.program_id(0)
@@ -176,9 +179,9 @@
         grad_total[...] = jnp.zeros_like(grad_total)
 
     for n in range(scaled.shape[1]):
-        up = weight_of(first, first_other, last, last_other, n, 0)
+        up = weight_of(parts, n, 0)
         pre_total[...] += jnp.dot(modulated[0, n], up, preferred_element_type=jnp.float32)
-        down = weight_of(first, first_other, last, last_other, n, 1)
+        down = weight_of(parts, n, 1)
         grad_total[...] += jnp.dot(scaled[0, n], down, preferred_element_type=jnp.float32)
 
     @pl.when(step == pl.num_programs(0) - 1)
@@ -200,7 +203,7 @@
         sums_out[...] = jnp.concatenate([high, sums - high], axis=0).astype(jnp.bfloat16)
 
 
-def outward_kernel(place, hidden, first, first_other, last, last_other, *refs):
+def outward_kernel(place, hidden, *refs):
     out = refs[-1]
     zh, c = place[1], place[2]
     count = out.shape[1]
@@ -208,15 +211,15 @@
     half = rows // 2
     low, high = halves(c, half)
     for n in range(count):
-        weight = weight_of(first, first_other, last, last_other, n, 0)
+        weight = weight_of(refs[:6], n, 0)
         value = jnp.dot(weight, hidden[...], preferred_element_type=jnp.float32).astype(
             jnp.bfloat16
         )
         zi = zh_of(zh, n, count)
         out[0, zi, low, :] = value[:half]
         out[0, zi, high, :] = value[half:]
-        if len(refs) == 2:
-            out[0, zi, rows : rows + 16, :] = refs[0][...]
+        if len(refs) == 8:
+            out[0, zi, rows : rows + 16, :] = refs[6][...]
 
 
 def joined_sums(terms):
@@ -225,23 +228,37 @@
     return jnp.concatenate([high, total - high], axis=0)
 
 
-def fold_kernel(place, blocks, *refs):
+def fold_kernel(place, blocks, out):
+    count, places, height, width = blocks.shape
+
+    def step(m, carry):
+        total = blocks[0, m].astype(jnp.float32)
+        for k in range(1, count):
+            total = total + blocks[k, m].astype(jnp.float32)
+        out[m, 0:width] = total[0:width].astype(jnp.bfloat16)
+        out[m, width:height] = joined_sums(total[width:height]).astype(jnp.bfloat16)
+        return carry
+
+    lax.fori_loop(0, places, step, 0)
+
+
+def fold_out_kernel(place, blocks, grad, member, out):
     zl = place[3]
-    count, places, height, width = blocks.shape
-    out = refs[0] if height > width else refs[2]
+    count, places, width, _ = blocks.shape
 
     def step(m, carry):
         total = blocks[0, m].astype(jnp.float32)
         for k in range(1, count):
             total = total + blocks[k, m].astype(jnp.float32)
         to = lax.rem(m - zl + places, places)
-        out[to, 0:width] = total[0:width].astype(jnp.bfloat16)
-        if height > width:
-            out[to, width:height] = joined_sums(total[width:height]).astype(jnp.bfloat16)
-        else:
-            grad, member, _, totals = refs
-            part = image_sums(member[...], grad[m].astype(jnp.float32) * total.T)
-            totals[to] = jnp.concatenate(part, axis=0)
+        out[to, 0:width] = total.astype(jnp.bfloat16)
+        part = image_sums(member[...], grad[m].astype(jnp.float32) * total.T)
+        part = jnp.concatenate(part, axis=0)
+        high = part.astype(jnp.bfloat16).astype(jnp.float32)
+        middle = (part - high).astype(jnp.bfloat16).astype(jnp.float32)
+        low = (part - high) - middle
+        terms = jnp.concatenate([high, middle, low, jnp.zeros_like(low)], axis=0)
+        out[to, width : width + 16] = terms.astype(jnp.bfloat16)
         return carry
 
     lax.fori_loop(0, places, step, 0)
@@ -261,14 +278,13 @@
 
 
 def finish_in_kernel(
-    features, piece0, piece1, piece2, piece3,
-    rows, grad, average, inv_scale, member, table, index, back, totals,
+    features, pieces, rows, grad, average, inv_scale, member, table, index, back, totals
 ):
     live = member[...]
     balanced = rows.shape[0]
-    total = piece0[...].astype(jnp.float32)
-    for piece in (piece1, piece2, piece3):
-        total = total + piece[...].astype(jnp.float32)
+    total = pieces[0].astype(jnp.float32)
+    for k in range(1, pieces.shape[0]):
+        total = total + pieces[k].astype(jnp.float32)
     mod_in_grad = total[0:balanced].T
     sums = total[balanced : balanced + 8] + total[balanced + 8 : balanced + 16]
     means = jnp.concatenate([sums, jnp.zeros((120, balanced), jnp.float32)], axis=0).T / features
@@ -286,9 +302,10 @@
 
 def finish_out_kernel(piece0, piece1, piece2, piece3, rows, member, table, out):
     live = member[...]
-    branch = piece0[...].astype(jnp.float32)
+    balanced = rows.shape[0]
+    branch = piece0[0:balanced].astype(jnp.float32)
     for piece in (piece1, piece2, piece3):
-        branch = branch + piece[...].astype(jnp.float32)
+        branch = branch + piece[0:balanced].astype(jnp.float32)
     branch = branch.T
     gate = sample_mix(live, table[8:12])
     out[...] = (rows[...].astype(jnp.float32) + gate * branch).astype(jnp.bfloat16)
@@ -332,6 +349,7 @@
     weights = jnp.stack([w_up, w_down.T])
     before = shifted(weights, "zh", 1)
     after = shifted(weights, "zh", -1)
+    near = direct_pieces(weights[None], "y")
 
     table = modulation.reshape(-1, width_local)
     pad = jnp.zeros((16 - table.shape[0], width_local), f32)
@@ -346,15 +364,15 @@
     local_rows = ((device_ids[:, None] - own_start) & low) + groups * slot_ids
     outgoing = hidden_in[local_rows.reshape(-1)].reshape(groups, per_pair, width_local)
     gathered = lax.all_gather(payload, TP, axis=0)
-    far = jnp.concatenate([shifted(before[:1], "zh", 1), shifted(after[1:], "zh", -1)], axis=0)
-    first = direct_pieces(jnp.stack([weights, before, after]), "y")
     incoming = lax.all_to_all(outgoing, DP, split_axis=0, concat_axis=0, tiled=True)
     global_rows = position + groups * jnp.arange(balanced, dtype=jnp.int32)
     before_row = row_ends[None, :] <= global_rows[:, None]
     owners = jnp.sum(before_row.astype(jnp.int32), axis=1)
     owner_start = jnp.sum(jnp.where(before_row, live_rows[None, :], 0), axis=1)
     owner_slot = (global_rows - owner_start) >> bits
-    incoming, far, first = lax.optimization_barrier((incoming, far, first))
+    incoming, before, after, near = lax.optimization_barrier((incoming, before, after, near))
+    far = jnp.concatenate([shifted(before[:1], "zh", 1), shifted(after[1:], "zh", -1)], axis=0)
+    pair = direct_pieces(jnp.stack([before, after]), "y")
     rows_bal = incoming.reshape(groups * per_pair, width_local)[owners * per_pair + owner_slot]
     sample_ends = jnp.cumsum(sample_tokens)
     sample_starts = sample_ends - sample_tokens
@@ -364,13 +382,15 @@
     ).astype(f32)
 
     rows_zl = spread(rows_bal, "zl")
-    rows_zl, gathered = lax.optimization_barrier((rows_zl, gathered))
+    rows_zl, far, pair, gathered = lax.optimization_barrier((rows_zl, far, pair, gathered))
     last = direct_pieces(far[None], "y")
-    first_other = shifted(first, "c", 1)
+    near_other = shifted(near, "c", 1)
+    pair_other = shifted(pair, "c", 1)
     rows_all = spread(rows_zl, "x")
 
     by_place = gathered.reshape(4, 4, -1, width_local)
-    grad_zl = lax.dynamic_index_in_dim(by_place, lax.axis_index("x"), 1, keepdims=False)[:, :balanced]
+    grad_zl = lax.dynamic_index_in_dim(by_place, lax.axis_index("x"), 1, keepdims=False)
+    grad_zl = grad_zl[:, :balanced]
     place = jnp.stack([lax.axis_index(a) for a in ("y", "zh", "c", "zl")]).astype(jnp.int32)
     block_shape = shape((4, 4, balanced, width_local), bf16)
     column = shape((balanced, 1), f32)
@@ -382,11 +402,11 @@
         0,
         place, gathered, member,
     )
-    rows_all, first_other, last, scaled_grad = lax.optimization_barrier(
-        (rows_all, first_other, last, scaled_grad)
+    rows_all, near_other, pair_other, last, scaled_grad = lax.optimization_barrier(
+        (rows_all, near_other, pair_other, last, scaled_grad)
     )
     last_other = shifted(last, "c", 1)
-    weight_parts = (first, first_other, last, last_other)
+    weight_parts = (near, pair, last, near_other, pair_other, last_other)
     modulated, average, inv_scale = call(
         rows_kernel,
         (shape((4, 4, balanced + 16, width_local), bf16), column, column),
@@ -408,9 +428,8 @@
             by_dy(4, balanced + 16, width_local),
             by_dy(4, balanced, width_local),
             whole(balanced, SAMPLES),
-            by_dy(3, 2, *planes), by_dy(3, 2, *planes),
-            by_dy(1, 2, *planes), by_dy(1, 2, *planes),
-        ],
+        ]
+        + [by_dy(n, 2, *planes) for n in (1, 2, 1)] * 2,
         out_specs=(whole(hid, balanced), whole(hid, balanced), whole(16, balanced)),
         scratch_shapes=[
             pltpu.VMEM((balanced + 16, hid), f32), pltpu.VMEM((balanced, hid), f32)
@@ -429,7 +448,8 @@
             grid_spec=pltpu.PrefetchScalarGridSpec(
                 num_scalar_prefetch=1,
                 grid=(4,),
-                in_specs=[whole(hid, balanced), pick(3), pick(3), pick(1), pick(1)]
+                in_specs=[whole(hid, balanced)]
+                + [pick(n) for n in (1, 2, 1)] * 2
                 + [whole(*e.shape) for e in extra],
                 out_specs=pl.BlockSpec(
                     (1, 4, height, balanced),
@@ -441,24 +461,21 @@
             cost_estimate=pl.CostEstimate(flops=5 * US, bytes_accessed=0, transcendentals=0),
         )(place, units, *weight_parts, *extra)
 
+    partial_out = outward(1, hidden)
     partial_in = outward(0, pre_grad, sums)
-    partial_out = outward(1, hidden)
-
-    from_x = lax.all_to_all(partial_in, "x", split_axis=0, concat_axis=0, tiled=True)
-    from_x, partial_out = lax.optimization_barrier((from_x, partial_out))
     out_x = lax.all_to_all(partial_out, "x", split_axis=0, concat_axis=0, tiled=True)
-    (in_x,) = call(fold_kernel, (shape(partial_in.shape[1:], bf16),), [], 2 * US, 0, place, from_x)
-    in_zl = [in_x[0]] + [shifted(in_x[k], "zl", k) for k in (1, 2, 3)]
-    out_x, in_zl = lax.optimization_barrier((out_x, in_zl))
-    out_x, totals_zl = call(
-        fold_kernel,
-        (shape(partial_out.shape[1:], bf16), shape((4, SAMPLES, width_local), f32)),
-        [], 3 * US, 0,
+    out_x, partial_in = lax.optimization_barrier((out_x, partial_in))
+    in_x = lax.all_to_all(partial_in, "x", split_axis=0, concat_axis=0, tiled=True)
+    (out_x,) = call(
+        fold_out_kernel, (shape((4, width_local + 16, balanced), bf16),), [], 3 * US, 0,
         place, out_x, grad_zl, member,
     )
-    totals_out = totals_zl[0]
-    for k in (1, 2, 3):
-        totals_out = totals_out + shifted(totals_zl[k], "zl", k)
+    out_zl = [out_x[0]] + [shifted(out_x[k], "zl", k) for k in (1, 2, 3)]
+    in_x, out_zl = lax.optimization_barrier((in_x, out_zl))
+    terms = jnp.sum(jnp.stack([o[width_local : width_local + 12] for o in out_zl]).astype(f32), 0)
+    totals_out = (terms[0:4] + terms[4:8]) + terms[8:12]
+    (in_x,) = call(fold_kernel, (shape(partial_in.shape[1:], bf16),), [], 2 * US, 0, place, in_x)
+    in_zl = lax.all_to_all(in_x, "zl", split_axis=0, concat_axis=0, tiled=True)
 
     source_rows = ((position - row_starts[:, None]) & low) + groups * slot_ids
     back_index = jnp.where(
@@ -470,15 +487,13 @@
         functools.partial(finish_in_kernel, model_width),
         (shape((slots_in, width_local), bf16), shape((2 * SAMPLES, width_local), f32)),
         [], 4 * US, 0,
-        *in_zl, rows_bal, out_grad, average, inv_scale, member, table, back_index,
+        in_zl, rows_bal, out_grad, average, inv_scale, member, table, back_index,
     )
     returning = returning.reshape(groups, per_pair, width_local)
     arrived = lax.all_to_all(returning, DP, split_axis=0, concat_axis=0, tiled=True)
 
-    mod_grad = summed(jnp.concatenate([totals_in, totals_out], axis=0), "c")
-    mod_grad, out_x = lax.optimization_barrier((mod_grad, out_x))
-    mod_grad = summed(summed(mod_grad, "y"), "zh").reshape(modulation.shape)
-    out_zl = [out_x[0]] + [shifted(out_x[k], "zl", k) for k in (1, 2, 3)]
+    mod_grad = jnp.concatenate([totals_in, totals_out], axis=0)
+    mod_grad = summed(summed(summed(mod_grad, "c"), "y"), "zh").reshape(modulation.shape)
     (block_out,) = call(
         finish_out_kernel, (shape((balanced, width_local), bf16),), [], 2 * US, 0,
         *out_zl, rows_bal, member, table,

time: 372 us -> 364 us (0.978)
  the two profiles are of different devices: /device:TPU:40 before, /device:TPU:8 now
where the time goes in v3:
time: 364 us; the launch traced here: 362 us
  starting transfers between devices  163 us (45%)
  waiting for transfers between devices  114 us (31%)
  Pallas kernels  38.1 us (10%)
  local copies, waits for them, and re-layouts  21.9 us (6%)
  between operations  14.6 us (4%)
  other arithmetic  11.2 us (3%)
    ppermute x19, starting transfers between devices, shifted(): lax.ppermute(value, axis, [(i, (i + step) % size) for i in range(size)])  67.4 us
    ppermute x19, waiting for transfers between devices, shifted(): lax.ppermute(value, axis, [(i, (i + step) % size) for i in range(size)])  65.4 us
    ppermute x5, starting transfers between devices, crossed(): return lax.ppermute(value, axis, [(i, i ^ mask) for i in range(size)])  27.6 us
    all_to_all x2, starting transfers between devices, spread(): return lax.all_to_all(copies, axis, split_axis=0, concat_axis=0, tiled=True)  26 us
    all_to_all x1, waiting for transfers between devices, body(): lax.all_to_all(partial_out, 'x', split_axis=0, concat_axis=0, tiled=True)  19.4 us
    all_to_all x1, starting transfers between devices, body(): lax.all_to_all(outgoing, DP, split_axis=0, concat_axis=0, tiled=True)  18.5 us
    pallas_call x7, Pallas kernels, call(): pl.pallas_call(kernel, out_shape=outs, in_specs=[SMEM_SPEC if a.ndim == 1...  17 us
    all_to_all x1, waiting for transfers between devices, body(): in_zl = lax.all_to_all(in_x, 'zl', split_axis=0, concat_axis=0, tiled=True)  13.7 us
  transfers between devices with their start and end apart: 32, of which 18 were waited for; matrix products, arithmetic and copies ran while one was open for 6% of the time, Pallas kernels for 5%

profile of v3, /device:TPU:8, one launch (start us, length us, event | category | flops | bytes accessed | tf_op | source)
XLA Modules:
  0.0 362.1 jit_solution(12083368319618659930)
XLA Ops:
  13.4 3.3 gather_fusion
  16.7 18.5 %all-to-all-start = ((bf16[32,24,256]{2,1,0:T(8,128)(2,1)}), bf16[32,24,256]{2,1,0:T(8,128)(2,1)S(1)}, u32[]{:S(2)}, u32[]{:S(2)}) async-start(bf16[32,24,256]{2,1,0:T(8,128)(2,1)} %bitcast.4), calls=%async_computation | async-start | bytes 786432 | tf_op jit(solution)/shard_map/all_to_all | solution.py:367
  35.4 7.3 %collective-permute-start.1 = (bf16[2,128,768]{2,1,0:T(8,128)(2,1)S(1)}, bf16[2,128,768]{2,1,0:T(8,128)(2,1)S(1)}, u32[]{:S(2)}, u32[]{:S(2)}) collective-permute-start(bf16[2,128,768]{2,1,0:T(8,128)(2,1)S(1)} %get-tuple-element.77), channel_id=1, source_target_pairs={{0,384},{128,0},{256,128},{384,256},{1,385},{129,1},{257,129},{385... | collective-permute-start | bytes 1179656 | tf_op jit(solution)/shard_map/ppermute | solution.py:37
  42.8 2.4 collective-permute-start
  45.2 2.1 collective-permute-start.4
  47.3 4.6 %collective-permute-start.3 = (bf16[1,2,128,768]{3,2,1,0:T(8,128)(2,1)S(1)}, bf16[1,2,128,768]{3,2,1,0:T(8,128)(2,1)S(1)}, u32[]{:S(2)}, u32[]{:S(2)}) collective-permute-start(bf16[1,2,128,768]{3,2,1,0:T(8,128)(2,1)S(1)} %get-tuple-element.76), channel_id=1, source_target_pairs={{0,64},{32,96},{64,0},{96,32},{1,65},{33,97},{65,1},{97,33},{2,66}... | collective-permute-start | bytes 1179656 | tf_op jit(solution)/shard_map/ppermute | solution.py:37
  51.9 3.7 %collective-permute-start.2 = (bf16[1,2,128,768]{3,2,1,0:T(8,128)(2,1)S(1)}, bf16[1,2,128,768]{3,2,1,0:T(8,128)(2,1)S(1)}, u32[]{:S(2)}, u32[]{:S(2)}) collective-permute-start(bf16[1,2,128,768]{3,2,1,0:T(8,128)(2,1)S(1)} %get-tuple-element.76), channel_id=1, source_target_pairs={{0,32},{32,64},{64,96},{96,0},{1,33},{33,65},{65,97},{97,1},{2,34}... | collective-permute-start | bytes 1179656 | tf_op jit(solution)/shard_map/ppermute | solution.py:37
  55.8 3.5 collective-permute-done.4
  59.3 8.9 %collective-permute-done.3 = bf16[1,2,128,768]{3,2,1,0:T(8,128)(2,1)S(1)} collective-permute-done((bf16[1,2,128,768]{3,2,1,0:T(8,128)(2,1)S(1)}, bf16[1,2,128,768]{3,2,1,0:T(8,128)(2,1)S(1)}, u32[]{:S(2)}, u32[]{:S(2)}) %collective-permute-start.3) | collective-permute-done | bytes 393248 | tf_op jit(solution)/shard_map/ppermute | solution.py:37
  68.1 2.6 collective-permute-done.2
  72.1 15.2 %collective-permute-done = bf16[2,128,768]{2,1,0:T(8,128)(2,1)S(1)} collective-permute-done((bf16[2,128,768]{2,1,0:T(8,128)(2,1)S(1)}, bf16[2,128,768]{2,1,0:T(8,128)(2,1)S(1)}, u32[]{:S(2)}, u32[]{:S(2)}) %collective-permute-start) | collective-permute-done | bytes 393248 | tf_op jit(solution)/shard_map/ppermute | solution.py:37
  89.2 21.1 %all-to-all-start.1 = ((bf16[4,256,256]{2,1,0:T(8,128)(2,1)}), bf16[4,256,256]{2,1,0:T(8,128)(2,1)S(1)}, u32[]{:S(2)}, u32[]{:S(2)}) async-start(bf16[4,256,256]{2,1,0:T(8,128)(2,1)} %broadcast_in_dim.33), calls=%async_computation.1 | async-start | bytes 1048576 | tf_op jit(solution)/shard_map/all_to_all | solution.py:51
  110.5 4.2 %collective-permute-start.8 = (bf16[2,2,128,768]{3,2,1,0:T(8,128)(2,1)S(1)}, bf16[2,2,128,768]{3,2,1,0:T(8,128)(2,1)S(1)}, u32[]{:S(2)}, u32[]{:S(2)}) collective-permute-start(bf16[2,2,128,768]{3,2,1,0:T(8,128)(2,1)S(1)} %get-tuple-element.70), channel_id=1, source_target_pairs={{0,64},{32,96},{64,0},{96,32},{1,65},{33,97},{65,1},{97,33},{2,66}... | collective-permute-start | bytes 2359304 | tf_op jit(solution)/shard_map/ppermute | solution.py:37
  116.6 3.9 %collective-permute-start.9 = (bf16[2,2,128,768]{3,2,1,0:T(8,128)(2,1)S(1)}, bf16[2,2,128,768]{3,2,1,0:T(8,128)(2,1)S(1)}, u32[]{:S(2)}, u32[]{:S(2)}) collective-permute-start(bf16[2,2,128,768]{3,2,1,0:T(8,128)(2,1)S(1)} %get-tuple-element.70), channel_id=1, source_target_pairs={{0,96},{32,0},{64,32},{96,64},{1,97},{33,1},{65,33},{97,65},{2,98}... | collective-permute-start | bytes 2359304 | tf_op jit(solution)/shard_map/ppermute | solution.py:37
  120.6 6.5 %collective-permute-start.6 = (bf16[1,128,768]{2,1,0:T(8,128)(2,1)S(1)}, bf16[1,128,768]{2,1,0:T(8,128)(2,1)S(1)}, u32[]{:S(2)}, u32[]{:S(2)}) collective-permute-start(bf16[1,128,768]{2,1,0:T(8,128)(2,1)S(1)} %slice.43), channel_id=1, source_target_pairs={{0,384},{128,0},{256,128},{384,256},{1,385},{129,1},{257,129},{385... | collective-permute-start | bytes 589832 | tf_op jit(solution)/shard_map/ppermute | solution.py:37
  127.1 3.3 collective-permute-start.5
  130.3 3.0 collective-permute-done.6
  133.4 5.7 %collective-permute-done.5 = bf16[1,128,768]{2,1,0:T(8,128)(2,1)S(1)} collective-permute-done((bf16[1,128,768]{2,1,0:T(8,128)(2,1)S(1)}, bf16[1,128,768]{2,1,0:T(8,128)(2,1)S(1)}, u32[]{:S(2)}, u32[]{:S(2)}) %collective-permute-start.5) | collective-permute-done | bytes 196640 | tf_op jit(solution)/shard_map/ppermute | solution.py:37
  139.1 10.5 %collective-permute-done.7 = bf16[2,2,128,768]{3,2,1,0:T(8,128)(2,1)S(1)} collective-permute-done((bf16[2,2,128,768]{3,2,1,0:T(8,128)(2,1)S(1)}, bf16[2,2,128,768]{3,2,1,0:T(8,128)(2,1)S(1)}, u32[]{:S(2)}, u32[]{:S(2)}) %collective-permute-start.7) | collective-permute-done | bytes 786464 | tf_op jit(solution)/shard_map/ppermute | solution.py:37
  153.4 2.4 collective-permute-start.10
  157.3 4.9 %all-to-all-start.2 = ((bf16[4,4,256,256]{3,2,1,0:T(8,128)(2,1)}), bf16[4,4,256,256]{3,2,1,0:T(8,128)(2,1)S(1)}, u32[]{:S(2)}, u32[]{:S(2)}) async-start(bf16[4,4,256,256]{3,2,1,0:T(8,128)(2,1)} %broadcast_in_dim.34), calls=%async_computation.2 | async-start | bytes 4194304 | tf_op jit(solution)/shard_map/all_to_all | solution.py:51
  162.5 2.9 collective-permute-start.14
  165.3 3.8 %collective-permute-start.13 = (bf16[1,2,128,768]{3,2,1,0:T(8,128)(2,1)S(1)}, bf16[1,2,128,768]{3,2,1,0:T(8,128)(2,1)S(1)}, u32[]{:S(2)}, u32[]{:S(2)}) collective-permute-start(bf16[1,2,128,768]{3,2,1,0:T(8,128)(2,1)S(1)} %bitcast.65), channel_id=1, source_target_pairs={{0,64},{32,96},{64,0},{96,32},{1,65},{33,97},{65,1},{97,33},{2,66}... | collective-permute-start | bytes 1179656 | tf_op jit(solution)/shard_map/ppermute | solution.py:37
  169.2 4.1 %collective-permute-start.12 = (bf16[1,2,128,768]{3,2,1,0:T(8,128)(2,1)S(1)}, bf16[1,2,128,768]{3,2,1,0:T(8,128)(2,1)S(1)}, u32[]{:S(2)}, u32[]{:S(2)}) collective-permute-start(bf16[1,2,128,768]{3,2,1,0:T(8,128)(2,1)S(1)} %bitcast.66), channel_id=1, source_target_pairs={{0,32},{32,64},{64,96},{96,0},{1,33},{33,65},{65,97},{97,1},{2,34}... | collective-permute-start | bytes 1179656 | tf_op jit(solution)/shard_map/ppermute | solution.py:37
  175.1 3.6 shard_map.94
  178.7 5.7 %collective-permute-done.13 = bf16[1,2,128,768]{3,2,1,0:T(8,128)(2,1)S(1)} collective-permute-done((bf16[1,2,128,768]{3,2,1,0:T(8,128)(2,1)S(1)}, bf16[1,2,128,768]{3,2,1,0:T(8,128)(2,1)S(1)}, u32[]{:S(2)}, u32[]{:S(2)}) %collective-permute-start.13) | collective-permute-done | bytes 393248 | tf_op jit(solution)/shard_map/ppermute | solution.py:37
  184.4 2.9 collective-permute-done.12
  190.6 5.1 %shard_map.95 = (bf16[4,4,272,256]{3,2,1,0:T(8,128)(2,1)S(1)}, f32[256,1]{1,0:T(8,128)S(1)}, f32[256,1]{1,0:T(8,128)S(1)}) custom-call(s32[4]{0:T(128)S(1)} %pad_add_fusion.place, bf16[4,4,256,256]{3,2,1,0:T(8,128)(2,1)S(1)} %all-to-all-done.2.rows, f32[16,16,256]{2,1,0:T(8,128)S(1)} %get-tuple-element.43.table_in, f32[256,4]{1,0:T(8,128)S(1)} %and_convert_fusion.member), custom_call_target="tpu_custom_call" | custom-call | flops 6000000000 | tf_op jit(solution)/shard_map/pallas_call | solution.py:323
  199.5 8.9 %shard_map.96 = (bf16[768,256]{1,0:T(8,128)(2,1)S(1)}, bf16[768,256]{1,0:T(8,128)(2,1)S(1)}, bf16[16,256]{1,0:T(8,128)(2,1)S(1)}) custom-call(bf16[4,4,272,256]{3,2,1,0:T(8,128)(2,1)} %copy-done.8, bf16[4,4,256,256]{3,2,1,0:T(8,128)(2,1)} %copy-done.7, f32[256,4]{1,0:T(8,128)S(1)} %and_convert_fusion.member, ...), custom_call_target="tpu_custom_call" | custom-call | flops 8000000000 | tf_op jit(solution)/shard_map/pallas_call | solution.py:423
  208.4 6.1 %shard_map.97 = bf16[4,4,256,256]{3,2,1,0:T(8,128)(2,1)} custom-call(s32[4]{0:T(128)S(1)} %pad_add_fusion.place, bf16[768,256]{1,0:T(8,128)(2,1)S(1)} %get-tuple-element.49.hidden, bf16[4,1,2,128,768]{4,3,2,1,0:T(8,128)(2,1)} %pad_maximum_fusion.1.part0.refs_0_, bf16[4,2,2,128,768]{4,3,2,1,0:T(8,128)(2,1)} %pad_maximum_fusion.part1.refs_1_, ...), custom_call_target="tpu_custom_call" | custom-call | flops 5000000000 | tf_op jit(solution)/shard_map/pallas_call | solution.py:446
  214.5 4.5 %all-to-all-start.3 = ((bf16[4,4,256,256]{3,2,1,0:T(8,128)(2,1)}), bf16[4,4,256,256]{3,2,1,0:T(8,128)(2,1)S(1)}, u32[]{:S(2)}, u32[]{:S(2)}) async-start(bf16[4,4,256,256]{3,2,1,0:T(8,128)(2,1)} %shard_map.97), calls=%async_computation.3 | async-start | bytes 4194304 | tf_op jit(solution)/shard_map/all_to_all | solution.py:466
  220.4 6.1 %shard_map.98 = bf16[4,4,272,256]{3,2,1,0:T(8,128)(2,1)} custom-call(s32[4]{0:T(128)S(1)} %pad_add_fusion.place, bf16[768,256]{1,0:T(8,128)(2,1)S(1)} %get-tuple-element.50.hidden, bf16[4,1,2,128,768]{4,3,2,1,0:T(8,128)(2,1)} %pad_maximum_fusion.1.part0.refs_0_, bf16[4,2,2,128,768]{4,3,2,1,0:T(8,128)(2,1)} %pad_maximum_fusion.part1.refs_1_, ...), custom_call_target="tpu_custom_call" | custom-call | flops 5000000000 | tf_op jit(solution)/shard_map/pallas_call | solution.py:446
  226.6 19.4 %all-to-all-done.3.blocks = bf16[4,4,256,256]{3,2,1,0:T(8,128)(2,1)S(1)} async-done(((bf16[4,4,256,256]{3,2,1,0:T(8,128)(2,1)}), bf16[4,4,256,256]{3,2,1,0:T(8,128)(2,1)S(1)}, u32[]{:S(2)}, u32[]{:S(2)}) %all-to-all-start.3) | async-done | bytes 2097184 | tf_op jit(solution)/shard_map/all_to_all | solution.py:466
  247.4 3.6 all-to-all-start.4
  254.7 5.5 %collective-permute-start.18 = (bf16[272,256]{1,0:T(8,128)(2,1)S(1)}, bf16[272,256]{1,0:T(8,128)(2,1)S(1)}, u32[]{:S(2)}, u32[]{:S(2)}) collective-permute-start(bf16[272,256]{1,0:T(8,128)(2,1)S(1)} %get-tuple-element.71), channel_id=1, source_target_pairs={{0,12},{4,0},{8,4},{12,8},{1,13},{5,1},{9,5},{13,9},{2,14},{6,2},{... | collective-permute-start | bytes 417800 | tf_op jit(solution)/shard_map/ppermute | solution.py:37
  260.2 2.3 collective-permute-start.17
  262.4 2.6 collective-permute-start.16
  265.1 7.6 %collective-permute-done.17.piece2 = bf16[272,256]{1,0:T(8,128)(2,1)S(1)} collective-permute-done((bf16[272,256]{1,0:T(8,128)(2,1)S(1)}, bf16[272,256]{1,0:T(8,128)(2,1)S(1)}, u32[]{:S(2)}, u32[]{:S(2)}) %collective-permute-start.17) | collective-permute-done | bytes 139296 | tf_op jit(solution)/shard_map/ppermute | solution.py:37
  272.6 5.9 %all-to-all-done.4.blocks = bf16[4,4,272,256]{3,2,1,0:T(8,128)(2,1)S(1)} async-done(((bf16[4,4,272,256]{3,2,1,0:T(8,128)(2,1)}), bf16[4,4,272,256]{3,2,1,0:T(8,128)(2,1)S(1)}, u32[]{:S(2)}, u32[]{:S(2)}) %all-to-all-start.4) | async-done | bytes 2228256 | tf_op jit(solution)/shard_map/all_to_all | solution.py:468
  280.2 4.9 %all-to-all-start.5 = ((bf16[4,272,256]{2,1,0:T(8,128)(2,1)}), bf16[4,272,256]{2,1,0:T(8,128)(2,1)S(1)}, u32[]{:S(2)}, u32[]{:S(2)}) async-start(bf16[4,272,256]{2,1,0:T(8,128)(2,1)} %shard_map.101), calls=%async_computation.5 | async-start | bytes 1114112 | tf_op jit(solution)/shard_map/all_to_all | solution.py:478
  285.2 13.7 %all-to-all-done.5.pieces = bf16[4,272,256]{2,1,0:T(8,128)(2,1)S(1)} async-done(((bf16[4,272,256]{2,1,0:T(8,128)(2,1)}), bf16[4,272,256]{2,1,0:T(8,128)(2,1)S(1)}, u32[]{:S(2)}, u32[]{:S(2)}) %all-to-all-start.5) | async-done | bytes 557088 | tf_op jit(solution)/shard_map/all_to_all | solution.py:478
  302.3 10.3 %all-to-all-start.6 = ((bf16[32,24,256]{2,1,0:T(8,128)(2,1)}), bf16[32,24,256]{2,1,0:T(8,128)(2,1)S(1)}, u32[]{:S(2)}, u32[]{:S(2)}) async-start(bf16[32,24,256]{2,1,0:T(8,128)(2,1)} %bitcast.38), calls=%async_computation.6 | async-start | bytes 786432 | tf_op jit(solution)/shard_map/all_to_all | solution.py:493
  316.5 2.1 collective-permute-start.20
  318.7 3.5 collective-permute-done.20
  322.1 4.0 %collective-permute-start.21 = (f32[12,256]{1,0:T(8,128)S(1)}, f32[12,256]{1,0:T(8,128)S(1)}, u32[]{:S(2)}, u32[]{:S(2)}) collective-permute-start(f32[12,256]{1,0:T(8,128)S(1)} %add.199), channel_id=1, source_target_pairs={{0,64},{32,96},{64,0},{96,32},{1,65},{33,97},{65,1},{97,33},{2,66}... | collective-permute-start | bytes 36872 | tf_op jit(solution)/shard_map/ppermute | solution.py:42
  326.1 3.2 collective-permute-done.21
  329.3 7.3 %collective-permute-start.22 = (f32[12,256]{1,0:T(8,128)S(1)}, f32[12,256]{1,0:T(8,128)S(1)}, u32[]{:S(2)}, u32[]{:S(2)}) collective-permute-start(f32[12,256]{1,0:T(8,128)S(1)} %add.200), channel_id=1, source_target_pairs={{0,128},{128,0},{256,384},{384,256},{1,129},{129,1},{257,385},{385... | collective-permute-start | bytes 36872 | tf_op jit(solution)/shard_map/ppermute | solution.py:42
  339.0 12.1 %collective-permute-start.23 = (f32[12,256]{1,0:T(8,128)S(1)}, f32[12,256]{1,0:T(8,128)S(1)}, u32[]{:S(2)}, u32[]{:S(2)}) collective-permute-start(f32[12,256]{1,0:T(8,128)S(1)} %add.201), channel_id=1, source_target_pairs={{0,256},{128,384},{256,0},{384,128},{1,257},{129,385},{257,1},{385... | collective-permute-start | bytes 36872 | tf_op jit(solution)/shard_map/ppermute | solution.py:42
  (114 shorter events, 48.4 us)
Async XLA Ops:
  7.2 6.2 %copy-start = (bf16[768,256]{1,0:T(8,128)(2,1)S(1)}, bf16[768,256]{1,0:T(8,128)(2,1)}, u32[]{:S(2)}) copy-start(bf16[768,256]{1,0:T(8,128)(2,1)} %param.7) | copy-start | bytes 1179652
  7.2 144.3 %all-gather.3.cloned.1.call-start = ((), (), s32[]{:S(2)}) async-start(), calls=%async_computation.7 | async-start | bytes 2646016 | tf_op jit(solution)/shard_map/all_gather | solution.py:366
  13.4 21.8 %copy-start.14 = (bf16[768,128]{1,0:T(8,128)(2,1)S(1)}, bf16[768,128]{1,0:T(8,128)(2,1)}, u32[]{:S(2)}) copy-start(bf16[768,128]{1,0:T(8,128)(2,1)} %param.11) | copy-start | bytes 589828
  13.4 21.9 %copy-start.13 = (bf16[128,768]{1,0:T(8,128)(2,1)S(1)}, bf16[128,768]{1,0:T(8,128)(2,1)}, u32[]{:S(2)}) copy-start(bf16[128,768]{1,0:T(8,128)(2,1)} %param.10) | copy-start | bytes 589828
  16.7 39.0 %copy-start.15 = (s32[32]{0:T(128)S(1)}, s32[32]{0:T(128)}, u32[]{:S(2)}) copy-start(s32[32]{0:T(128)} %param.8) | copy-start | bytes 388
  16.7 70.5 %all-to-all-start = ((bf16[32,24,256]{2,1,0:T(8,128)(2,1)}), bf16[32,24,256]{2,1,0:T(8,128)(2,1)S(1)}, u32[]{:S(2)}, u32[]{:S(2)}) async-start(bf16[32,24,256]{2,1,0:T(8,128)(2,1)} %bitcast.4), calls=%async_computation | async-start | bytes 786432 | tf_op jit(solution)/shard_map/all_to_all | solution.py:367
  35.4 36.6 %collective-permute-start.1 = (bf16[2,128,768]{2,1,0:T(8,128)(2,1)S(1)}, bf16[2,128,768]{2,1,0:T(8,128)(2,1)S(1)}, u32[]{:S(2)}, u32[]{:S(2)}) collective-permute-start(bf16[2,128,768]{2,1,0:T(8,128)(2,1)S(1)} %get-tuple-element.77), channel_id=1, source_target_pairs={{0,384},{128,0},{256,128},{384,256},{1,385},{129,1},{257,129},{385... | collective-permute-start | bytes 1179656 | tf_op jit(solution)/shard_map/ppermute | solution.py:37
  42.8 44.5 %collective-permute-start = (bf16[2,128,768]{2,1,0:T(8,128)(2,1)S(1)}, bf16[2,128,768]{2,1,0:T(8,128)(2,1)S(1)}, u32[]{:S(2)}, u32[]{:S(2)}) collective-permute-start(bf16[2,128,768]{2,1,0:T(8,128)(2,1)S(1)} %get-tuple-element.77), channel_id=1, source_target_pairs={{0,128},{128,256},{256,384},{384,0},{1,129},{129,257},{257,385},{3... | collective-permute-start | bytes 1179656 | tf_op jit(solution)/shard_map/ppermute | solution.py:37
  45.2 14.1 %collective-permute-start.4 = (bf16[1,2,128,768]{3,2,1,0:T(8,128)(2,1)S(1)}, bf16[1,2,128,768]{3,2,1,0:T(8,128)(2,1)S(1)}, u32[]{:S(2)}, u32[]{:S(2)}) collective-permute-start(bf16[1,2,128,768]{3,2,1,0:T(8,128)(2,1)S(1)} %get-tuple-element.76), channel_id=1, source_target_pairs={{0,96},{32,0},{64,32},{96,64},{1,97},{33,1},{65,33},{97,65},{2,98}... | collective-permute-start | bytes 1179656 | tf_op jit(solution)/shard_map/ppermute | solution.py:37
  47.3 20.8 %collective-permute-start.3 = (bf16[1,2,128,768]{3,2,1,0:T(8,128)(2,1)S(1)}, bf16[1,2,128,768]{3,2,1,0:T(8,128)(2,1)S(1)}, u32[]{:S(2)}, u32[]{:S(2)}) collective-permute-start(bf16[1,2,128,768]{3,2,1,0:T(8,128)(2,1)S(1)} %get-tuple-element.76), channel_id=1, source_target_pairs={{0,64},{32,96},{64,0},{96,32},{1,65},{33,97},{65,1},{97,33},{2,66}... | collective-permute-start | bytes 1179656 | tf_op jit(solution)/shard_map/ppermute | solution.py:37
  51.9 18.8 %collective-permute-start.2 = (bf16[1,2,128,768]{3,2,1,0:T(8,128)(2,1)S(1)}, bf16[1,2,128,768]{3,2,1,0:T(8,128)(2,1)S(1)}, u32[]{:S(2)}, u32[]{:S(2)}) collective-permute-start(bf16[1,2,128,768]{3,2,1,0:T(8,128)(2,1)S(1)} %get-tuple-element.76), channel_id=1, source_target_pairs={{0,32},{32,64},{64,96},{96,0},{1,33},{33,65},{65,97},{97,1},{2,34}... | collective-permute-start | bytes 1179656 | tf_op jit(solution)/shard_map/ppermute | solution.py:37
  89.2 62.2 %all-to-all-start.1 = ((bf16[4,256,256]{2,1,0:T(8,128)(2,1)}), bf16[4,256,256]{2,1,0:T(8,128)(2,1)S(1)}, u32[]{:S(2)}, u32[]{:S(2)}) async-start(bf16[4,256,256]{2,1,0:T(8,128)(2,1)} %broadcast_in_dim.33), calls=%async_computation.1 | async-start | bytes 1048576 | tf_op jit(solution)/shard_map/all_to_all | solution.py:51
  110.5 28.6 %collective-permute-start.8 = (bf16[2,2,128,768]{3,2,1,0:T(8,128)(2,1)S(1)}, bf16[2,2,128,768]{3,2,1,0:T(8,128)(2,1)S(1)}, u32[]{:S(2)}, u32[]{:S(2)}) collective-permute-start(bf16[2,2,128,768]{3,2,1,0:T(8,128)(2,1)S(1)} %get-tuple-element.70), channel_id=1, source_target_pairs={{0,64},{32,96},{64,0},{96,32},{1,65},{33,97},{65,1},{97,33},{2,66}... | collective-permute-start | bytes 2359304 | tf_op jit(solution)/shard_map/ppermute | solution.py:37
  114.7 34.9 %collective-permute-start.7 = (bf16[2,2,128,768]{3,2,1,0:T(8,128)(2,1)S(1)}, bf16[2,2,128,768]{3,2,1,0:T(8,128)(2,1)S(1)}, u32[]{:S(2)}, u32[]{:S(2)}) collective-permute-start(bf16[2,2,128,768]{3,2,1,0:T(8,128)(2,1)S(1)} %get-tuple-element.70), channel_id=1, source_target_pairs={{0,32},{32,64},{64,96},{96,0},{1,33},{33,65},{65,97},{97,1},{2,34}... | collective-permute-start | bytes 2359304 | tf_op jit(solution)/shard_map/ppermute | solution.py:37
  116.6 33.0 %collective-permute-start.9 = (bf16[2,2,128,768]{3,2,1,0:T(8,128)(2,1)S(1)}, bf16[2,2,128,768]{3,2,1,0:T(8,128)(2,1)S(1)}, u32[]{:S(2)}, u32[]{:S(2)}) collective-permute-start(bf16[2,2,128,768]{3,2,1,0:T(8,128)(2,1)S(1)} %get-tuple-element.70), channel_id=1, source_target_pairs={{0,96},{32,0},{64,32},{96,64},{1,97},{33,1},{65,33},{97,65},{2,98}... | collective-permute-start | bytes 2359304 | tf_op jit(solution)/shard_map/ppermute | solution.py:37
  120.6 12.8 %collective-permute-start.6 = (bf16[1,128,768]{2,1,0:T(8,128)(2,1)S(1)}, bf16[1,128,768]{2,1,0:T(8,128)(2,1)S(1)}, u32[]{:S(2)}, u32[]{:S(2)}) collective-permute-start(bf16[1,128,768]{2,1,0:T(8,128)(2,1)S(1)} %slice.43), channel_id=1, source_target_pairs={{0,384},{128,0},{256,128},{384,256},{1,385},{129,1},{257,129},{385... | collective-permute-start | bytes 589832 | tf_op jit(solution)/shard_map/ppermute | solution.py:37
  127.1 12.0 %collective-permute-start.5 = (bf16[1,128,768]{2,1,0:T(8,128)(2,1)S(1)}, bf16[1,128,768]{2,1,0:T(8,128)(2,1)S(1)}, u32[]{:S(2)}, u32[]{:S(2)}) collective-permute-start(bf16[1,128,768]{2,1,0:T(8,128)(2,1)S(1)} %slice.42), channel_id=1, source_target_pairs={{0,128},{128,256},{256,384},{384,0},{1,129},{129,257},{257,385},{3... | collective-permute-start | bytes 589832 | tf_op jit(solution)/shard_map/ppermute | solution.py:37
  151.5 37.2 %collective-permute-start.11 = (bf16[4,2,2,128,768]{4,3,2,1,0:T(8,128)(2,1)}, bf16[4,2,2,128,768]{4,3,2,1,0:T(8,128)(2,1)}, u32[]{:S(2)}, u32[]{:S(2)}) collective-permute-start(bf16[4,2,2,128,768]{4,3,2,1,0:T(8,128)(2,1)} %pad_maximum_fusion.part1.refs_1_), channel_id=1, source_target_pairs={{0,16},{16,0},{1,17},{17,1},{2,18},{18,2},{3,19},{19,3},{4,20},{20... | collective-permute-start | bytes 9437192 | tf_op jit(solution)/shard_map/ppermute | solution.py:37
  153.4 35.3 %collective-permute-start.10 = (bf16[4,1,2,128,768]{4,3,2,1,0:T(8,128)(2,1)}, bf16[4,1,2,128,768]{4,3,2,1,0:T(8,128)(2,1)}, u32[]{:S(2)}, u32[]{:S(2)}) collective-permute-start(bf16[4,1,2,128,768]{4,3,2,1,0:T(8,128)(2,1)} %pad_maximum_fusion.1.part0.refs_0_), channel_id=1, source_target_pairs={{0,16},{16,0},{1,17},{17,1},{2,18},{18,2},{3,19},{19,3},{4,20},{20... | collective-permute-start | bytes 4718600 | tf_op jit(solution)/shard_map/ppermute | solution.py:37
  157.3 4.9 %copy-start.17 = (s32[4]{0:T(128)S(1)}, s32[4]{0:T(128)}, u32[]{:S(2)}) copy-start(s32[4]{0:T(128)} %param.9) | copy-start | bytes 52
  157.3 31.4 %all-to-all-start.2 = ((bf16[4,4,256,256]{3,2,1,0:T(8,128)(2,1)}), bf16[4,4,256,256]{3,2,1,0:T(8,128)(2,1)S(1)}, u32[]{:S(2)}, u32[]{:S(2)}) async-start(bf16[4,4,256,256]{3,2,1,0:T(8,128)(2,1)} %broadcast_in_dim.34), calls=%async_computation.2 | async-start | bytes 4194304 | tf_op jit(solution)/shard_map/all_to_all | solution.py:51
  162.5 16.2 %collective-permute-start.14 = (bf16[1,2,128,768]{3,2,1,0:T(8,128)(2,1)S(1)}, bf16[1,2,128,768]{3,2,1,0:T(8,128)(2,1)S(1)}, u32[]{:S(2)}, u32[]{:S(2)}) collective-permute-start(bf16[1,2,128,768]{3,2,1,0:T(8,128)(2,1)S(1)} %bitcast.64), channel_id=1, source_target_pairs={{0,96},{32,0},{64,32},{96,64},{1,97},{33,1},{65,33},{97,65},{2,98}... | collective-permute-start | bytes 1179656 | tf_op jit(solution)/shard_map/ppermute | solution.py:37
  165.3 19.0 %collective-permute-start.13 = (bf16[1,2,128,768]{3,2,1,0:T(8,128)(2,1)S(1)}, bf16[1,2,128,768]{3,2,1,0:T(8,128)(2,1)S(1)}, u32[]{:S(2)}, u32[]{:S(2)}) collective-permute-start(bf16[1,2,128,768]{3,2,1,0:T(8,128)(2,1)S(1)} %bitcast.65), channel_id=1, source_target_pairs={{0,64},{32,96},{64,0},{96,32},{1,65},{33,97},{65,1},{97,33},{2,66}... | collective-permute-start | bytes 1179656 | tf_op jit(solution)/shard_map/ppermute | solution.py:37
  169.2 18.1 %collective-permute-start.12 = (bf16[1,2,128,768]{3,2,1,0:T(8,128)(2,1)S(1)}, bf16[1,2,128,768]{3,2,1,0:T(8,128)(2,1)S(1)}, u32[]{:S(2)}, u32[]{:S(2)}) collective-permute-start(bf16[1,2,128,768]{3,2,1,0:T(8,128)(2,1)S(1)} %bitcast.66), channel_id=1, source_target_pairs={{0,32},{32,64},{64,96},{96,0},{1,33},{33,65},{65,97},{97,1},{2,34}... | collective-permute-start | bytes 1179656 | tf_op jit(solution)/shard_map/ppermute | solution.py:37
  173.4 1.7 copy-start.5
  178.7 9.9 %copy-start.7 = (bf16[4,4,256,256]{3,2,1,0:T(8,128)(2,1)}, bf16[4,4,256,256]{3,2,1,0:T(8,128)(2,1)S(1)}, u32[]{:S(2)}) copy-start(bf16[4,4,256,256]{3,2,1,0:T(8,128)(2,1)S(1)} %get-tuple-element.45.scaled) | copy-start | bytes 6291460
  188.7 9.7 %collective-permute-start.15 = (bf16[4,1,2,128,768]{4,3,2,1,0:T(8,128)(2,1)}, bf16[4,1,2,128,768]{4,3,2,1,0:T(8,128)(2,1)S(1)}, u32[]{:S(2)}, u32[]{:S(2)}) collective-permute-start(bf16[4,1,2,128,768]{4,3,2,1,0:T(8,128)(2,1)} %pad_maximum_fusion.2.part2.refs_2_), channel_id=1, source_target_pairs={{0,16},{16,0},{1,17},{17,1},{2,18},{18,2},{3,19},{19,3},{4,20},{20... | collective-permute-start | bytes 4718600 | tf_op jit(solution)/shard_map/ppermute | solution.py:37
  190.6 8.9 %copy-start.3 = (bf16[4,1,2,128,768]{4,3,2,1,0:T(8,128)(2,1)S(1)}, bf16[4,1,2,128,768]{4,3,2,1,0:T(8,128)(2,1)}, u32[]{:S(2)}) copy-start(bf16[4,1,2,128,768]{4,3,2,1,0:T(8,128)(2,1)} %pad_maximum_fusion.2.part2.refs_2_) | copy-start | bytes 4718596
  195.7 1.4 copy-start.8
  198.3 1.2 copy-start.16
  214.5 31.5 %all-to-all-start.3 = ((bf16[4,4,256,256]{3,2,1,0:T(8,128)(2,1)}), bf16[4,4,256,256]{3,2,1,0:T(8,128)(2,1)S(1)}, u32[]{:S(2)}, u32[]{:S(2)}) async-start(bf16[4,4,256,256]{3,2,1,0:T(8,128)(2,1)} %shard_map.97), calls=%async_computation.3 | async-start | bytes 4194304 | tf_op jit(solution)/shard_map/all_to_all | solution.py:466
  219.0 1.4 copy-start.4
  246.0 1.4 copy-start.1
  247.4 31.2 %all-to-all-start.4 = ((bf16[4,4,272,256]{3,2,1,0:T(8,128)(2,1)}), bf16[4,4,272,256]{3,2,1,0:T(8,128)(2,1)S(1)}, u32[]{:S(2)}, u32[]{:S(2)}) async-start(bf16[4,4,272,256]{3,2,1,0:T(8,128)(2,1)} %shard_map.98), calls=%async_computation.4 | async-start | bytes 4456448 | tf_op jit(solution)/shard_map/all_to_all | solution.py:468
  251.0 1.8 copy-start.2
  254.7 10.4 %collective-permute-start.18 = (bf16[272,256]{1,0:T(8,128)(2,1)S(1)}, bf16[272,256]{1,0:T(8,128)(2,1)S(1)}, u32[]{:S(2)}, u32[]{:S(2)}) collective-permute-start(bf16[272,256]{1,0:T(8,128)(2,1)S(1)} %get-tuple-element.71), channel_id=1, source_target_pairs={{0,12},{4,0},{8,4},{12,8},{1,13},{5,1},{9,5},{13,9},{2,14},{6,2},{... | collective-permute-start | bytes 417800 | tf_op jit(solution)/shard_map/ppermute | solution.py:37
  260.2 12.5 %collective-permute-start.17 = (bf16[272,256]{1,0:T(8,128)(2,1)S(1)}, bf16[272,256]{1,0:T(8,128)(2,1)S(1)}, u32[]{:S(2)}, u32[]{:S(2)}) collective-permute-start(bf16[272,256]{1,0:T(8,128)(2,1)S(1)} %get-tuple-element.72), channel_id=1, source_target_pairs={{0,8},{4,12},{8,0},{12,4},{1,9},{5,13},{9,1},{13,5},{2,10},{6,14},... | collective-permute-start | bytes 417800 | tf_op jit(solution)/shard_map/ppermute | solution.py:37
  262.4 10.2 %collective-permute-start.16 = (bf16[272,256]{1,0:T(8,128)(2,1)S(1)}, bf16[272,256]{1,0:T(8,128)(2,1)}, u32[]{:S(2)}, u32[]{:S(2)}) collective-permute-start(bf16[272,256]{1,0:T(8,128)(2,1)S(1)} %get-tuple-element.73), channel_id=1, source_target_pairs={{0,4},{4,8},{8,12},{12,0},{1,5},{5,9},{9,13},{13,1},{2,6},{6,10},{... | collective-permute-start | bytes 417800 | tf_op jit(solution)/shard_map/ppermute | solution.py:37
  278.5 20.4 %copy-start.6 = (bf16[256,256]{1,0:T(8,128)(2,1)S(1)}, bf16[256,256]{1,0:T(8,128)(2,1)}, u32[]{:S(2)}) copy-start(bf16[256,256]{1,0:T(8,128)(2,1)} %grad.1) | copy-start | bytes 393220
  280.2 18.7 %all-to-all-start.5 = ((bf16[4,272,256]{2,1,0:T(8,128)(2,1)}), bf16[4,272,256]{2,1,0:T(8,128)(2,1)S(1)}, u32[]{:S(2)}, u32[]{:S(2)}) async-start(bf16[4,272,256]{2,1,0:T(8,128)(2,1)} %shard_map.101), calls=%async_computation.5 | async-start | bytes 1114112 | tf_op jit(solution)/shard_map/all_to_all | solution.py:478
  298.9 0.9 copy-start.10
  299.8 0.9 copy-start.12
  302.3 51.6 %all-to-all-start.6 = ((bf16[32,24,256]{2,1,0:T(8,128)(2,1)}), bf16[32,24,256]{2,1,0:T(8,128)(2,1)S(1)}, u32[]{:S(2)}, u32[]{:S(2)}) async-start(bf16[32,24,256]{2,1,0:T(8,128)(2,1)} %bitcast.38), calls=%async_computation.6 | async-start | bytes 786432 | tf_op jit(solution)/shard_map/all_to_all | solution.py:493
  313.4 3.1 collective-permute-start.19
  316.5 5.6 %collective-permute-start.20 = (f32[12,256]{1,0:T(8,128)S(1)}, f32[12,256]{1,0:T(8,128)S(1)}, u32[]{:S(2)}, u32[]{:S(2)}) collective-permute-start(f32[12,256]{1,0:T(8,128)S(1)} %fusion.10), channel_id=1, source_target_pairs={{0,32},{32,0},{64,96},{96,64},{1,33},{33,1},{65,97},{97,65},{2,34}... | collective-permute-start | bytes 36872 | tf_op jit(solution)/shard_map/ppermute | solution.py:42
  322.1 7.1 %collective-permute-start.21 = (f32[12,256]{1,0:T(8,128)S(1)}, f32[12,256]{1,0:T(8,128)S(1)}, u32[]{:S(2)}, u32[]{:S(2)}) collective-permute-start(f32[12,256]{1,0:T(8,128)S(1)} %add.199), channel_id=1, source_target_pairs={{0,64},{32,96},{64,0},{96,32},{1,65},{33,97},{65,1},{97,33},{2,66}... | collective-permute-start | bytes 36872 | tf_op jit(solution)/shard_map/ppermute | solution.py:42
  329.3 9.7 %collective-permute-start.22 = (f32[12,256]{1,0:T(8,128)S(1)}, f32[12,256]{1,0:T(8,128)S(1)}, u32[]{:S(2)}, u32[]{:S(2)}) collective-permute-start(f32[12,256]{1,0:T(8,128)S(1)} %add.200), channel_id=1, source_target_pairs={{0,128},{128,0},{256,384},{384,256},{1,129},{129,1},{257,385},{385... | collective-permute-start | bytes 36872 | tf_op jit(solution)/shard_map/ppermute | solution.py:42
  339.0 14.4 %collective-permute-start.23 = (f32[12,256]{1,0:T(8,128)S(1)}, f32[12,256]{1,0:T(8,128)S(1)}, u32[]{:S(2)}, u32[]{:S(2)}) collective-permute-start(f32[12,256]{1,0:T(8,128)S(1)} %add.201), channel_id=1, source_target_pairs={{0,256},{128,384},{256,0},{384,128},{1,257},{129,385},{257,1},{385... | collective-permute-start | bytes 36872 | tf_op jit(solution)/shard_map/ppermute | solution.py:42
  (2 other events, 1.3 us)
Sparse Core Ops, SparseCore 0:
  10.1 131.1 all-gather.2

commit v4 on v3

--- a/solution.py
+++ b/solution.py
@@ -311,6 +311,18 @@
     out[...] = (rows[...].astype(jnp.float32) + gate * branch).astype(jnp.bfloat16)
 
 
+def send_kernel(position, live_rows, values, out):
+    groups = live_rows.shape[0]
+    slots = values.shape[0] // groups
+    start = jnp.int32(0)
+    for i in range(groups):
+        start = start + jnp.where(i < position[0], live_rows[i], 0)
+    row = lax.broadcasted_iota(jnp.int32, (values.shape[0], 1), 0)
+    device = (row * (65536 // slots + 1)) >> 16
+    index = ((device - start) & (groups - 1)) + groups * (row - slots * device)
+    out[...] = picked(index, values[...])
+
+
 def pick_kernel(index, values, out):
     out[...] = picked(index[...], values[...])
 
@@ -361,8 +373,11 @@
     own_start = jnp.sum(jnp.where(device_ids < position, live_rows, 0))
     own_live = jnp.sum(jnp.where(device_ids == position, live_rows, 0))
     slot_ids = jnp.arange(per_pair, dtype=jnp.int32)[None, :]
-    local_rows = ((device_ids[:, None] - own_start) & low) + groups * slot_ids
-    outgoing = hidden_in[local_rows.reshape(-1)].reshape(groups, per_pair, width_local)
+    (outgoing,) = call(
+        send_kernel, (shape((slots_in, width_local), bf16),), [], 2 * US, 0,
+        position.astype(jnp.int32).reshape(1), live_rows, hidden_in,
+    )
+    outgoing = outgoing.reshape(groups, per_pair, width_local)
     gathered = lax.all_gather(payload, TP, axis=0)
     incoming = lax.all_to_all(outgoing, DP, split_axis=0, concat_axis=0, tiled=True)
     global_rows = position + groups * jnp.arange(balanced, dtype=jnp.int32)

time: 364 us -> 361 us (level)
  local copies, waits for them, and re-layouts: 21.9 us -> 15.7 us
  starting transfers between devices: 163 us -> 169 us
    ppermute x19, waiting for transfers between devices: 65.4 us -> 55.8 us  [shifted(): lax.ppermute(value, axis, [(i, (i + step) % size) for i in range(size)])]
    all_to_all x2, starting transfers between devices: 26 us -> 32.7 us  [spread(): return lax.all_to_all(copies, axis, split_axis=0, concat_axis=0, tiled=True)]
    all_gather x1, waiting for transfers between devices: 0.01 us -> 5.34 us  [body(): gathered = lax.all_gather(payload, TP, axis=0)]
    unnamed x37 -> x31, local copies, waits for them, and re-layouts: 10.7 us -> 9.26 us
    pallas_call x7 -> x8, Pallas kernels: 17 us -> 17.8 us  [call(): pl.pallas_call(kernel, out_shape=outs, in_specs=[SMEM_SPEC if a.ndim == 1...]
  transfers between devices with their start and end apart: 32 -> 32, of which waited for: 18 -> 21; matrix products, arithmetic and copies ran while one was open for 6% -> 4% of each run, Pallas kernels for 5% -> 5%
where the time goes in v4:
time: 361 us; the launch traced here: 360 us
  starting transfers between devices  169 us (47%)
  waiting for transfers between devices  112 us (31%)
  Pallas kernels  39 us (11%)
  local copies, waits for them, and re-layouts  15.7 us (4%)
  between operations  14.6 us (4%)
  other arithmetic  9.93 us (3%)
    ppermute x19, starting transfers between devices, shifted(): lax.ppermute(value, axis, [(i, (i + step) % size) for i in range(size)])  65 us
    ppermute x19, waiting for transfers between devices, shifted(): lax.ppermute(value, axis, [(i, (i + step) % size) for i in range(size)])  55.8 us
    all_to_all x2, starting transfers between devices, spread(): return lax.all_to_all(copies, axis, split_axis=0, concat_axis=0, tiled=True)  32.7 us
    ppermute x5, starting transfers between devices, crossed(): return lax.ppermute(value, axis, [(i, i ^ mask) for i in range(size)])  27.5 us
    all_to_all x1, waiting for transfers between devices, body(): lax.all_to_all(partial_out, 'x', split_axis=0, concat_axis=0, tiled=True)  19.4 us
    all_to_all x1, starting transfers between devices, body(): lax.all_to_all(outgoing, DP, split_axis=0, concat_axis=0, tiled=True)  18.3 us
    pallas_call x8, Pallas kernels, call(): pl.pallas_call(kernel, out_shape=outs, in_specs=[SMEM_SPEC if a.ndim == 1...  17.8 us
    all_to_all x1, starting transfers between devices, body(): lax.all_to_all(returning, DP, split_axis=0, concat_axis=0, tiled=True)  13.5 us
  transfers between devices with their start and end apart: 32, of which 21 were waited for; matrix products, arithmetic and copies ran while one was open for 4% of the time, Pallas kernels for 5%

profile of v4, /device:TPU:8, one launch (start us, length us, event | category | flops | bytes accessed | tf_op | source)
XLA Modules:
  0.0 359.7 jit_solution(4927243364427262372)
XLA Ops:
  13.0 18.3 %all-to-all-start = ((bf16[32,24,256]{2,1,0:T(8,128)(2,1)}), bf16[32,24,256]{2,1,0:T(8,128)(2,1)S(1)}, u32[]{:S(2)}, u32[]{:S(2)}) async-start(bf16[32,24,256]{2,1,0:T(8,128)(2,1)} %bitcast.5), calls=%async_computation | async-start | bytes 786432 | tf_op jit(solution)/shard_map/all_to_all | solution.py:382
  32.3 7.3 %collective-permute-start.1 = (bf16[2,128,768]{2,1,0:T(8,128)(2,1)S(1)}, bf16[2,128,768]{2,1,0:T(8,128)(2,1)S(1)}, u32[]{:S(2)}, u32[]{:S(2)}) collective-permute-start(bf16[2,128,768]{2,1,0:T(8,128)(2,1)S(1)} %get-tuple-element.77), channel_id=1, source_target_pairs={{0,384},{128,0},{256,128},{384,256},{1,385},{129,1},{257,129},{385... | collective-permute-start | bytes 1179656 | tf_op jit(solution)/shard_map/ppermute | solution.py:37
  39.7 2.4 collective-permute-start
  42.1 2.1 collective-permute-start.4
  44.2 4.6 %collective-permute-start.3 = (bf16[1,2,128,768]{3,2,1,0:T(8,128)(2,1)}, bf16[1,2,128,768]{3,2,1,0:T(8,128)(2,1)S(1)}, u32[]{:S(2)}, u32[]{:S(2)}) collective-permute-start(bf16[1,2,128,768]{3,2,1,0:T(8,128)(2,1)} %get-tuple-element.76), channel_id=1, source_target_pairs={{0,64},{32,96},{64,0},{96,32},{1,65},{33,97},{65,1},{97,33},{2,66}... | collective-permute-start | bytes 1179656 | tf_op jit(solution)/shard_map/ppermute | solution.py:37
  48.8 3.7 %collective-permute-start.2 = (bf16[1,2,128,768]{3,2,1,0:T(8,128)(2,1)}, bf16[1,2,128,768]{3,2,1,0:T(8,128)(2,1)S(1)}, u32[]{:S(2)}, u32[]{:S(2)}) collective-permute-start(bf16[1,2,128,768]{3,2,1,0:T(8,128)(2,1)} %get-tuple-element.76), channel_id=1, source_target_pairs={{0,32},{32,64},{64,96},{96,0},{1,33},{33,65},{65,97},{97,1},{2,34}... | collective-permute-start | bytes 1179656 | tf_op jit(solution)/shard_map/ppermute | solution.py:37
  52.9 3.6 collective-permute-done.4
  56.5 8.5 %collective-permute-done.3 = bf16[1,2,128,768]{3,2,1,0:T(8,128)(2,1)S(1)} collective-permute-done((bf16[1,2,128,768]{3,2,1,0:T(8,128)(2,1)}, bf16[1,2,128,768]{3,2,1,0:T(8,128)(2,1)S(1)}, u32[]{:S(2)}, u32[]{:S(2)}) %collective-permute-start.3) | collective-permute-done | bytes 393248 | tf_op jit(solution)/shard_map/ppermute | solution.py:37
  65.0 2.4 collective-permute-done.2
  68.7 4.8 %collective-permute-done = bf16[2,128,768]{2,1,0:T(8,128)(2,1)S(1)} collective-permute-done((bf16[2,128,768]{2,1,0:T(8,128)(2,1)S(1)}, bf16[2,128,768]{2,1,0:T(8,128)(2,1)S(1)}, u32[]{:S(2)}, u32[]{:S(2)}) %collective-permute-start) | collective-permute-done | bytes 393248 | tf_op jit(solution)/shard_map/ppermute | solution.py:37
  75.5 28.9 %all-to-all-start.1 = ((bf16[4,256,256]{2,1,0:T(8,128)(2,1)}), bf16[4,256,256]{2,1,0:T(8,128)(2,1)S(1)}, u32[]{:S(2)}, u32[]{:S(2)}) async-start(bf16[4,256,256]{2,1,0:T(8,128)(2,1)} %broadcast_in_dim.32), calls=%async_computation.1 | async-start | bytes 1048576 | tf_op jit(solution)/shard_map/all_to_all | solution.py:51
  104.5 6.1 %collective-permute-start.8 = (bf16[2,2,128,768]{3,2,1,0:T(8,128)(2,1)S(1)}, bf16[2,2,128,768]{3,2,1,0:T(8,128)(2,1)S(1)}, u32[]{:S(2)}, u32[]{:S(2)}) collective-permute-start(bf16[2,2,128,768]{3,2,1,0:T(8,128)(2,1)S(1)} %get-tuple-element.70), channel_id=1, source_target_pairs={{0,64},{32,96},{64,0},{96,32},{1,65},{33,97},{65,1},{97,33},{2,66}... | collective-permute-start | bytes 2359304 | tf_op jit(solution)/shard_map/ppermute | solution.py:37
  110.6 1.9 collective-permute-start.7
  112.5 3.9 %collective-permute-start.9 = (bf16[2,2,128,768]{3,2,1,0:T(8,128)(2,1)S(1)}, bf16[2,2,128,768]{3,2,1,0:T(8,128)(2,1)S(1)}, u32[]{:S(2)}, u32[]{:S(2)}) collective-permute-start(bf16[2,2,128,768]{3,2,1,0:T(8,128)(2,1)S(1)} %get-tuple-element.70), channel_id=1, source_target_pairs={{0,96},{32,0},{64,32},{96,64},{1,97},{33,1},{65,33},{97,65},{2,98}... | collective-permute-start | bytes 2359304 | tf_op jit(solution)/shard_map/ppermute | solution.py:37
  116.5 5.2 %collective-permute-start.6 = (bf16[1,128,768]{2,1,0:T(8,128)(2,1)S(1)}, bf16[1,128,768]{2,1,0:T(8,128)(2,1)S(1)}, u32[]{:S(2)}, u32[]{:S(2)}) collective-permute-start(bf16[1,128,768]{2,1,0:T(8,128)(2,1)S(1)} %slice.43), channel_id=1, source_target_pairs={{0,384},{128,0},{256,128},{384,256},{1,385},{129,1},{257,129},{385... | collective-permute-start | bytes 589832 | tf_op jit(solution)/shard_map/ppermute | solution.py:37
  121.7 4.6 %collective-permute-start.5 = (bf16[1,128,768]{2,1,0:T(8,128)(2,1)S(1)}, bf16[1,128,768]{2,1,0:T(8,128)(2,1)S(1)}, u32[]{:S(2)}, u32[]{:S(2)}) collective-permute-start(bf16[1,128,768]{2,1,0:T(8,128)(2,1)S(1)} %slice.42), channel_id=1, source_target_pairs={{0,128},{128,256},{256,384},{384,0},{1,129},{129,257},{257,385},{3... | collective-permute-start | bytes 589832 | tf_op jit(solution)/shard_map/ppermute | solution.py:37
  128.1 15.4 %collective-permute-done.5 = bf16[1,128,768]{2,1,0:T(8,128)(2,1)S(1)} collective-permute-done((bf16[1,128,768]{2,1,0:T(8,128)(2,1)S(1)}, bf16[1,128,768]{2,1,0:T(8,128)(2,1)S(1)}, u32[]{:S(2)}, u32[]{:S(2)}) %collective-permute-start.5) | collective-permute-done | bytes 196640 | tf_op jit(solution)/shard_map/ppermute | solution.py:37
  146.4 5.3 %all-gather.3.cloned.1.call-done = bf16[4864,256]{1,0:T(8,128)(2,1)} async-done(((bf16[304,256]{1,0:T(8,128)(2,1)}), bf16[4864,256]{1,0:T(8,128)(2,1)}) %all-gather.3.cloned.1.call-update) | async-done | bytes 2490384 | tf_op jit(solution)/shard_map/all_gather | solution.py:381
  153.6 2.4 collective-permute-start.10
  157.6 3.7 %all-to-all-start.2 = ((bf16[4,4,256,256]{3,2,1,0:T(8,128)(2,1)}), bf16[4,4,256,256]{3,2,1,0:T(8,128)(2,1)S(1)}, u32[]{:S(2)}, u32[]{:S(2)}) async-start(bf16[4,4,256,256]{3,2,1,0:T(8,128)(2,1)} %broadcast_in_dim.33), calls=%async_computation.2 | async-start | bytes 4194304 | tf_op jit(solution)/shard_map/all_to_all | solution.py:51
  161.6 1.9 collective-permute-start.14
  163.6 4.2 %collective-permute-start.13 = (bf16[1,2,128,768]{3,2,1,0:T(8,128)(2,1)S(1)}, bf16[1,2,128,768]{3,2,1,0:T(8,128)(2,1)S(1)}, u32[]{:S(2)}, u32[]{:S(2)}) collective-permute-start(bf16[1,2,128,768]{3,2,1,0:T(8,128)(2,1)S(1)} %bitcast.67), channel_id=1, source_target_pairs={{0,64},{32,96},{64,0},{96,32},{1,65},{33,97},{65,1},{97,33},{2,66}... | collective-permute-start | bytes 1179656 | tf_op jit(solution)/shard_map/ppermute | solution.py:37
  167.8 1.9 collective-permute-start.12
  171.5 3.6 %shard_map.95 = (bf16[4,4,256,256]{3,2,1,0:T(8,128)(2,1)S(1)}, f32[16,16,256]{2,1,0:T(8,128)S(1)}) custom-call(s32[4]{0:T(128)S(1)} %pad_add_fusion.place, bf16[16,304,256]{2,1,0:T(8,128)(2,1)S(1)} %bitcast.63, f32[256,4]{1,0:T(8,128)S(1)} %and_convert_fusion.member), custom_call_target="tpu_custom_call" | custom-call | flops 4000000000 | tf_op jit(solution)/shard_map/pallas_call | solution.py:335
  175.2 8.1 %collective-permute-done.13 = bf16[1,2,128,768]{3,2,1,0:T(8,128)(2,1)S(1)} collective-permute-done((bf16[1,2,128,768]{3,2,1,0:T(8,128)(2,1)S(1)}, bf16[1,2,128,768]{3,2,1,0:T(8,128)(2,1)S(1)}, u32[]{:S(2)}, u32[]{:S(2)}) %collective-permute-start.13) | collective-permute-done | bytes 393248 | tf_op jit(solution)/shard_map/ppermute | solution.py:37
  183.3 3.5 collective-permute-done.12
  190.0 5.0 %shard_map.96 = (bf16[4,4,272,256]{3,2,1,0:T(8,128)(2,1)S(1)}, f32[256,1]{1,0:T(8,128)S(1)}, f32[256,1]{1,0:T(8,128)S(1)}) custom-call(s32[4]{0:T(128)S(1)} %pad_add_fusion.place, bf16[4,4,256,256]{3,2,1,0:T(8,128)(2,1)S(1)} %all-to-all-done.2.rows, f32[16,16,256]{2,1,0:T(8,128)S(1)} %get-tuple-element.43.table_in, f32[256,4]{1,0:T(8,128)S(1)} %and_convert_fusion.member), custom_call_target="tpu_custom_call" | custom-call | flops 6000000000 | tf_op jit(solution)/shard_map/pallas_call | solution.py:335
  197.6 8.9 %shard_map.97 = (bf16[768,256]{1,0:T(8,128)(2,1)S(1)}, bf16[768,256]{1,0:T(8,128)(2,1)S(1)}, bf16[16,256]{1,0:T(8,128)(2,1)S(1)}) custom-call(bf16[4,4,272,256]{3,2,1,0:T(8,128)(2,1)} %copy-done.10, bf16[4,4,256,256]{3,2,1,0:T(8,128)(2,1)} %copy-done.9, f32[256,4]{1,0:T(8,128)S(1)} %and_convert_fusion.member, ...), custom_call_target="tpu_custom_call" | custom-call | flops 8000000000 | tf_op jit(solution)/shard_map/pallas_call | solution.py:438
  206.5 6.1 %shard_map.98 = bf16[4,4,256,256]{3,2,1,0:T(8,128)(2,1)} custom-call(s32[4]{0:T(128)S(1)} %pad_add_fusion.place, bf16[768,256]{1,0:T(8,128)(2,1)S(1)} %get-tuple-element.49.hidden, bf16[4,1,2,128,768]{4,3,2,1,0:T(8,128)(2,1)} %pad_maximum_fusion.1.part0.refs_0_, bf16[4,2,2,128,768]{4,3,2,1,0:T(8,128)(2,1)} %pad_maximum_fusion.part1.refs_1_, ...), custom_call_target="tpu_custom_call" | custom-call | flops 5000000000 | tf_op jit(solution)/shard_map/pallas_call | solution.py:461
  212.7 4.5 %all-to-all-start.3 = ((bf16[4,4,256,256]{3,2,1,0:T(8,128)(2,1)}), bf16[4,4,256,256]{3,2,1,0:T(8,128)(2,1)S(1)}, u32[]{:S(2)}, u32[]{:S(2)}) async-start(bf16[4,4,256,256]{3,2,1,0:T(8,128)(2,1)} %shard_map.98), calls=%async_computation.3 | async-start | bytes 4194304 | tf_op jit(solution)/shard_map/all_to_all | solution.py:481
  218.5 6.1 %shard_map.99 = bf16[4,4,272,256]{3,2,1,0:T(8,128)(2,1)} custom-call(s32[4]{0:T(128)S(1)} %pad_add_fusion.place, bf16[768,256]{1,0:T(8,128)(2,1)S(1)} %get-tuple-element.50.hidden, bf16[4,1,2,128,768]{4,3,2,1,0:T(8,128)(2,1)} %pad_maximum_fusion.1.part0.refs_0_, bf16[4,2,2,128,768]{4,3,2,1,0:T(8,128)(2,1)} %pad_maximum_fusion.part1.refs_1_, ...), custom_call_target="tpu_custom_call" | custom-call | flops 5000000000 | tf_op jit(solution)/shard_map/pallas_call | solution.py:461
  224.7 19.4 %all-to-all-done.3.blocks = bf16[4,4,256,256]{3,2,1,0:T(8,128)(2,1)S(1)} async-done(((bf16[4,4,256,256]{3,2,1,0:T(8,128)(2,1)}), bf16[4,4,256,256]{3,2,1,0:T(8,128)(2,1)S(1)}, u32[]{:S(2)}, u32[]{:S(2)}) %all-to-all-start.3) | async-done | bytes 2097184 | tf_op jit(solution)/shard_map/all_to_all | solution.py:481
  245.5 3.6 %all-to-all-start.4 = ((bf16[4,4,272,256]{3,2,1,0:T(8,128)(2,1)}), bf16[4,4,272,256]{3,2,1,0:T(8,128)(2,1)S(1)}, u32[]{:S(2)}, u32[]{:S(2)}) async-start(bf16[4,4,272,256]{3,2,1,0:T(8,128)(2,1)} %shard_map.99), calls=%async_computation.4 | async-start | bytes 4456448 | tf_op jit(solution)/shard_map/all_to_all | solution.py:483
  252.7 1.9 collective-permute-start.18
  254.7 3.0 collective-permute-start.17
  257.7 3.9 %collective-permute-start.16 = (bf16[272,256]{1,0:T(8,128)(2,1)S(1)}, bf16[272,256]{1,0:T(8,128)(2,1)S(1)}, u32[]{:S(2)}, u32[]{:S(2)}) collective-permute-start(bf16[272,256]{1,0:T(8,128)(2,1)S(1)} %get-tuple-element.73), channel_id=1, source_target_pairs={{0,4},{4,8},{8,12},{12,0},{1,5},{5,9},{9,13},{13,1},{2,6},{6,10},{... | collective-permute-start | bytes 417800 | tf_op jit(solution)/shard_map/ppermute | solution.py:37
  261.7 6.8 %collective-permute-done.17.piece2 = bf16[272,256]{1,0:T(8,128)(2,1)S(1)} collective-permute-done((bf16[272,256]{1,0:T(8,128)(2,1)S(1)}, bf16[272,256]{1,0:T(8,128)(2,1)S(1)}, u32[]{:S(2)}, u32[]{:S(2)}) %collective-permute-start.17) | collective-permute-done | bytes 139296 | tf_op jit(solution)/shard_map/ppermute | solution.py:37
  268.5 8.2 %all-to-all-done.4.blocks = bf16[4,4,272,256]{3,2,1,0:T(8,128)(2,1)S(1)} async-done(((bf16[4,4,272,256]{3,2,1,0:T(8,128)(2,1)}), bf16[4,4,272,256]{3,2,1,0:T(8,128)(2,1)S(1)}, u32[]{:S(2)}, u32[]{:S(2)}) %all-to-all-start.4) | async-done | bytes 2228256 | tf_op jit(solution)/shard_map/all_to_all | solution.py:483
  278.3 3.7 %all-to-all-start.5 = ((bf16[4,272,256]{2,1,0:T(8,128)(2,1)}), bf16[4,272,256]{2,1,0:T(8,128)(2,1)S(1)}, u32[]{:S(2)}, u32[]{:S(2)}) async-start(bf16[4,272,256]{2,1,0:T(8,128)(2,1)} %shard_map.102), calls=%async_computation.5 | async-start | bytes 1114112 | tf_op jit(solution)/shard_map/all_to_all | solution.py:493
  282.9 13.0 %all-to-all-done.5.pieces = bf16[4,272,256]{2,1,0:T(8,128)(2,1)S(1)} async-done(((bf16[4,272,256]{2,1,0:T(8,128)(2,1)}), bf16[4,272,256]{2,1,0:T(8,128)(2,1)S(1)}, u32[]{:S(2)}, u32[]{:S(2)}) %all-to-all-start.5) | async-done | bytes 557088 | tf_op jit(solution)/shard_map/all_to_all | solution.py:493
  297.5 13.5 %all-to-all-start.6 = ((bf16[32,24,256]{2,1,0:T(8,128)(2,1)}), bf16[32,24,256]{2,1,0:T(8,128)(2,1)S(1)}, u32[]{:S(2)}, u32[]{:S(2)}) async-start(bf16[32,24,256]{2,1,0:T(8,128)(2,1)} %bitcast.39), calls=%async_computation.6 | async-start | bytes 786432 | tf_op jit(solution)/shard_map/all_to_all | solution.py:508
  311.0 2.1 collective-permute-start.19
  314.1 2.1 collective-permute-start.20
  316.3 3.5 collective-permute-done.20
  319.8 4.0 %collective-permute-start.21 = (f32[12,256]{1,0:T(8,128)S(1)}, f32[12,256]{1,0:T(8,128)S(1)}, u32[]{:S(2)}, u32[]{:S(2)}) collective-permute-start(f32[12,256]{1,0:T(8,128)S(1)} %add.157), channel_id=1, source_target_pairs={{0,64},{32,96},{64,0},{96,32},{1,65},{33,97},{65,1},{97,33},{2,66}... | collective-permute-start | bytes 36872 | tf_op jit(solution)/shard_map/ppermute | solution.py:42
  323.7 3.2 collective-permute-done.21
  326.9 7.2 %collective-permute-start.22 = (f32[12,256]{1,0:T(8,128)S(1)}, f32[12,256]{1,0:T(8,128)S(1)}, u32[]{:S(2)}, u32[]{:S(2)}) collective-permute-start(f32[12,256]{1,0:T(8,128)S(1)} %add.158), channel_id=1, source_target_pairs={{0,128},{128,0},{256,384},{384,256},{1,129},{129,1},{257,385},{385... | collective-permute-start | bytes 36872 | tf_op jit(solution)/shard_map/ppermute | solution.py:42
  336.5 12.2 %collective-permute-start.23 = (f32[12,256]{1,0:T(8,128)S(1)}, f32[12,256]{1,0:T(8,128)S(1)}, u32[]{:S(2)}, u32[]{:S(2)}) collective-permute-start(f32[12,256]{1,0:T(8,128)S(1)} %add.159), channel_id=1, source_target_pairs={{0,256},{128,384},{256,0},{384,128},{1,257},{129,385},{257,1},{385... | collective-permute-start | bytes 36872 | tf_op jit(solution)/shard_map/ppermute | solution.py:42
  (104 shorter events, 44.9 us)
Async XLA Ops:
  7.2 144.6 %all-gather.3.cloned.1.call-start = ((), (), s32[]{:S(2)}) async-start(), calls=%async_computation.7 | async-start | bytes 2646016 | tf_op jit(solution)/shard_map/all_gather | solution.py:381
  9.6 0.7 copy-start.6
  10.2 1.0 copy-start.8
  11.2 20.1 %copy-start.12 = (bf16[768,128]{1,0:T(8,128)(2,1)S(1)}, bf16[768,128]{1,0:T(8,128)(2,1)}, u32[]{:S(2)}) copy-start(bf16[768,128]{1,0:T(8,128)(2,1)} %param.11) | copy-start | bytes 589828
  11.2 20.3 %copy-start.11 = (bf16[128,768]{1,0:T(8,128)(2,1)S(1)}, bf16[128,768]{1,0:T(8,128)(2,1)}, u32[]{:S(2)}) copy-start(bf16[128,768]{1,0:T(8,128)(2,1)} %param.10) | copy-start | bytes 589828
  13.0 60.5 %all-to-all-start = ((bf16[32,24,256]{2,1,0:T(8,128)(2,1)}), bf16[32,24,256]{2,1,0:T(8,128)(2,1)S(1)}, u32[]{:S(2)}, u32[]{:S(2)}) async-start(bf16[32,24,256]{2,1,0:T(8,128)(2,1)} %bitcast.5), calls=%async_computation | async-start | bytes 786432 | tf_op jit(solution)/shard_map/all_to_all | solution.py:382
  32.3 36.4 %collective-permute-start.1 = (bf16[2,128,768]{2,1,0:T(8,128)(2,1)S(1)}, bf16[2,128,768]{2,1,0:T(8,128)(2,1)S(1)}, u32[]{:S(2)}, u32[]{:S(2)}) collective-permute-start(bf16[2,128,768]{2,1,0:T(8,128)(2,1)S(1)} %get-tuple-element.77), channel_id=1, source_target_pairs={{0,384},{128,0},{256,128},{384,256},{1,385},{129,1},{257,129},{385... | collective-permute-start | bytes 1179656 | tf_op jit(solution)/shard_map/ppermute | solution.py:37
  39.7 33.8 %collective-permute-start = (bf16[2,128,768]{2,1,0:T(8,128)(2,1)S(1)}, bf16[2,128,768]{2,1,0:T(8,128)(2,1)S(1)}, u32[]{:S(2)}, u32[]{:S(2)}) collective-permute-start(bf16[2,128,768]{2,1,0:T(8,128)(2,1)S(1)} %get-tuple-element.77), channel_id=1, source_target_pairs={{0,128},{128,256},{256,384},{384,0},{1,129},{129,257},{257,385},{3... | collective-permute-start | bytes 1179656 | tf_op jit(solution)/shard_map/ppermute | solution.py:37
  42.1 14.4 %collective-permute-start.4 = (bf16[1,2,128,768]{3,2,1,0:T(8,128)(2,1)}, bf16[1,2,128,768]{3,2,1,0:T(8,128)(2,1)S(1)}, u32[]{:S(2)}, u32[]{:S(2)}) collective-permute-start(bf16[1,2,128,768]{3,2,1,0:T(8,128)(2,1)} %get-tuple-element.76), channel_id=1, source_target_pairs={{0,96},{32,0},{64,32},{96,64},{1,97},{33,1},{65,33},{97,65},{2,98}... | collective-permute-start | bytes 1179656 | tf_op jit(solution)/shard_map/ppermute | solution.py:37
  44.2 20.8 %collective-permute-start.3 = (bf16[1,2,128,768]{3,2,1,0:T(8,128)(2,1)}, bf16[1,2,128,768]{3,2,1,0:T(8,128)(2,1)S(1)}, u32[]{:S(2)}, u32[]{:S(2)}) collective-permute-start(bf16[1,2,128,768]{3,2,1,0:T(8,128)(2,1)} %get-tuple-element.76), channel_id=1, source_target_pairs={{0,64},{32,96},{64,0},{96,32},{1,65},{33,97},{65,1},{97,33},{2,66}... | collective-permute-start | bytes 1179656 | tf_op jit(solution)/shard_map/ppermute | solution.py:37
  48.8 18.5 %collective-permute-start.2 = (bf16[1,2,128,768]{3,2,1,0:T(8,128)(2,1)}, bf16[1,2,128,768]{3,2,1,0:T(8,128)(2,1)S(1)}, u32[]{:S(2)}, u32[]{:S(2)}) collective-permute-start(bf16[1,2,128,768]{3,2,1,0:T(8,128)(2,1)} %get-tuple-element.76), channel_id=1, source_target_pairs={{0,32},{32,64},{64,96},{96,0},{1,33},{33,65},{65,97},{97,1},{2,34}... | collective-permute-start | bytes 1179656 | tf_op jit(solution)/shard_map/ppermute | solution.py:37
  75.5 70.9 %all-to-all-start.1 = ((bf16[4,256,256]{2,1,0:T(8,128)(2,1)}), bf16[4,256,256]{2,1,0:T(8,128)(2,1)S(1)}, u32[]{:S(2)}, u32[]{:S(2)}) async-start(bf16[4,256,256]{2,1,0:T(8,128)(2,1)} %broadcast_in_dim.32), calls=%async_computation.1 | async-start | bytes 1048576 | tf_op jit(solution)/shard_map/all_to_all | solution.py:51
  104.5 39.1 %collective-permute-start.8 = (bf16[2,2,128,768]{3,2,1,0:T(8,128)(2,1)S(1)}, bf16[2,2,128,768]{3,2,1,0:T(8,128)(2,1)S(1)}, u32[]{:S(2)}, u32[]{:S(2)}) collective-permute-start(bf16[2,2,128,768]{3,2,1,0:T(8,128)(2,1)S(1)} %get-tuple-element.70), channel_id=1, source_target_pairs={{0,64},{32,96},{64,0},{96,32},{1,65},{33,97},{65,1},{97,33},{2,66}... | collective-permute-start | bytes 2359304 | tf_op jit(solution)/shard_map/ppermute | solution.py:37
  110.6 33.2 %collective-permute-start.7 = (bf16[2,2,128,768]{3,2,1,0:T(8,128)(2,1)S(1)}, bf16[2,2,128,768]{3,2,1,0:T(8,128)(2,1)S(1)}, u32[]{:S(2)}, u32[]{:S(2)}) collective-permute-start(bf16[2,2,128,768]{3,2,1,0:T(8,128)(2,1)S(1)} %get-tuple-element.70), channel_id=1, source_target_pairs={{0,32},{32,64},{64,96},{96,0},{1,33},{33,65},{65,97},{97,1},{2,34}... | collective-permute-start | bytes 2359304 | tf_op jit(solution)/shard_map/ppermute | solution.py:37
  112.5 32.0 %collective-permute-start.9 = (bf16[2,2,128,768]{3,2,1,0:T(8,128)(2,1)S(1)}, bf16[2,2,128,768]{3,2,1,0:T(8,128)(2,1)S(1)}, u32[]{:S(2)}, u32[]{:S(2)}) collective-permute-start(bf16[2,2,128,768]{3,2,1,0:T(8,128)(2,1)S(1)} %get-tuple-element.70), channel_id=1, source_target_pairs={{0,96},{32,0},{64,32},{96,64},{1,97},{33,1},{65,33},{97,65},{2,98}... | collective-permute-start | bytes 2359304 | tf_op jit(solution)/shard_map/ppermute | solution.py:37
  116.5 11.6 %collective-permute-start.6 = (bf16[1,128,768]{2,1,0:T(8,128)(2,1)S(1)}, bf16[1,128,768]{2,1,0:T(8,128)(2,1)S(1)}, u32[]{:S(2)}, u32[]{:S(2)}) collective-permute-start(bf16[1,128,768]{2,1,0:T(8,128)(2,1)S(1)} %slice.43), channel_id=1, source_target_pairs={{0,384},{128,0},{256,128},{384,256},{1,385},{129,1},{257,129},{385... | collective-permute-start | bytes 589832 | tf_op jit(solution)/shard_map/ppermute | solution.py:37
  121.7 21.8 %collective-permute-start.5 = (bf16[1,128,768]{2,1,0:T(8,128)(2,1)S(1)}, bf16[1,128,768]{2,1,0:T(8,128)(2,1)S(1)}, u32[]{:S(2)}, u32[]{:S(2)}) collective-permute-start(bf16[1,128,768]{2,1,0:T(8,128)(2,1)S(1)} %slice.42), channel_id=1, source_target_pairs={{0,128},{128,256},{256,384},{384,0},{1,129},{129,257},{257,385},{3... | collective-permute-start | bytes 589832 | tf_op jit(solution)/shard_map/ppermute | solution.py:37
  151.7 36.4 %collective-permute-start.11 = (bf16[4,2,2,128,768]{4,3,2,1,0:T(8,128)(2,1)}, bf16[4,2,2,128,768]{4,3,2,1,0:T(8,128)(2,1)}, u32[]{:S(2)}, u32[]{:S(2)}) collective-permute-start(bf16[4,2,2,128,768]{4,3,2,1,0:T(8,128)(2,1)} %pad_maximum_fusion.part1.refs_1_), channel_id=1, source_target_pairs={{0,16},{16,0},{1,17},{17,1},{2,18},{18,2},{3,19},{19,3},{4,20},{20... | collective-permute-start | bytes 9437192 | tf_op jit(solution)/shard_map/ppermute | solution.py:37
  153.6 34.4 %collective-permute-start.10 = (bf16[4,1,2,128,768]{4,3,2,1,0:T(8,128)(2,1)}, bf16[4,1,2,128,768]{4,3,2,1,0:T(8,128)(2,1)}, u32[]{:S(2)}, u32[]{:S(2)}) collective-permute-start(bf16[4,1,2,128,768]{4,3,2,1,0:T(8,128)(2,1)} %pad_maximum_fusion.1.part0.refs_0_), channel_id=1, source_target_pairs={{0,16},{16,0},{1,17},{17,1},{2,18},{18,2},{3,19},{19,3},{4,20},{20... | collective-permute-start | bytes 4718600 | tf_op jit(solution)/shard_map/ppermute | solution.py:37
  157.6 3.8 %copy-start.14 = (s32[4]{0:T(128)S(1)}, s32[4]{0:T(128)}, u32[]{:S(2)}) copy-start(s32[4]{0:T(128)} %param.9) | copy-start | bytes 52
  157.6 30.5 %all-to-all-start.2 = ((bf16[4,4,256,256]{3,2,1,0:T(8,128)(2,1)}), bf16[4,4,256,256]{3,2,1,0:T(8,128)(2,1)S(1)}, u32[]{:S(2)}, u32[]{:S(2)}) async-start(bf16[4,4,256,256]{3,2,1,0:T(8,128)(2,1)} %broadcast_in_dim.33), calls=%async_computation.2 | async-start | bytes 4194304 | tf_op jit(solution)/shard_map/all_to_all | solution.py:51
  161.6 13.6 %collective-permute-start.14 = (bf16[1,2,128,768]{3,2,1,0:T(8,128)(2,1)S(1)}, bf16[1,2,128,768]{3,2,1,0:T(8,128)(2,1)S(1)}, u32[]{:S(2)}, u32[]{:S(2)}) collective-permute-start(bf16[1,2,128,768]{3,2,1,0:T(8,128)(2,1)S(1)} %bitcast.66), channel_id=1, source_target_pairs={{0,96},{32,0},{64,32},{96,64},{1,97},{33,1},{65,33},{97,65},{2,98}... | collective-permute-start | bytes 1179656 | tf_op jit(solution)/shard_map/ppermute | solution.py:37
  163.6 19.7 %collective-permute-start.13 = (bf16[1,2,128,768]{3,2,1,0:T(8,128)(2,1)S(1)}, bf16[1,2,128,768]{3,2,1,0:T(8,128)(2,1)S(1)}, u32[]{:S(2)}, u32[]{:S(2)}) collective-permute-start(bf16[1,2,128,768]{3,2,1,0:T(8,128)(2,1)S(1)} %bitcast.67), channel_id=1, source_target_pairs={{0,64},{32,96},{64,0},{96,32},{1,65},{33,97},{65,1},{97,33},{2,66}... | collective-permute-start | bytes 1179656 | tf_op jit(solution)/shard_map/ppermute | solution.py:37
  167.8 19.0 %collective-permute-start.12 = (bf16[1,2,128,768]{3,2,1,0:T(8,128)(2,1)S(1)}, bf16[1,2,128,768]{3,2,1,0:T(8,128)(2,1)S(1)}, u32[]{:S(2)}, u32[]{:S(2)}) collective-permute-start(bf16[1,2,128,768]{3,2,1,0:T(8,128)(2,1)S(1)} %bitcast.68), channel_id=1, source_target_pairs={{0,32},{32,64},{64,96},{96,0},{1,33},{33,65},{65,97},{97,1},{2,34}... | collective-permute-start | bytes 1179656 | tf_op jit(solution)/shard_map/ppermute | solution.py:37
  169.8 1.7 copy-start.4
  175.1 13.0 %copy-start.9 = (bf16[4,4,256,256]{3,2,1,0:T(8,128)(2,1)}, bf16[4,4,256,256]{3,2,1,0:T(8,128)(2,1)S(1)}, u32[]{:S(2)}) copy-start(bf16[4,4,256,256]{3,2,1,0:T(8,128)(2,1)S(1)} %get-tuple-element.45.scaled) | copy-start | bytes 6291460
  188.1 8.3 %collective-permute-start.15 = (bf16[4,1,2,128,768]{4,3,2,1,0:T(8,128)(2,1)}, bf16[4,1,2,128,768]{4,3,2,1,0:T(8,128)(2,1)S(1)}, u32[]{:S(2)}, u32[]{:S(2)}) collective-permute-start(bf16[4,1,2,128,768]{4,3,2,1,0:T(8,128)(2,1)} %pad_maximum_fusion.2.part2.refs_2_), channel_id=1, source_target_pairs={{0,16},{16,0},{1,17},{17,1},{2,18},{18,2},{3,19},{19,3},{4,20},{20... | collective-permute-start | bytes 4718600 | tf_op jit(solution)/shard_map/ppermute | solution.py:37
  190.0 7.6 %copy-start.2 = (bf16[4,1,2,128,768]{4,3,2,1,0:T(8,128)(2,1)S(1)}, bf16[4,1,2,128,768]{4,3,2,1,0:T(8,128)(2,1)}, u32[]{:S(2)}) copy-start(bf16[4,1,2,128,768]{4,3,2,1,0:T(8,128)(2,1)} %pad_maximum_fusion.2.part2.refs_2_) | copy-start | bytes 4718596
  195.1 1.4 copy-start.10
  196.4 1.2 copy-start.13
  212.7 31.5 %all-to-all-start.3 = ((bf16[4,4,256,256]{3,2,1,0:T(8,128)(2,1)}), bf16[4,4,256,256]{3,2,1,0:T(8,128)(2,1)S(1)}, u32[]{:S(2)}, u32[]{:S(2)}) async-start(bf16[4,4,256,256]{3,2,1,0:T(8,128)(2,1)} %shard_map.98), calls=%async_computation.3 | async-start | bytes 4194304 | tf_op jit(solution)/shard_map/all_to_all | solution.py:481
  217.1 1.4 copy-start.3
  244.1 1.4 copy-start
  245.5 31.2 %all-to-all-start.4 = ((bf16[4,4,272,256]{3,2,1,0:T(8,128)(2,1)}), bf16[4,4,272,256]{3,2,1,0:T(8,128)(2,1)S(1)}, u32[]{:S(2)}, u32[]{:S(2)}) async-start(bf16[4,4,272,256]{3,2,1,0:T(8,128)(2,1)} %shard_map.99), calls=%async_computation.4 | async-start | bytes 4456448 | tf_op jit(solution)/shard_map/all_to_all | solution.py:483
  249.1 1.8 copy-start.1
  252.7 8.9 %collective-permute-start.18 = (bf16[272,256]{1,0:T(8,128)(2,1)S(1)}, bf16[272,256]{1,0:T(8,128)(2,1)S(1)}, u32[]{:S(2)}, u32[]{:S(2)}) collective-permute-start(bf16[272,256]{1,0:T(8,128)(2,1)S(1)} %get-tuple-element.71), channel_id=1, source_target_pairs={{0,12},{4,0},{8,4},{12,8},{1,13},{5,1},{9,5},{13,9},{2,14},{6,2},{... | collective-permute-start | bytes 417800 | tf_op jit(solution)/shard_map/ppermute | solution.py:37
  254.7 13.8 %collective-permute-start.17 = (bf16[272,256]{1,0:T(8,128)(2,1)S(1)}, bf16[272,256]{1,0:T(8,128)(2,1)S(1)}, u32[]{:S(2)}, u32[]{:S(2)}) collective-permute-start(bf16[272,256]{1,0:T(8,128)(2,1)S(1)} %get-tuple-element.72), channel_id=1, source_target_pairs={{0,8},{4,12},{8,0},{12,4},{1,9},{5,13},{9,1},{13,5},{2,10},{6,14},... | collective-permute-start | bytes 417800 | tf_op jit(solution)/shard_map/ppermute | solution.py:37
  257.7 10.7 %collective-permute-start.16 = (bf16[272,256]{1,0:T(8,128)(2,1)S(1)}, bf16[272,256]{1,0:T(8,128)(2,1)S(1)}, u32[]{:S(2)}, u32[]{:S(2)}) collective-permute-start(bf16[272,256]{1,0:T(8,128)(2,1)S(1)} %get-tuple-element.73), channel_id=1, source_target_pairs={{0,4},{4,8},{8,12},{12,0},{1,5},{5,9},{9,13},{13,1},{2,6},{6,10},{... | collective-permute-start | bytes 417800 | tf_op jit(solution)/shard_map/ppermute | solution.py:37
  276.6 5.3 %copy-start.7 = (s32[32]{0:T(128)S(1)}, s32[32]{0:T(128)}, u32[]{:S(2)}) copy-start(s32[32]{0:T(128)} %live_rows.1) | copy-start | bytes 388
  276.6 19.2 %copy-start.5 = (bf16[256,256]{1,0:T(8,128)(2,1)S(1)}, bf16[256,256]{1,0:T(8,128)(2,1)}, u32[]{:S(2)}) copy-start(bf16[256,256]{1,0:T(8,128)(2,1)} %grad.1) | copy-start | bytes 393220
  278.3 17.6 %all-to-all-start.5 = ((bf16[4,272,256]{2,1,0:T(8,128)(2,1)}), bf16[4,272,256]{2,1,0:T(8,128)(2,1)S(1)}, u32[]{:S(2)}, u32[]{:S(2)}) async-start(bf16[4,272,256]{2,1,0:T(8,128)(2,1)} %shard_map.102), calls=%async_computation.5 | async-start | bytes 1114112 | tf_op jit(solution)/shard_map/all_to_all | solution.py:493
  297.5 54.0 %all-to-all-start.6 = ((bf16[32,24,256]{2,1,0:T(8,128)(2,1)}), bf16[32,24,256]{2,1,0:T(8,128)(2,1)S(1)}, u32[]{:S(2)}, u32[]{:S(2)}) async-start(bf16[32,24,256]{2,1,0:T(8,128)(2,1)} %bitcast.39), calls=%async_computation.6 | async-start | bytes 786432 | tf_op jit(solution)/shard_map/all_to_all | solution.py:508
  311.0 3.1 collective-permute-start.19
  314.1 5.7 %collective-permute-start.20 = (f32[12,256]{1,0:T(8,128)S(1)}, f32[12,256]{1,0:T(8,128)S(1)}, u32[]{:S(2)}, u32[]{:S(2)}) collective-permute-start(f32[12,256]{1,0:T(8,128)S(1)} %fusion.9), channel_id=1, source_target_pairs={{0,32},{32,0},{64,96},{96,64},{1,33},{33,1},{65,97},{97,65},{2,34}... | collective-permute-start | bytes 36872 | tf_op jit(solution)/shard_map/ppermute | solution.py:42
  319.8 7.1 %collective-permute-start.21 = (f32[12,256]{1,0:T(8,128)S(1)}, f32[12,256]{1,0:T(8,128)S(1)}, u32[]{:S(2)}, u32[]{:S(2)}) collective-permute-start(f32[12,256]{1,0:T(8,128)S(1)} %add.157), channel_id=1, source_target_pairs={{0,64},{32,96},{64,0},{96,32},{1,65},{33,97},{65,1},{97,33},{2,66}... | collective-permute-start | bytes 36872 | tf_op jit(solution)/shard_map/ppermute | solution.py:42
  326.9 9.5 %collective-permute-start.22 = (f32[12,256]{1,0:T(8,128)S(1)}, f32[12,256]{1,0:T(8,128)S(1)}, u32[]{:S(2)}, u32[]{:S(2)}) collective-permute-start(f32[12,256]{1,0:T(8,128)S(1)} %add.158), channel_id=1, source_target_pairs={{0,128},{128,0},{256,384},{384,256},{1,129},{129,1},{257,385},{385... | collective-permute-start | bytes 36872 | tf_op jit(solution)/shard_map/ppermute | solution.py:42
  336.5 14.4 %collective-permute-start.23 = (f32[12,256]{1,0:T(8,128)S(1)}, f32[12,256]{1,0:T(8,128)S(1)}, u32[]{:S(2)}, u32[]{:S(2)}) collective-permute-start(f32[12,256]{1,0:T(8,128)S(1)} %add.159), channel_id=1, source_target_pairs={{0,256},{128,384},{256,0},{384,128},{1,257},{129,385},{257,1},{385... | collective-permute-start | bytes 36872 | tf_op jit(solution)/shard_map/ppermute | solution.py:42
Sparse Core Ops, SparseCore 0:
  10.1 141.5 all-gather.2

commit v5 on v4

--- a/solution.py
+++ b/solution.py
@@ -397,7 +397,7 @@
     ).astype(f32)
 
     rows_zl = spread(rows_bal, "zl")
-    rows_zl, far, pair, gathered = lax.optimization_barrier((rows_zl, far, pair, gathered))
+    rows_zl, far, pair = lax.optimization_barrier((rows_zl, far, pair))
     last = direct_pieces(far[None], "y")
     near_other = shifted(near, "c", 1)
     pair_other = shifted(pair, "c", 1)

time: 361 us -> 354 us (0.981)
  starting transfers between devices: 169 us -> 153 us
  waiting for transfers between devices: 112 us -> 120 us
    all_to_all x2, starting transfers between devices: 32.7 us -> 15.8 us  [spread(): return lax.all_to_all(copies, axis, split_axis=0, concat_axis=0, tiled=True)]
    ppermute x19, waiting for transfers between devices: 55.8 us -> 72.6 us  [shifted(): lax.ppermute(value, axis, [(i, (i + step) % size) for i in range(size)])]
    all_gather x1, waiting for transfers between devices: 5.34 us -> 0.01 us  [body(): gathered = lax.all_gather(payload, TP, axis=0)]
    all_to_all x1, starting transfers between devices: 13.5 us -> 8.42 us  [body(): lax.all_to_all(returning, DP, split_axis=0, concat_axis=0, tiled=True)]
    unnamed x31 -> x33, local copies, waits for them, and re-layouts: 9.26 us -> 10.7 us
  transfers between devices with their start and end apart: 32 -> 32, of which waited for: 21 -> 19; matrix products, arithmetic and copies ran while one was open for 4% -> 5% of each run, Pallas kernels for 5% -> 5%
where the time goes in v5:
time: 354 us; the launch traced here: 352 us
  starting transfers between devices  153 us (43%)
  waiting for transfers between devices  120 us (34%)
  Pallas kernels  39 us (11%)
  local copies, waits for them, and re-layouts  16.4 us (5%)
  between operations  14.6 us (4%)
  other arithmetic  10.3 us (3%)
    ppermute x19, waiting for transfers between devices, shifted(): lax.ppermute(value, axis, [(i, (i + step) % size) for i in range(size)])  72.6 us
    ppermute x19, starting transfers between devices, shifted(): lax.ppermute(value, axis, [(i, (i + step) % size) for i in range(size)])  67.8 us
    ppermute x5, starting transfers between devices, crossed(): return lax.ppermute(value, axis, [(i, i ^ mask) for i in range(size)])  27.5 us
    all_to_all x1, waiting for transfers between devices, body(): lax.all_to_all(partial_out, 'x', split_axis=0, concat_axis=0, tiled=True)  19.5 us
    all_to_all x1, starting transfers between devices, body(): lax.all_to_all(outgoing, DP, split_axis=0, concat_axis=0, tiled=True)  18.5 us
    pallas_call x8, Pallas kernels, call(): pl.pallas_call(kernel, out_shape=outs, in_specs=[SMEM_SPEC if a.ndim == 1...  17.8 us
    all_to_all x2, starting transfers between devices, spread(): return lax.all_to_all(copies, axis, split_axis=0, concat_axis=0, tiled=True)  15.8 us
    all_to_all x1, waiting for transfers between devices, body(): in_zl = lax.all_to_all(in_x, 'zl', split_axis=0, concat_axis=0, tiled=True)  12.9 us
  transfers between devices with their start and end apart: 32, of which 19 were waited for; matrix products, arithmetic and copies ran while one was open for 5% of the time, Pallas kernels for 5%

profile of v5, /device:TPU:8, one launch (start us, length us, event | category | flops | bytes accessed | tf_op | source)
XLA Modules:
  0.0 352.4 jit_solution(8820632576219512670)
XLA Ops:
  10.6 18.5 %all-to-all-start = ((bf16[32,24,256]{2,1,0:T(8,128)(2,1)}), bf16[32,24,256]{2,1,0:T(8,128)(2,1)S(1)}, u32[]{:S(2)}, u32[]{:S(2)}) async-start(bf16[32,24,256]{2,1,0:T(8,128)(2,1)} %bitcast.5), calls=%async_computation | async-start | bytes 786432 | tf_op jit(solution)/shard_map/all_to_all | solution.py:382
  30.1 7.3 %collective-permute-start.1 = (bf16[2,128,768]{2,1,0:T(8,128)(2,1)S(1)}, bf16[2,128,768]{2,1,0:T(8,128)(2,1)S(1)}, u32[]{:S(2)}, u32[]{:S(2)}) collective-permute-start(bf16[2,128,768]{2,1,0:T(8,128)(2,1)S(1)} %get-tuple-element.75), channel_id=1, source_target_pairs={{0,384},{128,0},{256,128},{384,256},{1,385},{129,1},{257,129},{385... | collective-permute-start | bytes 1179656 | tf_op jit(solution)/shard_map/ppermute | solution.py:37
  37.5 2.4 collective-permute-start
  39.9 2.1 collective-permute-start.4
  42.0 4.6 %collective-permute-start.3 = (bf16[1,2,128,768]{3,2,1,0:T(8,128)(2,1)}, bf16[1,2,128,768]{3,2,1,0:T(8,128)(2,1)S(1)}, u32[]{:S(2)}, u32[]{:S(2)}) collective-permute-start(bf16[1,2,128,768]{3,2,1,0:T(8,128)(2,1)} %get-tuple-element.74), channel_id=1, source_target_pairs={{0,64},{32,96},{64,0},{96,32},{1,65},{33,97},{65,1},{97,33},{2,66}... | collective-permute-start | bytes 1179656 | tf_op jit(solution)/shard_map/ppermute | solution.py:37
  46.6 3.7 %collective-permute-start.2 = (bf16[1,2,128,768]{3,2,1,0:T(8,128)(2,1)}, bf16[1,2,128,768]{3,2,1,0:T(8,128)(2,1)S(1)}, u32[]{:S(2)}, u32[]{:S(2)}) collective-permute-start(bf16[1,2,128,768]{3,2,1,0:T(8,128)(2,1)} %get-tuple-element.74), channel_id=1, source_target_pairs={{0,32},{32,64},{64,96},{96,0},{1,33},{33,65},{65,97},{97,1},{2,34}... | collective-permute-start | bytes 1179656 | tf_op jit(solution)/shard_map/ppermute | solution.py:37
  51.5 3.0 collective-permute-done.4
  54.5 8.4 %collective-permute-done.3 = bf16[1,2,128,768]{3,2,1,0:T(8,128)(2,1)S(1)} collective-permute-done((bf16[1,2,128,768]{3,2,1,0:T(8,128)(2,1)}, bf16[1,2,128,768]{3,2,1,0:T(8,128)(2,1)S(1)}, u32[]{:S(2)}, u32[]{:S(2)}) %collective-permute-start.3) | collective-permute-done | bytes 393248 | tf_op jit(solution)/shard_map/ppermute | solution.py:37
  62.9 2.3 collective-permute-done.2
  66.6 17.3 %collective-permute-done.1 = bf16[2,128,768]{2,1,0:T(8,128)(2,1)S(1)} collective-permute-done((bf16[2,128,768]{2,1,0:T(8,128)(2,1)S(1)}, bf16[2,128,768]{2,1,0:T(8,128)(2,1)S(1)}, u32[]{:S(2)}, u32[]{:S(2)}) %collective-permute-start.1) | collective-permute-done | bytes 393248 | tf_op jit(solution)/shard_map/ppermute | solution.py:37
  85.8 6.3 %all-to-all-start.1 = ((bf16[4,256,256]{2,1,0:T(8,128)(2,1)}), bf16[4,256,256]{2,1,0:T(8,128)(2,1)S(1)}, u32[]{:S(2)}, u32[]{:S(2)}) async-start(bf16[4,256,256]{2,1,0:T(8,128)(2,1)} %broadcast_in_dim.32), calls=%async_computation.1 | async-start | bytes 1048576 | tf_op jit(solution)/shard_map/all_to_all | solution.py:51
  92.2 4.0 %collective-permute-start.8 = (bf16[2,2,128,768]{3,2,1,0:T(8,128)(2,1)S(1)}, bf16[2,2,128,768]{3,2,1,0:T(8,128)(2,1)S(1)}, u32[]{:S(2)}, u32[]{:S(2)}) collective-permute-start(bf16[2,2,128,768]{3,2,1,0:T(8,128)(2,1)S(1)} %get-tuple-element.68), channel_id=1, source_target_pairs={{0,64},{32,96},{64,0},{96,32},{1,65},{33,97},{65,1},{97,33},{2,66}... | collective-permute-start | bytes 2359304 | tf_op jit(solution)/shard_map/ppermute | solution.py:37
  98.1 3.9 %collective-permute-start.9 = (bf16[2,2,128,768]{3,2,1,0:T(8,128)(2,1)S(1)}, bf16[2,2,128,768]{3,2,1,0:T(8,128)(2,1)S(1)}, u32[]{:S(2)}, u32[]{:S(2)}) collective-permute-start(bf16[2,2,128,768]{3,2,1,0:T(8,128)(2,1)S(1)} %get-tuple-element.68), channel_id=1, source_target_pairs={{0,96},{32,0},{64,32},{96,64},{1,97},{33,1},{65,33},{97,65},{2,98}... | collective-permute-start | bytes 2359304 | tf_op jit(solution)/shard_map/ppermute | solution.py:37
  102.1 6.7 %collective-permute-start.6 = (bf16[1,128,768]{2,1,0:T(8,128)(2,1)S(1)}, bf16[1,128,768]{2,1,0:T(8,128)(2,1)S(1)}, u32[]{:S(2)}, u32[]{:S(2)}) collective-permute-start(bf16[1,128,768]{2,1,0:T(8,128)(2,1)S(1)} %slice.43), channel_id=1, source_target_pairs={{0,384},{128,0},{256,128},{384,256},{1,385},{129,1},{257,129},{385... | collective-permute-start | bytes 589832 | tf_op jit(solution)/shard_map/ppermute | solution.py:37
  108.8 3.0 collective-permute-start.5
  111.9 2.8 collective-permute-done.6
  114.6 11.8 %collective-permute-done.5 = bf16[1,128,768]{2,1,0:T(8,128)(2,1)S(1)} collective-permute-done((bf16[1,128,768]{2,1,0:T(8,128)(2,1)S(1)}, bf16[1,128,768]{2,1,0:T(8,128)(2,1)S(1)}, u32[]{:S(2)}, u32[]{:S(2)}) %collective-permute-start.5) | collective-permute-done | bytes 196640 | tf_op jit(solution)/shard_map/ppermute | solution.py:37
  126.5 4.8 %collective-permute-done.7 = bf16[2,2,128,768]{3,2,1,0:T(8,128)(2,1)S(1)} collective-permute-done((bf16[2,2,128,768]{3,2,1,0:T(8,128)(2,1)S(1)}, bf16[2,2,128,768]{3,2,1,0:T(8,128)(2,1)S(1)}, u32[]{:S(2)}, u32[]{:S(2)}) %collective-permute-start.7) | collective-permute-done | bytes 786464 | tf_op jit(solution)/shard_map/ppermute | solution.py:37
  133.2 2.0 collective-permute-start.11
  135.2 2.4 collective-permute-start.10
  139.0 9.6 %all-to-all-start.2 = ((bf16[4,4,256,256]{3,2,1,0:T(8,128)(2,1)}), bf16[4,4,256,256]{3,2,1,0:T(8,128)(2,1)S(1)}, u32[]{:S(2)}, u32[]{:S(2)}) async-start(bf16[4,4,256,256]{3,2,1,0:T(8,128)(2,1)} %broadcast_in_dim.33), calls=%async_computation.2 | async-start | bytes 4194304 | tf_op jit(solution)/shard_map/all_to_all | solution.py:51
  150.7 5.1 %collective-permute-start.13 = (bf16[1,2,128,768]{3,2,1,0:T(8,128)(2,1)S(1)}, bf16[1,2,128,768]{3,2,1,0:T(8,128)(2,1)}, u32[]{:S(2)}, u32[]{:S(2)}) collective-permute-start(bf16[1,2,128,768]{3,2,1,0:T(8,128)(2,1)S(1)} %bitcast.67), channel_id=1, source_target_pairs={{0,64},{32,96},{64,0},{96,32},{1,65},{33,97},{65,1},{97,33},{2,66}... | collective-permute-start | bytes 1179656 | tf_op jit(solution)/shard_map/ppermute | solution.py:37
  158.0 3.7 %collective-permute-done.14 = bf16[1,2,128,768]{3,2,1,0:T(8,128)(2,1)} collective-permute-done((bf16[1,2,128,768]{3,2,1,0:T(8,128)(2,1)S(1)}, bf16[1,2,128,768]{3,2,1,0:T(8,128)(2,1)}, u32[]{:S(2)}, u32[]{:S(2)}) %collective-permute-start.14) | collective-permute-done | bytes 393248 | tf_op jit(solution)/shard_map/ppermute | solution.py:37
  161.6 9.5 %collective-permute-done.13 = bf16[1,2,128,768]{3,2,1,0:T(8,128)(2,1)} collective-permute-done((bf16[1,2,128,768]{3,2,1,0:T(8,128)(2,1)S(1)}, bf16[1,2,128,768]{3,2,1,0:T(8,128)(2,1)}, u32[]{:S(2)}, u32[]{:S(2)}) %collective-permute-start.13) | collective-permute-done | bytes 393248 | tf_op jit(solution)/shard_map/ppermute | solution.py:37
  171.2 2.6 collective-permute-done.12
  173.7 2.6 pad_maximum_fusion.2.part2.refs_2_
  178.0 3.6 %shard_map.95 = (bf16[4,4,256,256]{3,2,1,0:T(8,128)(2,1)S(1)}, f32[16,16,256]{2,1,0:T(8,128)S(1)}) custom-call(s32[4]{0:T(128)S(1)} %pad_add_fusion.place, bf16[16,304,256]{2,1,0:T(8,128)(2,1)S(1)} %bitcast.63, f32[256,4]{1,0:T(8,128)S(1)} %and_convert_fusion.member), custom_call_target="tpu_custom_call" | custom-call | flops 4000000000 | tf_op jit(solution)/shard_map/pallas_call | solution.py:335
  185.1 5.1 %shard_map.96 = (bf16[4,4,272,256]{3,2,1,0:T(8,128)(2,1)S(1)}, f32[256,1]{1,0:T(8,128)S(1)}, f32[256,1]{1,0:T(8,128)S(1)}) custom-call(s32[4]{0:T(128)S(1)} %pad_add_fusion.place, bf16[4,4,256,256]{3,2,1,0:T(8,128)(2,1)S(1)} %all-to-all-done.2.rows, f32[16,16,256]{2,1,0:T(8,128)S(1)} %get-tuple-element.41.table_in, f32[256,4]{1,0:T(8,128)S(1)} %and_convert_fusion.member), custom_call_target="tpu_custom_call" | custom-call | flops 6000000000 | tf_op jit(solution)/shard_map/pallas_call | solution.py:335
  192.6 8.9 %shard_map.97 = (bf16[768,256]{1,0:T(8,128)(2,1)S(1)}, bf16[768,256]{1,0:T(8,128)(2,1)S(1)}, bf16[16,256]{1,0:T(8,128)(2,1)S(1)}) custom-call(bf16[4,4,272,256]{3,2,1,0:T(8,128)(2,1)} %copy-done.10, bf16[4,4,256,256]{3,2,1,0:T(8,128)(2,1)} %copy-done.9, f32[256,4]{1,0:T(8,128)S(1)} %and_convert_fusion.member, ...), custom_call_target="tpu_custom_call" | custom-call | flops 8000000000 | tf_op jit(solution)/shard_map/pallas_call | solution.py:438
  201.6 6.1 %shard_map.98 = bf16[4,4,256,256]{3,2,1,0:T(8,128)(2,1)} custom-call(s32[4]{0:T(128)S(1)} %pad_add_fusion.place, bf16[768,256]{1,0:T(8,128)(2,1)S(1)} %get-tuple-element.47.hidden, bf16[4,1,2,128,768]{4,3,2,1,0:T(8,128)(2,1)} %pad_maximum_fusion.1.part0.refs_0_, bf16[4,2,2,128,768]{4,3,2,1,0:T(8,128)(2,1)} %pad_maximum_fusion.part1.refs_1_, ...), custom_call_target="tpu_custom_call" | custom-call | flops 5000000000 | tf_op jit(solution)/shard_map/pallas_call | solution.py:461
  207.7 4.5 %all-to-all-start.3 = ((bf16[4,4,256,256]{3,2,1,0:T(8,128)(2,1)}), bf16[4,4,256,256]{3,2,1,0:T(8,128)(2,1)S(1)}, u32[]{:S(2)}, u32[]{:S(2)}) async-start(bf16[4,4,256,256]{3,2,1,0:T(8,128)(2,1)} %shard_map.98), calls=%async_computation.3 | async-start | bytes 4194304 | tf_op jit(solution)/shard_map/all_to_all | solution.py:481
  213.6 6.1 %shard_map.99 = bf16[4,4,272,256]{3,2,1,0:T(8,128)(2,1)} custom-call(s32[4]{0:T(128)S(1)} %pad_add_fusion.place, bf16[768,256]{1,0:T(8,128)(2,1)S(1)} %get-tuple-element.48.hidden, bf16[4,1,2,128,768]{4,3,2,1,0:T(8,128)(2,1)} %pad_maximum_fusion.1.part0.refs_0_, bf16[4,2,2,128,768]{4,3,2,1,0:T(8,128)(2,1)} %pad_maximum_fusion.part1.refs_1_, ...), custom_call_target="tpu_custom_call" | custom-call | flops 5000000000 | tf_op jit(solution)/shard_map/pallas_call | solution.py:461
  219.7 19.5 %all-to-all-done.3.blocks = bf16[4,4,256,256]{3,2,1,0:T(8,128)(2,1)S(1)} async-done(((bf16[4,4,256,256]{3,2,1,0:T(8,128)(2,1)}), bf16[4,4,256,256]{3,2,1,0:T(8,128)(2,1)S(1)}, u32[]{:S(2)}, u32[]{:S(2)}) %all-to-all-start.3) | async-done | bytes 2097184 | tf_op jit(solution)/shard_map/all_to_all | solution.py:481
  240.5 3.6 %all-to-all-start.4 = ((bf16[4,4,272,256]{3,2,1,0:T(8,128)(2,1)}), bf16[4,4,272,256]{3,2,1,0:T(8,128)(2,1)S(1)}, u32[]{:S(2)}, u32[]{:S(2)}) async-start(bf16[4,4,272,256]{3,2,1,0:T(8,128)(2,1)} %shard_map.99), calls=%async_computation.4 | async-start | bytes 4456448 | tf_op jit(solution)/shard_map/all_to_all | solution.py:483
  249.7 7.3 %collective-permute-start.17 = (bf16[272,256]{1,0:T(8,128)(2,1)S(1)}, bf16[272,256]{1,0:T(8,128)(2,1)S(1)}, u32[]{:S(2)}, u32[]{:S(2)}) collective-permute-start(bf16[272,256]{1,0:T(8,128)(2,1)S(1)} %get-tuple-element.70), channel_id=1, source_target_pairs={{0,8},{4,12},{8,0},{12,4},{1,9},{5,13},{9,1},{13,5},{2,10},{6,14},... | collective-permute-start | bytes 417800 | tf_op jit(solution)/shard_map/ppermute | solution.py:37
  257.1 3.6 %collective-permute-start.16 = (bf16[272,256]{1,0:T(8,128)(2,1)S(1)}, bf16[272,256]{1,0:T(8,128)(2,1)S(1)}, u32[]{:S(2)}, u32[]{:S(2)}) collective-permute-start(bf16[272,256]{1,0:T(8,128)(2,1)S(1)} %get-tuple-element.71), channel_id=1, source_target_pairs={{0,4},{4,8},{8,12},{12,0},{1,5},{5,9},{9,13},{13,1},{2,6},{6,10},{... | collective-permute-start | bytes 417800 | tf_op jit(solution)/shard_map/ppermute | solution.py:37
  260.7 6.4 %collective-permute-done.17.piece2 = bf16[272,256]{1,0:T(8,128)(2,1)S(1)} collective-permute-done((bf16[272,256]{1,0:T(8,128)(2,1)S(1)}, bf16[272,256]{1,0:T(8,128)(2,1)S(1)}, u32[]{:S(2)}, u32[]{:S(2)}) %collective-permute-start.17) | collective-permute-done | bytes 139296 | tf_op jit(solution)/shard_map/ppermute | solution.py:37
  267.1 4.6 %all-to-all-done.4.blocks = bf16[4,4,272,256]{3,2,1,0:T(8,128)(2,1)S(1)} async-done(((bf16[4,4,272,256]{3,2,1,0:T(8,128)(2,1)}), bf16[4,4,272,256]{3,2,1,0:T(8,128)(2,1)S(1)}, u32[]{:S(2)}, u32[]{:S(2)}) %all-to-all-start.4) | async-done | bytes 2228256 | tf_op jit(solution)/shard_map/all_to_all | solution.py:483
  273.3 6.4 %all-to-all-start.5 = ((bf16[4,272,256]{2,1,0:T(8,128)(2,1)}), bf16[4,272,256]{2,1,0:T(8,128)(2,1)S(1)}, u32[]{:S(2)}, u32[]{:S(2)}) async-start(bf16[4,272,256]{2,1,0:T(8,128)(2,1)} %shard_map.102), calls=%async_computation.5 | async-start | bytes 1114112 | tf_op jit(solution)/shard_map/all_to_all | solution.py:493
  280.6 12.9 %all-to-all-done.5.pieces = bf16[4,272,256]{2,1,0:T(8,128)(2,1)S(1)} async-done(((bf16[4,272,256]{2,1,0:T(8,128)(2,1)}), bf16[4,272,256]{2,1,0:T(8,128)(2,1)S(1)}, u32[]{:S(2)}, u32[]{:S(2)}) %all-to-all-start.5) | async-done | bytes 557088 | tf_op jit(solution)/shard_map/all_to_all | solution.py:493
  295.2 8.4 %all-to-all-start.6 = ((bf16[32,24,256]{2,1,0:T(8,128)(2,1)}), bf16[32,24,256]{2,1,0:T(8,128)(2,1)S(1)}, u32[]{:S(2)}, u32[]{:S(2)}) async-start(bf16[32,24,256]{2,1,0:T(8,128)(2,1)} %bitcast.39), calls=%async_computation.6 | async-start | bytes 786432 | tf_op jit(solution)/shard_map/all_to_all | solution.py:508
  303.7 2.1 collective-permute-start.19
  306.8 2.1 collective-permute-start.20
  308.9 3.5 %collective-permute-done.20 = f32[12,256]{1,0:T(8,128)S(1)} collective-permute-done((f32[12,256]{1,0:T(8,128)S(1)}, f32[12,256]{1,0:T(8,128)S(1)}, u32[]{:S(2)}, u32[]{:S(2)}) %collective-permute-start.20) | collective-permute-done | bytes 12320 | tf_op jit(solution)/shard_map/ppermute | solution.py:42
  312.4 4.0 %collective-permute-start.21 = (f32[12,256]{1,0:T(8,128)S(1)}, f32[12,256]{1,0:T(8,128)S(1)}, u32[]{:S(2)}, u32[]{:S(2)}) collective-permute-start(f32[12,256]{1,0:T(8,128)S(1)} %add.157), channel_id=1, source_target_pairs={{0,64},{32,96},{64,0},{96,32},{1,65},{33,97},{65,1},{97,33},{2,66}... | collective-permute-start | bytes 36872 | tf_op jit(solution)/shard_map/ppermute | solution.py:42
  316.4 3.2 collective-permute-done.21
  319.6 7.2 %collective-permute-start.22 = (f32[12,256]{1,0:T(8,128)S(1)}, f32[12,256]{1,0:T(8,128)S(1)}, u32[]{:S(2)}, u32[]{:S(2)}) collective-permute-start(f32[12,256]{1,0:T(8,128)S(1)} %add.158), channel_id=1, source_target_pairs={{0,128},{128,0},{256,384},{384,256},{1,129},{129,1},{257,385},{385... | collective-permute-start | bytes 36872 | tf_op jit(solution)/shard_map/ppermute | solution.py:42
  329.1 12.1 %collective-permute-start.23 = (f32[12,256]{1,0:T(8,128)S(1)}, f32[12,256]{1,0:T(8,128)S(1)}, u32[]{:S(2)}, u32[]{:S(2)}) collective-permute-start(f32[12,256]{1,0:T(8,128)S(1)} %add.159), channel_id=1, source_target_pairs={{0,256},{128,384},{256,0},{384,128},{1,257},{129,385},{257,1},{385... | collective-permute-start | bytes 36872 | tf_op jit(solution)/shard_map/ppermute | solution.py:42
  (106 shorter events, 46.1 us)
Async XLA Ops:
  7.2 0.7 copy-start.6
  7.8 1.0 copy-start.8
  8.8 20.3 %copy-start.12 = (bf16[768,128]{1,0:T(8,128)(2,1)S(1)}, bf16[768,128]{1,0:T(8,128)(2,1)}, u32[]{:S(2)}) copy-start(bf16[768,128]{1,0:T(8,128)(2,1)} %param.11) | copy-start | bytes 589828
  8.8 20.5 %copy-start.11 = (bf16[128,768]{1,0:T(8,128)(2,1)S(1)}, bf16[128,768]{1,0:T(8,128)(2,1)}, u32[]{:S(2)}) copy-start(bf16[128,768]{1,0:T(8,128)(2,1)} %param.10) | copy-start | bytes 589828
  10.6 39.7 %copy-start.13 = (f32[3,4,256]{2,1,0:T(4,128)S(1)}, f32[3,4,256]{2,1,0:T(4,128)}, u32[]{:S(2)}) copy-start(f32[3,4,256]{2,1,0:T(4,128)} %param.12) | copy-start | bytes 36868
  10.6 39.8 %copy-start.5 = (bf16[256,256]{1,0:T(8,128)(2,1)S(1)}, bf16[256,256]{1,0:T(8,128)(2,1)}, u32[]{:S(2)}) copy-start(bf16[256,256]{1,0:T(8,128)(2,1)} %grad.1) | copy-start | bytes 393220
  10.6 40.5 %copy-start.7 = (s32[32]{0:T(128)S(1)}, s32[32]{0:T(128)}, u32[]{:S(2)}) copy-start(s32[32]{0:T(128)} %live_rows.1) | copy-start | bytes 388
  10.6 73.2 %all-to-all-start = ((bf16[32,24,256]{2,1,0:T(8,128)(2,1)}), bf16[32,24,256]{2,1,0:T(8,128)(2,1)S(1)}, u32[]{:S(2)}, u32[]{:S(2)}) async-start(bf16[32,24,256]{2,1,0:T(8,128)(2,1)} %bitcast.5), calls=%async_computation | async-start | bytes 786432 | tf_op jit(solution)/shard_map/all_to_all | solution.py:382
  29.1 147.2 %all-gather.3.cloned.1.call-start = ((), (), s32[]{:S(2)}) async-start(), calls=%async_computation.7 | async-start | bytes 2646016 | tf_op jit(solution)/shard_map/all_gather | solution.py:381
  30.1 53.7 %collective-permute-start.1 = (bf16[2,128,768]{2,1,0:T(8,128)(2,1)S(1)}, bf16[2,128,768]{2,1,0:T(8,128)(2,1)S(1)}, u32[]{:S(2)}, u32[]{:S(2)}) collective-permute-start(bf16[2,128,768]{2,1,0:T(8,128)(2,1)S(1)} %get-tuple-element.75), channel_id=1, source_target_pairs={{0,384},{128,0},{256,128},{384,256},{1,385},{129,1},{257,129},{385... | collective-permute-start | bytes 1179656 | tf_op jit(solution)/shard_map/ppermute | solution.py:37
  37.5 46.4 %collective-permute-start = (bf16[2,128,768]{2,1,0:T(8,128)(2,1)S(1)}, bf16[2,128,768]{2,1,0:T(8,128)(2,1)S(1)}, u32[]{:S(2)}, u32[]{:S(2)}) collective-permute-start(bf16[2,128,768]{2,1,0:T(8,128)(2,1)S(1)} %get-tuple-element.75), channel_id=1, source_target_pairs={{0,128},{128,256},{256,384},{384,0},{1,129},{129,257},{257,385},{3... | collective-permute-start | bytes 1179656 | tf_op jit(solution)/shard_map/ppermute | solution.py:37
  39.9 14.6 %collective-permute-start.4 = (bf16[1,2,128,768]{3,2,1,0:T(8,128)(2,1)}, bf16[1,2,128,768]{3,2,1,0:T(8,128)(2,1)S(1)}, u32[]{:S(2)}, u32[]{:S(2)}) collective-permute-start(bf16[1,2,128,768]{3,2,1,0:T(8,128)(2,1)} %get-tuple-element.74), channel_id=1, source_target_pairs={{0,96},{32,0},{64,32},{96,64},{1,97},{33,1},{65,33},{97,65},{2,98}... | collective-permute-start | bytes 1179656 | tf_op jit(solution)/shard_map/ppermute | solution.py:37
  42.0 20.9 %collective-permute-start.3 = (bf16[1,2,128,768]{3,2,1,0:T(8,128)(2,1)}, bf16[1,2,128,768]{3,2,1,0:T(8,128)(2,1)S(1)}, u32[]{:S(2)}, u32[]{:S(2)}) collective-permute-start(bf16[1,2,128,768]{3,2,1,0:T(8,128)(2,1)} %get-tuple-element.74), channel_id=1, source_target_pairs={{0,64},{32,96},{64,0},{96,32},{1,65},{33,97},{65,1},{97,33},{2,66}... | collective-permute-start | bytes 1179656 | tf_op jit(solution)/shard_map/ppermute | solution.py:37
  46.6 18.6 %collective-permute-start.2 = (bf16[1,2,128,768]{3,2,1,0:T(8,128)(2,1)}, bf16[1,2,128,768]{3,2,1,0:T(8,128)(2,1)S(1)}, u32[]{:S(2)}, u32[]{:S(2)}) collective-permute-start(bf16[1,2,128,768]{3,2,1,0:T(8,128)(2,1)} %get-tuple-element.74), channel_id=1, source_target_pairs={{0,32},{32,64},{64,96},{96,0},{1,33},{33,65},{65,97},{97,1},{2,34}... | collective-permute-start | bytes 1179656 | tf_op jit(solution)/shard_map/ppermute | solution.py:37
  85.8 47.4 %all-to-all-start.1 = ((bf16[4,256,256]{2,1,0:T(8,128)(2,1)}), bf16[4,256,256]{2,1,0:T(8,128)(2,1)S(1)}, u32[]{:S(2)}, u32[]{:S(2)}) async-start(bf16[4,256,256]{2,1,0:T(8,128)(2,1)} %broadcast_in_dim.32), calls=%async_computation.1 | async-start | bytes 1048576 | tf_op jit(solution)/shard_map/all_to_all | solution.py:51
  92.2 34.3 %collective-permute-start.8 = (bf16[2,2,128,768]{3,2,1,0:T(8,128)(2,1)S(1)}, bf16[2,2,128,768]{3,2,1,0:T(8,128)(2,1)S(1)}, u32[]{:S(2)}, u32[]{:S(2)}) collective-permute-start(bf16[2,2,128,768]{3,2,1,0:T(8,128)(2,1)S(1)} %get-tuple-element.68), channel_id=1, source_target_pairs={{0,64},{32,96},{64,0},{96,32},{1,65},{33,97},{65,1},{97,33},{2,66}... | collective-permute-start | bytes 2359304 | tf_op jit(solution)/shard_map/ppermute | solution.py:37
  96.2 35.1 %collective-permute-start.7 = (bf16[2,2,128,768]{3,2,1,0:T(8,128)(2,1)S(1)}, bf16[2,2,128,768]{3,2,1,0:T(8,128)(2,1)S(1)}, u32[]{:S(2)}, u32[]{:S(2)}) collective-permute-start(bf16[2,2,128,768]{3,2,1,0:T(8,128)(2,1)S(1)} %get-tuple-element.68), channel_id=1, source_target_pairs={{0,32},{32,64},{64,96},{96,0},{1,33},{33,65},{65,97},{97,1},{2,34}... | collective-permute-start | bytes 2359304 | tf_op jit(solution)/shard_map/ppermute | solution.py:37
  98.1 33.2 %collective-permute-start.9 = (bf16[2,2,128,768]{3,2,1,0:T(8,128)(2,1)S(1)}, bf16[2,2,128,768]{3,2,1,0:T(8,128)(2,1)S(1)}, u32[]{:S(2)}, u32[]{:S(2)}) collective-permute-start(bf16[2,2,128,768]{3,2,1,0:T(8,128)(2,1)S(1)} %get-tuple-element.68), channel_id=1, source_target_pairs={{0,96},{32,0},{64,32},{96,64},{1,97},{33,1},{65,33},{97,65},{2,98}... | collective-permute-start | bytes 2359304 | tf_op jit(solution)/shard_map/ppermute | solution.py:37
  102.1 12.5 %collective-permute-start.6 = (bf16[1,128,768]{2,1,0:T(8,128)(2,1)S(1)}, bf16[1,128,768]{2,1,0:T(8,128)(2,1)S(1)}, u32[]{:S(2)}, u32[]{:S(2)}) collective-permute-start(bf16[1,128,768]{2,1,0:T(8,128)(2,1)S(1)} %slice.43), channel_id=1, source_target_pairs={{0,384},{128,0},{256,128},{384,256},{1,385},{129,1},{257,129},{385... | collective-permute-start | bytes 589832 | tf_op jit(solution)/shard_map/ppermute | solution.py:37
  108.8 17.6 %collective-permute-start.5 = (bf16[1,128,768]{2,1,0:T(8,128)(2,1)S(1)}, bf16[1,128,768]{2,1,0:T(8,128)(2,1)S(1)}, u32[]{:S(2)}, u32[]{:S(2)}) collective-permute-start(bf16[1,128,768]{2,1,0:T(8,128)(2,1)S(1)} %slice.42), channel_id=1, source_target_pairs={{0,128},{128,256},{256,384},{384,0},{1,129},{129,257},{257,385},{3... | collective-permute-start | bytes 589832 | tf_op jit(solution)/shard_map/ppermute | solution.py:37
  133.2 49.9 %collective-permute-start.11 = (bf16[4,2,2,128,768]{4,3,2,1,0:T(8,128)(2,1)}, bf16[4,2,2,128,768]{4,3,2,1,0:T(8,128)(2,1)}, u32[]{:S(2)}, u32[]{:S(2)}) collective-permute-start(bf16[4,2,2,128,768]{4,3,2,1,0:T(8,128)(2,1)} %pad_maximum_fusion.part1.refs_1_), channel_id=1, source_target_pairs={{0,16},{16,0},{1,17},{17,1},{2,18},{18,2},{3,19},{19,3},{4,20},{20... | collective-permute-start | bytes 9437192 | tf_op jit(solution)/shard_map/ppermute | solution.py:37
  135.2 47.9 %collective-permute-start.10 = (bf16[4,1,2,128,768]{4,3,2,1,0:T(8,128)(2,1)}, bf16[4,1,2,128,768]{4,3,2,1,0:T(8,128)(2,1)}, u32[]{:S(2)}, u32[]{:S(2)}) collective-permute-start(bf16[4,1,2,128,768]{4,3,2,1,0:T(8,128)(2,1)} %pad_maximum_fusion.1.part0.refs_0_), channel_id=1, source_target_pairs={{0,16},{16,0},{1,17},{17,1},{2,18},{18,2},{3,19},{19,3},{4,20},{20... | collective-permute-start | bytes 4718600 | tf_op jit(solution)/shard_map/ppermute | solution.py:37
  139.0 9.6 %copy-start.15 = (s32[4]{0:T(128)S(1)}, s32[4]{0:T(128)}, u32[]{:S(2)}) copy-start(s32[4]{0:T(128)} %param.9) | copy-start | bytes 52
  139.0 44.1 %all-to-all-start.2 = ((bf16[4,4,256,256]{3,2,1,0:T(8,128)(2,1)}), bf16[4,4,256,256]{3,2,1,0:T(8,128)(2,1)S(1)}, u32[]{:S(2)}, u32[]{:S(2)}) async-start(bf16[4,4,256,256]{3,2,1,0:T(8,128)(2,1)} %broadcast_in_dim.33), calls=%async_computation.2 | async-start | bytes 4194304 | tf_op jit(solution)/shard_map/all_to_all | solution.py:51
  148.8 12.9 %collective-permute-start.14 = (bf16[1,2,128,768]{3,2,1,0:T(8,128)(2,1)S(1)}, bf16[1,2,128,768]{3,2,1,0:T(8,128)(2,1)}, u32[]{:S(2)}, u32[]{:S(2)}) collective-permute-start(bf16[1,2,128,768]{3,2,1,0:T(8,128)(2,1)S(1)} %bitcast.66), channel_id=1, source_target_pairs={{0,96},{32,0},{64,32},{96,64},{1,97},{33,1},{65,33},{97,65},{2,98}... | collective-permute-start | bytes 1179656 | tf_op jit(solution)/shard_map/ppermute | solution.py:37
  150.7 20.5 %collective-permute-start.13 = (bf16[1,2,128,768]{3,2,1,0:T(8,128)(2,1)S(1)}, bf16[1,2,128,768]{3,2,1,0:T(8,128)(2,1)}, u32[]{:S(2)}, u32[]{:S(2)}) collective-permute-start(bf16[1,2,128,768]{3,2,1,0:T(8,128)(2,1)S(1)} %bitcast.67), channel_id=1, source_target_pairs={{0,64},{32,96},{64,0},{96,32},{1,65},{33,97},{65,1},{97,33},{2,66}... | collective-permute-start | bytes 1179656 | tf_op jit(solution)/shard_map/ppermute | solution.py:37
  155.8 17.9 %collective-permute-start.12 = (bf16[1,2,128,768]{3,2,1,0:T(8,128)(2,1)S(1)}, bf16[1,2,128,768]{3,2,1,0:T(8,128)(2,1)}, u32[]{:S(2)}, u32[]{:S(2)}) collective-permute-start(bf16[1,2,128,768]{3,2,1,0:T(8,128)(2,1)S(1)} %bitcast.68), channel_id=1, source_target_pairs={{0,32},{32,64},{64,96},{96,0},{1,33},{33,65},{65,97},{97,1},{2,34}... | collective-permute-start | bytes 1179656 | tf_op jit(solution)/shard_map/ppermute | solution.py:37
  176.3 1.7 copy-start.4
  181.7 1.4 copy-start.9
  183.1 8.4 %collective-permute-start.15 = (bf16[4,1,2,128,768]{4,3,2,1,0:T(8,128)(2,1)}, bf16[4,1,2,128,768]{4,3,2,1,0:T(8,128)(2,1)S(1)}, u32[]{:S(2)}, u32[]{:S(2)}) collective-permute-start(bf16[4,1,2,128,768]{4,3,2,1,0:T(8,128)(2,1)} %pad_maximum_fusion.2.part2.refs_2_), channel_id=1, source_target_pairs={{0,16},{16,0},{1,17},{17,1},{2,18},{18,2},{3,19},{19,3},{4,20},{20... | collective-permute-start | bytes 4718600 | tf_op jit(solution)/shard_map/ppermute | solution.py:37
  185.0 7.6 %copy-start.2 = (bf16[4,1,2,128,768]{4,3,2,1,0:T(8,128)(2,1)S(1)}, bf16[4,1,2,128,768]{4,3,2,1,0:T(8,128)(2,1)}, u32[]{:S(2)}) copy-start(bf16[4,1,2,128,768]{4,3,2,1,0:T(8,128)(2,1)} %pad_maximum_fusion.2.part2.refs_2_) | copy-start | bytes 4718596
  190.1 1.4 copy-start.10
  191.5 1.1 copy-start.14
  207.7 31.5 %all-to-all-start.3 = ((bf16[4,4,256,256]{3,2,1,0:T(8,128)(2,1)}), bf16[4,4,256,256]{3,2,1,0:T(8,128)(2,1)S(1)}, u32[]{:S(2)}, u32[]{:S(2)}) async-start(bf16[4,4,256,256]{3,2,1,0:T(8,128)(2,1)} %shard_map.98), calls=%async_computation.3 | async-start | bytes 4194304 | tf_op jit(solution)/shard_map/all_to_all | solution.py:481
  212.2 1.4 copy-start.3
  239.2 1.4 copy-start
  240.5 31.2 %all-to-all-start.4 = ((bf16[4,4,272,256]{3,2,1,0:T(8,128)(2,1)}), bf16[4,4,272,256]{3,2,1,0:T(8,128)(2,1)S(1)}, u32[]{:S(2)}, u32[]{:S(2)}) async-start(bf16[4,4,272,256]{3,2,1,0:T(8,128)(2,1)} %shard_map.99), calls=%async_computation.4 | async-start | bytes 4456448 | tf_op jit(solution)/shard_map/all_to_all | solution.py:483
  244.2 1.8 copy-start.1
  247.8 12.9 %collective-permute-start.18 = (bf16[272,256]{1,0:T(8,128)(2,1)S(1)}, bf16[272,256]{1,0:T(8,128)(2,1)S(1)}, u32[]{:S(2)}, u32[]{:S(2)}) collective-permute-start(bf16[272,256]{1,0:T(8,128)(2,1)S(1)} %get-tuple-element.69), channel_id=1, source_target_pairs={{0,12},{4,0},{8,4},{12,8},{1,13},{5,1},{9,5},{13,9},{2,14},{6,2},{... | collective-permute-start | bytes 417800 | tf_op jit(solution)/shard_map/ppermute | solution.py:37
  249.7 17.4 %collective-permute-start.17 = (bf16[272,256]{1,0:T(8,128)(2,1)S(1)}, bf16[272,256]{1,0:T(8,128)(2,1)S(1)}, u32[]{:S(2)}, u32[]{:S(2)}) collective-permute-start(bf16[272,256]{1,0:T(8,128)(2,1)S(1)} %get-tuple-element.70), channel_id=1, source_target_pairs={{0,8},{4,12},{8,0},{12,4},{1,9},{5,13},{9,1},{13,5},{2,10},{6,14},... | collective-permute-start | bytes 417800 | tf_op jit(solution)/shard_map/ppermute | solution.py:37
  257.1 10.0 %collective-permute-start.16 = (bf16[272,256]{1,0:T(8,128)(2,1)S(1)}, bf16[272,256]{1,0:T(8,128)(2,1)S(1)}, u32[]{:S(2)}, u32[]{:S(2)}) collective-permute-start(bf16[272,256]{1,0:T(8,128)(2,1)S(1)} %get-tuple-element.71), channel_id=1, source_target_pairs={{0,4},{4,8},{8,12},{12,0},{1,5},{5,9},{9,13},{13,1},{2,6},{6,10},{... | collective-permute-start | bytes 417800 | tf_op jit(solution)/shard_map/ppermute | solution.py:37
  273.3 20.2 %all-to-all-start.5 = ((bf16[4,272,256]{2,1,0:T(8,128)(2,1)}), bf16[4,272,256]{2,1,0:T(8,128)(2,1)S(1)}, u32[]{:S(2)}, u32[]{:S(2)}) async-start(bf16[4,272,256]{2,1,0:T(8,128)(2,1)} %shard_map.102), calls=%async_computation.5 | async-start | bytes 1114112 | tf_op jit(solution)/shard_map/all_to_all | solution.py:493
  295.2 49.0 %all-to-all-start.6 = ((bf16[32,24,256]{2,1,0:T(8,128)(2,1)}), bf16[32,24,256]{2,1,0:T(8,128)(2,1)S(1)}, u32[]{:S(2)}, u32[]{:S(2)}) async-start(bf16[32,24,256]{2,1,0:T(8,128)(2,1)} %bitcast.39), calls=%async_computation.6 | async-start | bytes 786432 | tf_op jit(solution)/shard_map/all_to_all | solution.py:508
  303.7 3.1 collective-permute-start.19
  306.8 5.7 %collective-permute-start.20 = (f32[12,256]{1,0:T(8,128)S(1)}, f32[12,256]{1,0:T(8,128)S(1)}, u32[]{:S(2)}, u32[]{:S(2)}) collective-permute-start(f32[12,256]{1,0:T(8,128)S(1)} %fusion.9), channel_id=1, source_target_pairs={{0,32},{32,0},{64,96},{96,64},{1,33},{33,1},{65,97},{97,65},{2,34}... | collective-permute-start | bytes 36872 | tf_op jit(solution)/shard_map/ppermute | solution.py:42
  312.4 7.1 %collective-permute-start.21 = (f32[12,256]{1,0:T(8,128)S(1)}, f32[12,256]{1,0:T(8,128)S(1)}, u32[]{:S(2)}, u32[]{:S(2)}) collective-permute-start(f32[12,256]{1,0:T(8,128)S(1)} %add.157), channel_id=1, source_target_pairs={{0,64},{32,96},{64,0},{96,32},{1,65},{33,97},{65,1},{97,33},{2,66}... | collective-permute-start | bytes 36872 | tf_op jit(solution)/shard_map/ppermute | solution.py:42
  319.6 9.5 %collective-permute-start.22 = (f32[12,256]{1,0:T(8,128)S(1)}, f32[12,256]{1,0:T(8,128)S(1)}, u32[]{:S(2)}, u32[]{:S(2)}) collective-permute-start(f32[12,256]{1,0:T(8,128)S(1)} %add.158), channel_id=1, source_target_pairs={{0,128},{128,0},{256,384},{384,256},{1,129},{129,1},{257,385},{385... | collective-permute-start | bytes 36872 | tf_op jit(solution)/shard_map/ppermute | solution.py:42
  329.1 14.4 %collective-permute-start.23 = (f32[12,256]{1,0:T(8,128)S(1)}, f32[12,256]{1,0:T(8,128)S(1)}, u32[]{:S(2)}, u32[]{:S(2)}) collective-permute-start(f32[12,256]{1,0:T(8,128)S(1)} %add.159), channel_id=1, source_target_pairs={{0,256},{128,384},{256,0},{384,128},{1,257},{129,385},{257,1},{385... | collective-permute-start | bytes 36872 | tf_op jit(solution)/shard_map/ppermute | solution.py:42
Sparse Core Ops, SparseCore 0:
  51.2 114.7 all-gather.2
